TPU v7x, 32 devices: a whole 2x2x4 slice. The times are simulated.
32 devices in a mesh: leaf: 16 (over z, y, core), samp: 2 (over x).
Axes of the slice: x: 2, y: 2, z: 4, core: 2. Of those that a mesh axis runs over, the one named last changes fastest.
Arguments:
- stiffness_block_row: bfloat16 [256, 8, 128, 128], P('leaf'), may hold values from -2 to 2
- stored_block_column: int32 [256, 8], P('leaf'), may hold values from 0 to 255, as said below
- samples_t: bfloat16 [256, 32768], P('samp', 'leaf'), may hold values from -8 to 8
Outputs:
- products: float32 [256, 32768], P('samp', 'leaf')
- bases: float32 [256, 32768], P('samp', 'leaf')
- transfer_one: float32 [4096, 256], P('leaf', 'samp')
- transfer_two: float32 [4096, 256], P('leaf', 'samp')
- transfer_three: float32 [4096, 256], P('leaf', 'samp')
- top_factor: float32 [4096, 256], P('leaf', 'samp')
Inputs may be any that keep to these rules, and one draw needn't show every extreme that they name: `stored_block_column`: slot 0 of block row r names block column r; the other slots name block columns of the same leaf, or of a neighbouring leaf within 4 block rows of the boundary that the two leaves share; the first block row of every leaf that has a neighbour on a side reaches exactly 4 block rows into it, and every one of those 4 block rows is named by some block row of the leaf.
All inputs are finite; a program needn't handle non-finite values.
Results may differ from a plain program's by a relative error of at most 0.0003.
Values may be sent and summed in bfloat16 or wider, within the bound.
No kernel may reach another device: no remote copies, remote signals or barrier semaphores. Data moves between devices by JAX's collectives and lax.ppermute only.
A program may use at most 64 MiB of HBM per device.

v0:
```python
import math

import jax
import jax.numpy as jnp
from jax import lax
from jax.sharding import PartitionSpec as P

HB = 4
LEVELS = 3


def with_halo(cells, sides, width):
    for axis, dim in sides:
        count = lax.axis_size(axis)
        ends = count - 1
        head = lax.slice_in_dim(cells, 0, width, axis=dim)
        tail = lax.slice_in_dim(cells, cells.shape[dim] - width, cells.shape[dim], axis=dim)
        cells = jnp.concatenate(
            [
                lax.ppermute(tail, axis, [(i, (i + 1) % count) for i in range(ends)]),
                cells,
                lax.ppermute(head, axis, [((i + 1) % count, i) for i in range(ends)]),
            ],
            axis=dim,
        )
    return cells


def from_partner(block, axis, bit):
    count = lax.axis_size(axis)
    route = []
    for low in range(count):
        high = low | 1 << bit
        if high != low and high < count:
            route += [(low, high), (high, low)]
    return lax.ppermute(block, axis, route)


def lower_solve(factor, right_side):
    return jax.scipy.linalg.solve_triangular(factor, right_side, lower=True)


def pick_blocks(sample_blocks, positions, keep_mask):
    sample_count = sample_blocks.shape[0]
    picked = jnp.take(sample_blocks, positions.reshape(-1), axis=1)
    picked = picked.reshape((sample_count,) + positions.shape + (sample_blocks.shape[2],))
    return jnp.where(keep_mask[None, :, :, None], picked, jnp.zeros_like(picked))


def shards(stiffness_block_row, stored_block_column, samples_t):
    block_sequence = stiffness_block_row.shape[2]
    blocks_here = stored_block_column.shape[0]
    sample_count = samples_t.shape[0]
    row_count = samples_t.shape[1]
    leaf_position_index = lax.axis_index("leaf")
    sample_index = lax.axis_index("samp")
    local_cols = stored_block_column - leaf_position_index * blocks_here
    inside = (local_cols >= 0) & (local_cols < blocks_here)
    own_blocks = samples_t.reshape(sample_count, blocks_here, block_sequence)
    near_terms = pick_blocks(own_blocks, jnp.clip(local_cols, 0, blocks_here - 1), inside)
    nearfield_portion = jnp.einsum(
        "rkij,srkj->sri", stiffness_block_row, near_terms, preferred_element_type=jnp.float32
    )
    window = with_halo(samples_t, (("leaf", 1),), HB * block_sequence)
    window_blocks = window.reshape(sample_count, blocks_here + 2 * HB, block_sequence)
    far_terms = pick_blocks(
        window_blocks,
        jnp.clip(local_cols + HB, 0, blocks_here + 2 * HB - 1),
        jnp.logical_not(inside),
    )
    far_part = jnp.einsum(
        "rkij,srkj->sri", stiffness_block_row, far_terms, preferred_element_type=jnp.float32
    )
    distant_portion = far_part.reshape(sample_count, row_count)
    products = (nearfield_portion + far_part).reshape(sample_count, row_count)
    gathered = lax.all_gather(distant_portion, "samp", axis=0, tiled=True)
    gramian_product = jnp.einsum("sr,tr->st", gathered, gathered, precision=lax.Precision.HIGHEST)

    def own_columns(matrix):
        return lax.dynamic_slice_in_dim(
            matrix, sample_index * sample_count, sample_count, matrix.ndim - 1
        )

    level_grams = [gramian_product]
    current = gramian_product
    for height in range(LEVELS):
        partner = from_partner(current, "leaf", height)
        current = current + partner
        level_grams.append(current)
    factors = jnp.linalg.cholesky(jnp.stack(level_grams))
    basis_whole = lower_solve(factors[0], gathered)
    leaf_basis = lax.dynamic_slice_in_dim(basis_whole, sample_index * sample_count, sample_count, 0)
    bases = leaf_basis * math.sqrt(row_count)
    child_pieces = own_columns(factors[:-1])
    transfer_blocks = jax.vmap(lower_solve)(factors[1:], child_pieces)
    top_factor = own_columns(factors[-1]) / math.sqrt(2**LEVELS * row_count)
    return (products, bases, transfer_blocks[0], transfer_blocks[1], transfer_blocks[2], top_factor)


def solution(mesh):
    return jax.shard_map(
        shards,
        mesh=mesh,
        in_specs=(P("leaf", None, None, None), P("leaf", None), P("samp", "leaf")),
        out_specs=(
            P("samp", "leaf"),
            P("samp", "leaf"),
            P("leaf", "samp"),
            P("leaf", "samp"),
            P("leaf", "samp"),
            P("leaf", "samp"),
        ),
        check_vma=False,
    )
```

profile of v0, /device:TPU:0, one launch (start us, length us, event | category | flops | bytes accessed | tf_op | source)
XLA Modules:
  0.0 332.9 jit_solution(3278176915888678277)
XLA Ops:
  7.2 1.3 copy.68
  8.6 2.4 collective-permute-start
  10.9 1.3 collective-permute-start.1
  13.3 3.0 collective-permute-done.1
  16.7 3.0 gather_fusion.1
  19.8 4.8 %fusion = f32[16,128,128,1]{1,2,3,0:T(8,128)S(1)} fusion(bf16[16,8,128,128]{3,2,1,0:T(8,128)(2,1)} %param.3, bf16[128,16,8,128]{3,0,2,1:T(8,128)(2,1)} %bitcast.104, pred[16,8]{1,0:T(8,128)(4,1)S(1)} %copy.72, pred[16,8]{1,0:T(8,128)(4,1)S(1)} %copy.71), kind=kOutput, calls=%fused_computation.6 | convolution fusion | flops 541065216 | bytes 9437440 | tf_op jit(solution)/shard_map/rkij,srkj->sri/dot_general | solution.py:71
  24.6 1.3 copy.78
  26.1 37.4 %all-gather.2.cloned.1.call-done = f32[256,2048]{1,0:T(8,128)} async-done(((f32[128,2048]{1,0:T(8,128)}), f32[256,2048]{1,0:T(8,128)}) %all-gather.2.cloned.1.call-update) | async-done | bytes 2097168 | tf_op jit(solution)/shard_map/all_gather | solution.py:76
  63.5 4.1 %fusion.51 = f32[256,256]{0,1:T(8,128)S(1)} fusion(f32[256,2048]{1,0:T(8,128)} %all-gather.2.cloned.1.call-done), kind=kOutput, calls=%fused_computation.97 | convolution fusion | flops 1610612736 | bytes 2359296 | tf_op jit(solution)/shard_map/sr,tr->st/dot_general | solution.py:77
  67.7 1.5 collective-permute-done.2
  69.3 1.5 collective-permute-start.3
  71.3 3.0 gather_fusion
  74.3 3.3 collective-permute-done.3
  77.7 1.6 collective-permute-start.4
  79.3 5.8 %fusion.17 = f32[128,16,128]{0,2,1:T(8,128)} fusion(bf16[16,8,128,128]{3,2,1,0:T(8,128)(2,1)} %param.3, bf16[128,16,8,128]{3,0,2,1:T(8,128)(2,1)} %bitcast.103, pred[16,8]{1,0:T(8,128)(4,1)S(1)} %copy.67, pred[16,8]{1,0:T(8,128)(4,1)S(1)} %copy.66, f32[16,128,128,1]{1,2,3,0:T(8,128)S(1)} %copy-done.3), kind=kOutput, calls=%fused_computation.24 | convolution fusion | flops 541327360 | bytes 10486016 | tf_op jit(solution)/shard_map/rkij,srkj->sri/dot_general | solution.py:61
  85.1 2.5 copy.88
  88.2 47.1 %custom-call.21 = f32[4,128,128]{2,1,0:T(8,128)S(1)} custom-call(f32[4,128,128]{2,1,0:T(8,128)S(1)} %cholesky.122), custom_call_target="Cholesky" | custom-call | tf_op jit(solution)/shard_map/jit(cholesky)/cholesky | solution.py:90
  135.5 39.3 %custom-call.22 = f32[4,1,128,128]{2,3,1,0:T(8,128)S(1)} custom-call(f32[4,1,128,128]{3,2,1,0:T(8,128)S(1)} %select_bitcast_fusion), custom_call_target="InvertDiagBlocksLowerTriangular" | custom-call | tf_op jit(solution)/shard_map/jit(cholesky)/cholesky | solution.py:90
  175.8 46.9 %custom-call.23 = f32[4,128,128]{2,1,0:T(8,128)S(1)} custom-call(f32[4,128,128]{2,1,0:T(8,128)S(1)} %convolution_subtract_fusion.1), custom_call_target="Cholesky" | custom-call | tf_op jit(solution)/shard_map/jit(cholesky)/cholesky | solution.py:90
  223.2 1.4 slice_select_fusion
  224.7 7.3 %while.3 = (s32[]{:T(128)}, f32[3,256,256]{2,1,0:T(8,128)}, s32[2,2]{1,0:T(2,128)S(1)}, f32[2,3,128,128]{3,2,0,1:T(8,128)}, s32[]{:T(128)}) while((s32[]{:T(128)}, f32[3,256,256]{2,1,0:T(8,128)}, s32[2,2]{1,0:T(2,128)S(1)}, f32[2,3,128,128]{3,2,0,1:T(8,128)}, s32[]{:T(128)}) %tuple.59), condition=%wide.while_cond.1, body=%wide.while_body.1.sunk | while | flops 2 | bytes 394849 | solution.py:40
  225.3 3.1 bitcast_dynamic-update-slice_fusion.5
  229.0 3.0 bitcast_dynamic-update-slice_fusion.5
  232.0 60.4 %custom-call.25 = f32[3,2,128,128]{2,3,1,0:T(8,128)} custom-call(f32[3,2,128,128]{3,2,1,0:T(8,128)} %bitcast.114), custom_call_target="InvertDiagBlocksLowerTriangular" | custom-call | tf_op jit(solution)/shard_map/vmap(jit(_solve_triangular))/triangular_solve | solution.py:40
  292.4 1.5 fusion.31
  294.0 1.4 convolution_subtract_fusion.2
  295.3 1.4 fusion.30
  297.5 3.8 %while.2 = (s32[]{:T(128)}, f32[256,256]{1,0:T(8,128)S(1)}, s32[2,2]{1,0:T(2,128)S(1)}, f32[2,128,128]{2,1,0:T(8,128)S(1)}, s32[]{:T(128)}) while((s32[]{:T(128)}, f32[256,256]{1,0:T(8,128)S(1)}, s32[2,2]{1,0:T(2,128)S(1)}, f32[2,128,128]{2,1,0:T(8,128)S(1)}, s32[]{:T(128)}) %tuple.64), condition=%wide.while_cond, body=%wide.while_body.sunk | while | flops 2 | bytes 131181 | solution.py:40
  298.1 1.3 bitcast_dynamic-update-slice_fusion.4
  300.0 1.3 bitcast_dynamic-update-slice_fusion.4
  301.4 19.7 %custom-call.24 = f32[2,128,128]{1,2,0:T(8,128)S(1)} custom-call(f32[2,128,128]{2,1,0:T(8,128)S(1)} %get-tuple-element.13), custom_call_target="InvertDiagBlocksLowerTriangular" | custom-call | tf_op jit(solution)/shard_map/jit(_solve_triangular)/triangular_solve | solution.py:40
  324.2 1.2 fusion.21
  (68 shorter events, 11.5 us)
Async XLA Ops:
  7.2 56.4 %all-gather.2.cloned.1.call-start = ((), (), s32[]{:S(2)}) async-start(), calls=%async_computation | async-start | bytes 3145728 | tf_op jit(solution)/shard_map/all_gather | solution.py:76
  8.6 4.7 %collective-permute-start = (bf16[128,512]{0,1:T(8,128)(2,1)S(1)}, bf16[128,512]{0,1:T(8,128)(2,1)S(1)}, u32[]{:S(2)}, u32[]{:S(2)}) collective-permute-start(bf16[128,512]{0,1:T(8,128)(2,1)S(1)} %get-tuple-element.76), channel_id=1, source_target_pairs={{0,2},{2,4},{4,6},{6,8},{8,10},{10,12},{12,14},{14,16},{16,18},{18... | collective-permute-start | bytes 393224 | tf_op jit(solution)/shard_map/ppermute | solution.py:20
  10.9 5.4 %collective-permute-start.1 = (bf16[128,512]{0,1:T(8,128)(2,1)S(1)}, bf16[128,512]{0,1:T(8,128)(2,1)S(1)}, u32[]{:S(2)}, u32[]{:S(2)}) collective-permute-start(bf16[128,512]{0,1:T(8,128)(2,1)S(1)} %get-tuple-element.77), channel_id=1, source_target_pairs={{2,0},{4,2},{6,4},{8,6},{10,8},{12,10},{14,12},{16,14},{18,16},{20... | collective-permute-start | bytes 393224 | tf_op jit(solution)/shard_map/ppermute | solution.py:22
  24.6 1.5 copy-start.2
  67.6 1.6 collective-permute-start.2
  69.3 8.4 %collective-permute-start.3 = (f32[256,256]{0,1:T(8,128)S(1)}, f32[256,256]{0,1:T(8,128)S(1)}, u32[]{:S(2)}, u32[]{:S(2)}) collective-permute-start(f32[256,256]{0,1:T(8,128)S(1)} %add.101), channel_id=1, source_target_pairs={{0,4},{4,0},{2,6},{6,2},{8,12},{12,8},{10,14},{14,10},{16,20},{20,... | collective-permute-start | bytes 786440 | tf_op jit(solution)/shard_map/ppermute | solution.py:36
  71.3 8.0 %copy-start.3 = (f32[16,128,128,1]{1,2,3,0:T(8,128)S(1)}, f32[16,128,128,1]{1,2,3,0:T(8,128)}, u32[]{:S(2)}) copy-start(f32[16,128,128,1]{1,2,3,0:T(8,128)} %copy-done.2) | copy-start | bytes 3145732
  77.7 9.9 %collective-permute-start.4 = (f32[256,256]{0,1:T(8,128)S(1)}, f32[256,256]{0,1:T(8,128)S(1)}, u32[]{:S(2)}, u32[]{:S(2)}) collective-permute-start(f32[256,256]{0,1:T(8,128)S(1)} %add.102), channel_id=1, source_target_pairs={{0,8},{8,0},{2,10},{10,2},{4,12},{12,4},{6,14},{14,6},{16,24},{24,... | collective-permute-start | bytes 786440 | tf_op jit(solution)/shard_map/ppermute | solution.py:36
  223.1 74.4 %copy-start.1 = (f32[4,256,256]{2,1,0:T(8,128)}, f32[4,256,256]{2,1,0:T(8,128)S(1)}, u32[]{:S(2)}) copy-start(f32[4,256,256]{2,1,0:T(8,128)S(1)} %select_select_fusion) | copy-start | bytes 3145732
  224.6 96.5 %copy-start = (f32[256,2048]{1,0:T(8,128)S(1)}, f32[256,2048]{1,0:T(8,128)}, u32[]{:S(2)}) copy-start(f32[256,2048]{1,0:T(8,128)} %all-gather.2.cloned.1.call-done) | copy-start | bytes 6291460
  322.1 3.3 slice-start
Sparse Core Ops, SparseCore 0:
  26.1 37.4 all-gather.1
where the time goes:
time: 333 us
  other arithmetic  219 us (66%)
  waiting for transfers between devices  45.2 us (14%)
  local copies, waits for them, and re-layouts  24.2 us (7%)
  matrix products  23.2 us (7%)
  between operations  14.4 us (4%)
  starting transfers between devices  6.86 us (2%)
    another operation x11, other arithmetic, shards(): factors = jnp.linalg.cholesky(jnp.stack(level_grams))  134 us
    another operation x6, other arithmetic, lower_solve(): return jax.scipy.linalg.solve_triangular(factor, right_side, lower=True)  81.6 us
    all_gather x1, waiting for transfers between devices, shards(): gathered = lax.all_gather(distant_portion, 'samp', axis=0, tiled=True)  37.4 us
    another operation x12, local copies, waits for them, and re-layouts  11.1 us
    another operation x6, matrix products, lower_solve(): return jax.scipy.linalg.solve_triangular(factor, right_side, lower=True)  7.44 us
  transfers between devices with their start and end apart: 6, of which 4 were waited for; matrix products, arithmetic and copies ran while one was open for 4% of the time, Pallas kernels for 0%

commit v1 on v0

v1 whole, which is shorter than its diff:
```python
import functools
import math

import jax
import jax.numpy as jnp
from jax import lax
from jax.experimental import pallas as pl
from jax.experimental.pallas import tpu as pltpu
from jax.sharding import PartitionSpec as P

HB = 4
LEVELS = 3
LANES = 128
GROUP = 8
PANEL = 32
ROWS_A_STEP = 2
VMEM_LIMIT = 48 * 1024 * 1024
F32 = jnp.float32
BF16 = jnp.bfloat16
NN = (((1,), (0,)), ((), ()))
NT = (((1,), (1,)), ((), ()))
TN = (((0,), (0,)), ((), ()))


def dot(a, b, dims):
    return lax.dot_general(a, b, dims, preferred_element_type=F32)


def split_two(x):
    high = x.astype(BF16)
    return high, (x - high.astype(F32)).astype(BF16)


def split_three(x):
    high = x.astype(BF16)
    rest = x - high.astype(F32)
    middle = rest.astype(BF16)
    return high, middle, (rest - middle.astype(F32)).astype(BF16)


def dot_split(a, b, dims):
    (a_high, a_low), (b_high, b_low) = a, b
    return dot(a_high, b_high, dims) + (dot(a_high, b_low, dims) + dot(a_low, b_high, dims))


def block_row_product(window, chosen, blocks, rr):
    total = None
    count = blocks.shape[1]
    width = blocks.shape[3]
    for k in range(0, count, 2):
        taken = [window[:, pl.ds(pl.multiple_of(chosen(k + e) * width, LANES), width)] for e in (0, 1)]
        left = jnp.concatenate(taken, axis=1)
        right = jnp.concatenate([blocks[rr, k], blocks[rr, k + 1]], axis=1)
        term = dot(left, right, NT)
        total = term if total is None else total + term
    return total


def near_kernel(place, columns, blocks, samples, near, window):
    step = pl.program_id(0)
    width = blocks.shape[3]
    rows_step = blocks.shape[0]
    count = rows_step * pl.num_programs(0)

    @pl.when(step == 0)
    def _():
        window[:, : samples.shape[1]] = samples[...]
        window[:, samples.shape[1] :] = jnp.zeros((samples.shape[0], width), BF16)

    for rr in range(rows_step):

        def chosen(k):
            local = columns[step * rows_step + rr, k] - place[0] * count
            return jnp.where((local >= 0) & (local < count), local, count)

        near[:, rr * width : (rr + 1) * width] = block_row_product(window, chosen, blocks, rr)


def far_kernel(sample_parts, place, columns, blocks, *refs):
    pieces = refs[: 2 * sample_parts]
    near, products, z_high, z_low, packed, window, z_scr, gram, cross = refs[2 * sample_parts :]
    step = pl.program_id(0)
    steps = pl.num_programs(0)
    width = blocks.shape[3]
    rows_step = blocks.shape[0]
    count = rows_step * steps
    own = near.shape[0]
    reach = HB * width

    @pl.when(step == 0)
    def _():
        for d in range(sample_parts):
            source = lax.rem(place[1] + sample_parts - d, sample_parts)
            rows = pl.ds(pl.multiple_of(source * own, own), own)
            window[rows, :reach] = pieces[2 * d][...]
            window[rows, reach : 2 * reach] = pieces[2 * d + 1][...]
        window[:, 2 * reach :] = jnp.zeros((window.shape[0], width), BF16)
        gram[...] = jnp.zeros_like(gram)
        cross[...] = jnp.zeros_like(cross)

    for rr in range(rows_step):

        def chosen(k):
            local = columns[step * rows_step + rr, k] - place[0] * count
            below = jnp.clip(local + HB, 0, HB - 1)
            above = jnp.clip(local - count + HB, HB, 2 * HB - 1)
            return jnp.where(local < 0, below, jnp.where(local < count, 2 * HB, above))

        z_scr[:, rr * width : (rr + 1) * width] = block_row_product(window, chosen, blocks, rr)
    remote = z_scr[...]
    high, low = split_two(remote)
    z_high[...] = high
    z_low[...] = low
    products[...] = near[...] + z_scr[pl.ds(pl.multiple_of(place[1] * own, own), own), :]
    gram[...] += dot(high, high, NT)
    cross[...] += dot(high, low, NT)

    @pl.when(step == steps - 1)
    def _():
        pack_symmetric(packed, gram[...] + (cross[...] + cross[...].T))


def square_iota(n):
    return lax.broadcasted_iota(jnp.int32, (n, n), 0), lax.broadcasted_iota(jnp.int32, (n, n), 1)


def pack_symmetric(packed, full):
    h = full.shape[0] // 2
    row, col = square_iota(h)
    first = full[:h, :h]
    packed[:h, :] = full[:h, h:]
    packed[h : 2 * h, :] = jnp.where(row > col, first, full[h:, h:])
    diagonal = jnp.sum(jnp.where(row == col, first, 0.0), axis=0, keepdims=True)
    packed[2 * h :, :] = jnp.broadcast_to(diagonal, (GROUP, h))


def unpack_symmetric(packed, full, b):
    h = packed.shape[1]
    row, col = square_iota(h)
    shared = packed[h : 2 * h, :]
    lower = jnp.where(row > col, shared, 0.0)
    diagonal = jnp.where(row == col, jnp.broadcast_to(packed[2 * h : 2 * h + 1, :], (h, h)), 0.0)
    upper = jnp.where(row <= col, shared, 0.0)
    full[b, :h, :h] = lower + lower.T + diagonal
    full[b, h:, h:] = upper + jnp.where(row < col, upper, 0.0).T
    full[b, :h, h:] = packed[:h, :]


def row_of(x, j):
    return jnp.broadcast_to(x[:, j : j + 1, :], x.shape)


def factor(a, m):
    batch, n, _ = a.shape
    chunks = n // LANES
    groups = PANEL // GROUP
    tile = (batch, GROUP, LANES)
    sub = lax.broadcasted_iota(jnp.int32, tile, 1)
    lane = lax.broadcasted_iota(jnp.int32, tile, 2)
    for c in range(chunks):
        for b in range(batch):
            row, col = square_iota(LANES)
            for e in range(c + 1):
                m[b, c * LANES : (c + 1) * LANES, e * LANES : (e + 1) * LANES] = (
                    (row == col).astype(F32) if e == c else jnp.zeros((LANES, LANES), F32)
                )
            for e in range(c + 1, chunks):
                m[b, c * LANES : (c + 1) * LANES, e * LANES : (e + 1) * LANES] = jnp.zeros((LANES, LANES), F32)
    for p in range(0, n, PANEL):
        ch = p // LANES
        parts = [(a, c) for c in range(ch, chunks)] + [(m, c) for c in range(ch + 1)]
        rows = [slice(p + GROUP * g, p + GROUP * (g + 1)) for g in range(groups)]
        r = [[ref[:, rows[g], c * LANES : (c + 1) * LANES] for ref, c in parts] for g in range(groups)]
        for g0 in range(groups):
            at = p - ch * LANES + GROUP * g0
            v = [
                [jnp.broadcast_to(r[g][0][:, :, at + k : at + k + 1], tile) for k in range(GROUP)]
                if g >= g0
                else None
                for g in range(groups)
            ]
            head, top = v[g0], r[g0]
            recips, v_rows, r_rows = [], [], []
            pivots = None
            for j in range(GROUP):
                d = row_of(head[j], j)
                rc = 1.0 / d
                recips.append(rc)
                pivots = d if pivots is None else jnp.where(sub == j, d, pivots)
                v_rows.append([row_of(head[k], j) if k > j else None for k in range(GROUP)])
                r_rows.append([row_of(x, j) for x in top])
                if j < GROUP - 1:
                    below = jnp.where(sub > j, head[j], 0.0)
                    scaled = below * rc
                    for k in range(j + 1, GROUP):
                        if k == j + 1:
                            head[k] = head[k] - (below * v_rows[j][k]) * rc
                        else:
                            head[k] = head[k] - scaled * v_rows[j][k]
                    for x in range(len(top)):
                        top[x] = top[x] - scaled * r_rows[j][x]
            for g in range(g0 + 1, groups):
                for j in range(GROUP):
                    scaled = v[g][j] * recips[j]
                    for k in range(j + 1, GROUP):
                        v[g][k] = v[g][k] - scaled * v_rows[j][k]
                    for x in range(len(top)):
                        r[g][x] = r[g][x] - scaled * r_rows[j][x]
            scale = lax.rsqrt(pivots)
            for x, (ref, c) in enumerate(parts):
                done = top[x] * scale
                if ref is a and c == ch:
                    done = jnp.where(lane >= sub + at, done, 0.0)
                r[g0][x] = done
                ref[:, rows[g0], c * LANES : (c + 1) * LANES] = done
        if p + PANEL == n:
            break
        for b in range(batch):
            panel = jnp.concatenate(
                [jnp.concatenate([r[g][x][b] for g in range(groups)], axis=0) for x in range(len(parts))], axis=1
            )
            h, mid, low = split_three(panel)
            left = jnp.concatenate([h, h, mid, mid, h, low], axis=0)
            right = jnp.concatenate([h, mid, h, mid, low, h], axis=0)
            for c in range(ch, chunks):
                start = max(p + PANEL, c * LANES)
                stop = (c + 1) * LANES
                if start >= stop:
                    continue
                x0 = c - ch
                update = dot(left[:, x0 * LANES : (x0 + 1) * LANES], right, TN)[start - c * LANES :, :]
                for x, (ref, e) in enumerate(parts):
                    if ref is a and e < c:
                        continue
                    lanes = slice(e * LANES, (e + 1) * LANES)
                    ref[b, start:stop, lanes] = ref[b, start:stop, lanes] - update[:, x * LANES : (x + 1) * LANES]
    for b in range(batch):
        for c in range(1, chunks):
            for e in range(c):
                a[b, c * LANES : (c + 1) * LANES, e * LANES : (e + 1) * LANES] = jnp.zeros((LANES, LANES), F32)


def leaf_kernel(scale, place, packed, z_high, z_low, bases, upper_own, a, m):
    unpack_symmetric(packed, a, 0)
    factor(a, m)
    own = upper_own.shape[0]
    rows = pl.ds(pl.multiple_of(place[1] * own, own), own)
    upper_own[...] = a[0, rows, :]
    inverse = split_two(m[0, rows, :] * scale)
    for c in range(0, z_high.shape[1], 512):
        lanes = slice(c, c + 512)
        bases[:, lanes] = dot_split(inverse, (z_high[:, lanes], z_low[:, lanes]), NN)


def tree_kernel(top_scale, place, upper_own, *refs):
    levels = (len(refs) - 3) // 2
    packed = refs[:levels]
    transfers = refs[levels : 2 * levels]
    top, a, m = refs[2 * levels :]
    for b in range(levels):
        unpack_symmetric(packed[b], a, b)
    factor(a, m)
    own = upper_own.shape[0]
    rows = pl.ds(pl.multiple_of(place[1] * own, own), own)
    for b in range(levels):
        child = upper_own[...] if b == 0 else a[b - 1, rows, :]
        transfers[b][...] = dot_split(split_two(m[b]), split_two(child), NT)
    top[...] = (a[levels - 1, rows, :] * top_scale).T


def whole():
    return pl.BlockSpec(memory_space=pltpu.VMEM)


def params():
    return pltpu.CompilerParams(vmem_limit_bytes=VMEM_LIMIT)


def from_partner(block, axis, bit):
    count = lax.axis_size(axis)
    route = []
    for low in range(count):
        high = low | 1 << bit
        if high != low and high < count:
            route += [(low, high), (high, low)]
    return lax.ppermute(block, axis, route)


def halo_pieces(samples, reach):
    leaves, parts = lax.axis_size("leaf"), lax.axis_size("samp")
    head = samples[:, :reach]
    tail = samples[:, samples.shape[1] - reach :]
    pieces = []
    for d in range(parts):
        up, down = [], []
        for leaf in range(leaves):
            for part in range(parts):
                source = leaf * parts + part
                other = (part + d) % parts
                if leaf + 1 < leaves:
                    up.append((source, (leaf + 1) * parts + other))
                if leaf > 0:
                    down.append((source, (leaf - 1) * parts + other))
        pieces.append(lax.ppermute(tail, ("leaf", "samp"), up))
        pieces.append(lax.ppermute(head, ("leaf", "samp"), down))
    return pieces


def shards(stiffness, columns, samples):
    blocks_here, slots, width, _ = stiffness.shape
    own, row_count = samples.shape
    parts = lax.axis_size("samp")
    total = own * parts
    reach = HB * width
    place = jnp.stack([lax.axis_index("leaf"), lax.axis_index("samp")]).astype(jnp.int32)
    steps = blocks_here // ROWS_A_STEP
    step_lanes = ROWS_A_STEP * width
    shape = jax.ShapeDtypeStruct

    pieces = halo_pieces(samples, reach)

    block_spec = pl.BlockSpec((ROWS_A_STEP, slots, width, width), lambda i, *_: (i, 0, 0, 0))
    own_spec = pl.BlockSpec((own, step_lanes), lambda i, *_: (0, i))
    all_spec = pl.BlockSpec((total, step_lanes), lambda i, *_: (0, i))

    def fixed(*dims):
        return pl.BlockSpec(dims, lambda i, *_: (0,) * len(dims))

    near = pl.pallas_call(
        near_kernel,
        grid_spec=pltpu.PrefetchScalarGridSpec(
            num_scalar_prefetch=2,
            grid=(steps,),
            in_specs=[block_spec, fixed(own, row_count)],
            out_specs=own_spec,
            scratch_shapes=[pltpu.VMEM((own, row_count + width), BF16)],
        ),
        out_shape=shape((own, row_count), F32),
        compiler_params=params(),
        cost_estimate=pl.CostEstimate(
            flops=2 * own * slots * width * row_count, bytes_accessed=6 * 1024 * 1024, transcendentals=0
        ),
        name="near",
    )(place, columns, stiffness, samples)

    packed_shape = (total + GROUP, total // 2)
    products, z_high, z_low, packed = pl.pallas_call(
        functools.partial(far_kernel, parts),
        grid_spec=pltpu.PrefetchScalarGridSpec(
            num_scalar_prefetch=2,
            grid=(steps,),
            in_specs=[block_spec] + [fixed(own, reach)] * (2 * parts) + [own_spec],
            out_specs=[own_spec, all_spec, all_spec, fixed(*packed_shape)],
            scratch_shapes=[
                pltpu.VMEM((total, 2 * reach + width), BF16),
                pltpu.VMEM((total, step_lanes), F32),
                pltpu.VMEM((total, total), F32),
                pltpu.VMEM((total, total), F32),
            ],
        ),
        out_shape=[
            shape((own, row_count), F32),
            shape((total, row_count), BF16),
            shape((total, row_count), BF16),
            shape(packed_shape, F32),
        ],
        compiler_params=params(),
        name="far",
    )(place, columns, stiffness, *pieces, near)

    smem = pl.BlockSpec(memory_space=pltpu.SMEM)
    grams = []
    current = packed
    for height in range(LEVELS):
        current = current + from_partner(current, "leaf", height)
        grams.append(current)

    def factor_scratch(batch):
        return [pltpu.VMEM((batch, total, total), F32)] * 2

    bases, upper_own = pl.pallas_call(
        functools.partial(leaf_kernel, math.sqrt(row_count)),
        in_specs=[smem] + [whole()] * 3,
        out_specs=[whole()] * 2,
        out_shape=[shape((own, row_count), F32), shape((own, total), F32)],
        scratch_shapes=factor_scratch(1),
        compiler_params=params(),
        name="leaf",
    )(place, packed, z_high, z_low)

    outs = pl.pallas_call(
        functools.partial(tree_kernel, 1.0 / math.sqrt(2**LEVELS * row_count)),
        in_specs=[smem, whole()] + [whole()] * LEVELS,
        out_specs=[whole()] * (LEVELS + 1),
        out_shape=[shape((total, own), F32)] * (LEVELS + 1),
        scratch_shapes=factor_scratch(LEVELS),
        compiler_params=params(),
        name="tree",
    )(place, upper_own, *grams)
    return (products, bases, *outs)


def solution(mesh):
    return jax.shard_map(
        shards,
        mesh=mesh,
        in_specs=(P("leaf", None, None, None), P("leaf", None), P("samp", "leaf")),
        out_specs=(
            P("samp", "leaf"),
            P("samp", "leaf"),
            P("leaf", "samp"),
            P("leaf", "samp"),
            P("leaf", "samp"),
            P("leaf", "samp"),
        ),
        check_vma=False,
    )
```

time: 333 us -> 63.1 us (0.19)
  other arithmetic: 219 us -> 0.13 us
  waiting for transfers between devices: 45.2 us -> 4.9 us
  Pallas kernels: 0 us -> 35 us
  matrix products: 23.2 us -> 0 us
  local copies, waits for them, and re-layouts: 24.2 us -> 4.98 us
  between operations: 14.4 us -> 0.72 us
  starting transfers between devices: 6.86 us -> 16.9 us
    another operation x17 -> x1, other arithmetic: 215 us -> 0.07 us  [shards(): jnp.stack([lax.axis_index('leaf'), lax.axis_index('samp')])]
    all_gather x1 -> x0, waiting for transfers between devices: 37.4 us -> none  [shards(): gathered = lax.all_gather(distant_portion, 'samp', axis=0, tiled=True)]
    pallas_call x0 -> x4, Pallas kernels: none -> 35 us  [the longest x1 12.7 us: shards(): pl.pallas_call(functools.partial(tree_kernel, 1.0 / math.sqrt(2 ** LEVELS...]
    dot_general x3 -> x0, matrix products: 14.7 us -> none  [the longest x1 5.81 us: shards(): jnp.einsum('rkij,srkj->sri', stiffness_block_row, near_terms, preferred_e...]
    another operation x16 -> x0, local copies, waits for them, and re-layouts: 11.6 us -> none
    another operation x8 -> x0, matrix products: 8.49 us -> none  [the longest x6 7.44 us: lower_solve(): return jax.scipy.linalg.solve_triangular(factor, right_side, lower=True)]
    ppermute x2 -> x4, starting transfers between devices: 3.66 us -> 11.7 us  [the longest x2 9.09 us: halo_pieces(): pieces.append(lax.ppermute(tail, ('leaf', 'samp'), up))]
    gather x2 -> x0, local copies, waits for them, and re-layouts: 6.07 us -> none  [pick_blocks(): picked = jnp.take(sample_blocks, positions.reshape(-1), axis=1)]
  transfers between devices with their start and end apart: 6 -> 7, of which waited for: 4 -> 2; matrix products, arithmetic and copies ran while one was open for 4% -> 1% of each run, Pallas kernels for 0% -> 21%
where the time goes in v1:
time: 63.1 us; the launch traced here: 62.6 us
  Pallas kernels  35 us (55%)
  starting transfers between devices  16.9 us (27%)
  local copies, waits for them, and re-layouts  4.98 us (8%)
  waiting for transfers between devices  4.9 us (8%)
  between operations  0.72 us (1%)
    pallas_call x1, Pallas kernels, shards(): pl.pallas_call(functools.partial(tree_kernel, 1.0 / math.sqrt(2 ** LEVELS...  12.7 us
    pallas_call x1, Pallas kernels, shards(): pl.pallas_call(functools.partial(leaf_kernel, math.sqrt(row_count)), in_s...  9.66 us
    pallas_call x1, Pallas kernels, shards(): pl.pallas_call(functools.partial(far_kernel, parts), grid_spec=pltpu.Pref...  9.29 us
    ppermute x2, starting transfers between devices, halo_pieces(): pieces.append(lax.ppermute(tail, ('leaf', 'samp'), up))  9.09 us
    ppermute x3, starting transfers between devices, from_partner(): return lax.ppermute(block, axis, route)  5.2 us
    ppermute x3, waiting for transfers between devices, from_partner(): return lax.ppermute(block, axis, route)  4.89 us
    unnamed x5, local copies, waits for them, and re-layouts  3.99 us
    pallas_call x1, Pallas kernels, shards(): pl.pallas_call(near_kernel, grid_spec=pltpu.PrefetchScalarGridSpec(num_sc...  3.31 us
  transfers between devices with their start and end apart: 7, of which 2 were waited for; matrix products, arithmetic and copies ran while one was open for 1% of the time, Pallas kernels for 21%

profile of v1, /device:TPU:0, one launch (start us, length us, event | category | flops | bytes accessed | tf_op | source)
XLA Modules:
  0.0 62.6 jit_solution(2979008912121587476)
XLA Ops:
  0.6 1.0 %fusion = (bf16[128,512]{1,0:T(8,128)(2,1)S(1)}, bf16[128,512]{1,0:T(8,128)(2,1)S(1)}) fusion(bf16[128,2048]{1,0:T(8,128)(2,1)} %samples.1), kind=kLoop, calls=%fused_computation.1 | loop fusion | bytes 524288 | tf_op jit(solution)/shard_map/slice | solution.py:291
  1.6 1.3 %collective-permute-start.3 = (bf16[128,512]{1,0:T(8,128)(2,1)S(1)}, bf16[128,512]{1,0:T(8,128)(2,1)S(1)}, u32[]{:S(2)}, u32[]{:S(2)}) collective-permute-start(bf16[128,512]{1,0:T(8,128)(2,1)S(1)} %get-tuple-element.26), channel_id=1, source_target_pairs={{2,1},{3,0},{4,3},{5,2},{6,5},{7,4},{8,7},{9,6},{10,9},{11,8},{12,... | collective-permute-start | bytes 393224 | tf_op jit(solution)/shard_map/ppermute | solution.py:305
  2.9 1.3 %collective-permute-start.1 = (bf16[128,512]{1,0:T(8,128)(2,1)S(1)}, bf16[128,512]{1,0:T(8,128)(2,1)S(1)}, u32[]{:S(2)}, u32[]{:S(2)}) collective-permute-start(bf16[128,512]{1,0:T(8,128)(2,1)S(1)} %get-tuple-element.26), channel_id=1, source_target_pairs={{2,0},{3,1},{4,2},{5,3},{6,4},{7,5},{8,6},{9,7},{10,8},{11,9},{12,... | collective-permute-start | bytes 393224 | tf_op jit(solution)/shard_map/ppermute | solution.py:305
  4.2 5.6 %collective-permute-start.2 = (bf16[128,512]{1,0:T(8,128)(2,1)S(1)}, bf16[128,512]{1,0:T(8,128)(2,1)S(1)}, u32[]{:S(2)}, u32[]{:S(2)}) collective-permute-start(bf16[128,512]{1,0:T(8,128)(2,1)S(1)} %get-tuple-element.27), channel_id=1, source_target_pairs={{0,3},{1,2},{2,5},{3,4},{4,7},{5,6},{6,9},{7,8},{8,11},{9,10},{10,... | collective-permute-start | bytes 393224 | tf_op jit(solution)/shard_map/ppermute | solution.py:304
  9.8 3.5 %collective-permute-start = (bf16[128,512]{1,0:T(8,128)(2,1)S(1)}, bf16[128,512]{1,0:T(8,128)(2,1)S(1)}, u32[]{:S(2)}, u32[]{:S(2)}) collective-permute-start(bf16[128,512]{1,0:T(8,128)(2,1)S(1)} %get-tuple-element.27), channel_id=1, source_target_pairs={{0,2},{1,3},{2,4},{3,5},{4,6},{5,7},{6,8},{7,9},{8,10},{9,11},{10,... | collective-permute-start | bytes 393224 | tf_op jit(solution)/shard_map/ppermute | solution.py:304
  13.3 0.8 %copy.10.columns = s32[16,8]{1,0:T(8,128)S(1)} copy(s32[16,8]{0,1:T(8,128)} %param.4) | data formatting | bytes 1024 | tf_op args[1]
  14.1 0.1 pad_add_fusion.place
  14.2 0.0 copy-start
  14.2 2.2 %copy-done = bf16[16,8,128,128]{3,2,1,0:T(8,128)(2,1)S(1)} copy-done((bf16[16,8,128,128]{3,2,1,0:T(8,128)(2,1)S(1)}, bf16[16,8,128,128]{3,2,1,0:T(8,128)(2,1)}, u32[]{:S(2)}) %copy-start) | copy-done | bytes 4194328
  16.4 0.0 copy-start.1
  16.4 1.0 %copy-done.1 = bf16[128,2048]{1,0:T(8,128)(2,1)S(1)} copy-done((bf16[128,2048]{1,0:T(8,128)(2,1)S(1)}, bf16[128,2048]{1,0:T(8,128)(2,1)}, u32[]{:S(2)}) %copy-start.1) | copy-done | bytes 524312
  17.4 3.3 %near.1.refs_4_ = f32[128,2048]{1,0:T(8,128)S(1)} custom-call(s32[2]{0:T(128)S(1)} %pad_add_fusion.place, s32[16,8]{1,0:T(8,128)S(1)} %copy.10.columns, bf16[16,8,128,128]{3,2,1,0:T(8,128)(2,1)S(1)} %copy-done, bf16[128,2048]{1,0:T(8,128)(2,1)S(1)} %copy-done.1), custom_call_target="tpu_custom_call" | custom-call | flops 536870912 | bytes 6291456 | tf_op jit(solution)/shard_map/near/pallas_call | solution.py:329
  20.7 0.0 collective-permute-done.3.refs_3_
  20.7 0.0 collective-permute-done.1.refs_1_
  20.7 0.0 collective-permute-done.2.refs_2_
  20.7 0.0 collective-permute-done.refs_0_
  20.8 9.3 %far.1 = (f32[128,2048]{1,0:T(8,128)}, bf16[256,2048]{1,0:T(8,128)(2,1)S(1)}, bf16[256,2048]{1,0:T(8,128)(2,1)S(1)}, f32[264,128]{1,0:T(8,128)S(1)}) custom-call(s32[2]{0:T(128)S(1)} %pad_add_fusion.place, s32[16,8]{1,0:T(8,128)S(1)} %copy.10.columns, bf16[16,8,128,128]{3,2,1,0:T(8,128)(2,1)} %blocks.3, bf16[128,512]{1,0:T(8,128)(2,1)S(1)} %collective-permute-done.refs_0_, ...), custom_call_target="tpu_custom_call" | custom-call | tf_op jit(solution)/shard_map/far/pallas_call | solution.py:347
  30.0 0.8 %collective-permute-start.4 = (f32[264,128]{1,0:T(8,128)S(1)}, f32[264,128]{1,0:T(8,128)S(1)}, u32[]{:S(2)}, u32[]{:S(2)}) collective-permute-start(f32[264,128]{1,0:T(8,128)S(1)} %get-tuple-element.17.packed), channel_id=1, source_target_pairs={{0,2},{2,0},{4,6},{6,4},{8,10},{10,8},{12,14},{14,12},{16,18},{18,... | collective-permute-start | bytes 405512 | tf_op jit(solution)/shard_map/ppermute | solution.py:286
  30.8 1.0 %collective-permute-done.4 = f32[264,128]{1,0:T(8,128)S(1)} collective-permute-done((f32[264,128]{1,0:T(8,128)S(1)}, f32[264,128]{1,0:T(8,128)S(1)}, u32[]{:S(2)}, u32[]{:S(2)}) %collective-permute-start.4) | collective-permute-done | bytes 135200 | tf_op jit(solution)/shard_map/ppermute | solution.py:286
  31.8 2.8 %collective-permute-start.5 = (f32[264,128]{1,0:T(8,128)S(1)}, f32[264,128]{1,0:T(8,128)S(1)}, u32[]{:S(2)}, u32[]{:S(2)}) collective-permute-start(f32[264,128]{1,0:T(8,128)S(1)} %add.9.refs_0_), channel_id=1, source_target_pairs={{0,4},{4,0},{2,6},{6,2},{8,12},{12,8},{10,14},{14,10},{16,20},{20,... | collective-permute-start | bytes 405512 | tf_op jit(solution)/shard_map/ppermute | solution.py:286
  34.6 3.9 %collective-permute-done.5 = f32[264,128]{1,0:T(8,128)S(1)} collective-permute-done((f32[264,128]{1,0:T(8,128)S(1)}, f32[264,128]{1,0:T(8,128)S(1)}, u32[]{:S(2)}, u32[]{:S(2)}) %collective-permute-start.5) | collective-permute-done | bytes 135200 | tf_op jit(solution)/shard_map/ppermute | solution.py:286
  38.5 1.6 %collective-permute-start.6 = (f32[264,128]{1,0:T(8,128)S(1)}, f32[264,128]{1,0:T(8,128)S(1)}, u32[]{:S(2)}, u32[]{:S(2)}) collective-permute-start(f32[264,128]{1,0:T(8,128)S(1)} %add.10.refs_1_), channel_id=1, source_target_pairs={{0,8},{8,0},{2,10},{10,2},{4,12},{12,4},{6,14},{14,6},{16,24},{24,... | collective-permute-start | bytes 405512 | tf_op jit(solution)/shard_map/ppermute | solution.py:286
  40.2 9.7 %leaf.1 = (f32[128,2048]{1,0:T(8,128)}, f32[128,256]{1,0:T(8,128)S(1)}) custom-call(s32[2]{0:T(128)S(1)} %pad_add_fusion.place, f32[264,128]{1,0:T(8,128)S(1)} %get-tuple-element.17.packed, bf16[256,2048]{1,0:T(8,128)(2,1)S(1)} %get-tuple-element.18.z_high, bf16[256,2048]{1,0:T(8,128)(2,1)S(1)} %get-tuple-element.19.z_low), custom_call_target="tpu_custom_call" | custom-call | tf_op jit(solution)/shard_map/leaf/pallas_call | solution.py:381
  49.8 0.0 collective-permute-done.6
  49.9 12.7 %tree.1 = (f32[256,128]{1,0:T(8,128)}, f32[256,128]{1,0:T(8,128)}, f32[256,128]{1,0:T(8,128)}, f32[256,128]{1,0:T(8,128)}) custom-call(s32[2]{0:T(128)S(1)} %pad_add_fusion.place, f32[128,256]{1,0:T(8,128)S(1)} %get-tuple-element.21.upper_own, f32[264,128]{1,0:T(8,128)S(1)} %add.9.refs_0_, f32[264,128]{1,0:T(8,128)S(1)} %add.10.refs_1_, ...), custom_call_target="tpu_custom_call" | custom-call | tf_op jit(solution)/shard_map/tree/pallas_call | solution.py:391
  (3 shorter events, 0.1 us)
Async XLA Ops:
  1.6 19.1 %collective-permute-start.3 = (bf16[128,512]{1,0:T(8,128)(2,1)S(1)}, bf16[128,512]{1,0:T(8,128)(2,1)S(1)}, u32[]{:S(2)}, u32[]{:S(2)}) collective-permute-start(bf16[128,512]{1,0:T(8,128)(2,1)S(1)} %get-tuple-element.26), channel_id=1, source_target_pairs={{2,1},{3,0},{4,3},{5,2},{6,5},{7,4},{8,7},{9,6},{10,9},{11,8},{12,... | collective-permute-start | bytes 393224 | tf_op jit(solution)/shard_map/ppermute | solution.py:305
  2.9 17.8 %collective-permute-start.1 = (bf16[128,512]{1,0:T(8,128)(2,1)S(1)}, bf16[128,512]{1,0:T(8,128)(2,1)S(1)}, u32[]{:S(2)}, u32[]{:S(2)}) collective-permute-start(bf16[128,512]{1,0:T(8,128)(2,1)S(1)} %get-tuple-element.26), channel_id=1, source_target_pairs={{2,0},{3,1},{4,2},{5,3},{6,4},{7,5},{8,6},{9,7},{10,8},{11,9},{12,... | collective-permute-start | bytes 393224 | tf_op jit(solution)/shard_map/ppermute | solution.py:305
  4.2 16.5 %collective-permute-start.2 = (bf16[128,512]{1,0:T(8,128)(2,1)S(1)}, bf16[128,512]{1,0:T(8,128)(2,1)S(1)}, u32[]{:S(2)}, u32[]{:S(2)}) collective-permute-start(bf16[128,512]{1,0:T(8,128)(2,1)S(1)} %get-tuple-element.27), channel_id=1, source_target_pairs={{0,3},{1,2},{2,5},{3,4},{4,7},{5,6},{6,9},{7,8},{8,11},{9,10},{10,... | collective-permute-start | bytes 393224 | tf_op jit(solution)/shard_map/ppermute | solution.py:304
  9.8 10.9 %collective-permute-start = (bf16[128,512]{1,0:T(8,128)(2,1)S(1)}, bf16[128,512]{1,0:T(8,128)(2,1)S(1)}, u32[]{:S(2)}, u32[]{:S(2)}) collective-permute-start(bf16[128,512]{1,0:T(8,128)(2,1)S(1)} %get-tuple-element.27), channel_id=1, source_target_pairs={{0,2},{1,3},{2,4},{3,5},{4,6},{5,7},{6,8},{7,9},{8,10},{9,11},{10,... | collective-permute-start | bytes 393224 | tf_op jit(solution)/shard_map/ppermute | solution.py:304
  14.2 2.2 %copy-start = (bf16[16,8,128,128]{3,2,1,0:T(8,128)(2,1)S(1)}, bf16[16,8,128,128]{3,2,1,0:T(8,128)(2,1)}, u32[]{:S(2)}) copy-start(bf16[16,8,128,128]{3,2,1,0:T(8,128)(2,1)} %blocks.3) | copy-start | bytes 12582916
  16.4 1.0 %copy-start.1 = (bf16[128,2048]{1,0:T(8,128)(2,1)S(1)}, bf16[128,2048]{1,0:T(8,128)(2,1)}, u32[]{:S(2)}) copy-start(bf16[128,2048]{1,0:T(8,128)(2,1)} %samples.1) | copy-start | bytes 1572868
  30.0 1.8 %collective-permute-start.4 = (f32[264,128]{1,0:T(8,128)S(1)}, f32[264,128]{1,0:T(8,128)S(1)}, u32[]{:S(2)}, u32[]{:S(2)}) collective-permute-start(f32[264,128]{1,0:T(8,128)S(1)} %get-tuple-element.17.packed), channel_id=1, source_target_pairs={{0,2},{2,0},{4,6},{6,4},{8,10},{10,8},{12,14},{14,12},{16,18},{18,... | collective-permute-start | bytes 405512 | tf_op jit(solution)/shard_map/ppermute | solution.py:286
  31.8 6.7 %collective-permute-start.5 = (f32[264,128]{1,0:T(8,128)S(1)}, f32[264,128]{1,0:T(8,128)S(1)}, u32[]{:S(2)}, u32[]{:S(2)}) collective-permute-start(f32[264,128]{1,0:T(8,128)S(1)} %add.9.refs_0_), channel_id=1, source_target_pairs={{0,4},{4,0},{2,6},{6,2},{8,12},{12,8},{10,14},{14,10},{16,20},{20,... | collective-permute-start | bytes 405512 | tf_op jit(solution)/shard_map/ppermute | solution.py:286
  38.5 11.3 %collective-permute-start.6 = (f32[264,128]{1,0:T(8,128)S(1)}, f32[264,128]{1,0:T(8,128)S(1)}, u32[]{:S(2)}, u32[]{:S(2)}) collective-permute-start(f32[264,128]{1,0:T(8,128)S(1)} %add.10.refs_1_), channel_id=1, source_target_pairs={{0,8},{8,0},{2,10},{10,2},{4,12},{12,4},{6,14},{14,6},{16,24},{24,... | collective-permute-start | bytes 405512 | tf_op jit(solution)/shard_map/ppermute | solution.py:286

commit v2 on v1

v2 whole, which is shorter than its diff:
```python
import functools
import math

import jax
import jax.numpy as jnp
from jax import lax
from jax.experimental import pallas as pl
from jax.experimental.pallas import tpu as pltpu
from jax.sharding import PartitionSpec as P

HB = 4
LEVELS = 3
LANES = 128
GROUP = 8
PANEL = 32
ROWS_A_STEP = 4
VMEM_LIMIT = 48 * 1024 * 1024
F32 = jnp.float32
BF16 = jnp.bfloat16
NN = (((1,), (0,)), ((), ()))
NT = (((1,), (1,)), ((), ()))
TN = (((0,), (0,)), ((), ()))


def dot(a, b, dims):
    return lax.dot_general(a, b, dims, preferred_element_type=F32)


def split_two(x):
    high = x.astype(BF16)
    return high, (x - high.astype(F32)).astype(BF16)


def split_three(x):
    high = x.astype(BF16)
    rest = x - high.astype(F32)
    middle = rest.astype(BF16)
    return high, middle, (rest - middle.astype(F32)).astype(BF16)


def dot_split(a, b, dims):
    (a_high, a_low), (b_high, b_low) = a, b
    return dot(a_high, b_high, dims) + (dot(a_high, b_low, dims) + dot(a_low, b_high, dims))


def taken(window, chosen, slots, width):
    lanes = [pl.ds(pl.multiple_of(chosen(k) * width, LANES), width) for k in range(slots)]
    return jnp.concatenate([window[:, at] for at in lanes], axis=1)


def block_row(blocks, rr):
    return jnp.concatenate([blocks[rr, k] for k in range(blocks.shape[1])], axis=1)


def far_position(local, count, odd):
    lower = jnp.where(odd, 0, HB)
    below = jnp.clip(local + HB, 0, HB - 1) + lower
    above = jnp.clip(local - count, 0, HB - 1) + (HB - lower)
    return jnp.where(local < 0, below, jnp.where(local < count, 2 * HB, above))


def own_kernel(place, columns, blocks, samples, halo, products, z_high, z_low, near_window, far_window):
    step = pl.program_id(0)
    rows_step, slots, width, _ = blocks.shape
    count = rows_step * pl.num_programs(0)
    own = samples.shape[0]
    odd = lax.rem(place[0], 2) == 1

    @pl.when(step == 0)
    def _():
        near_window[:, : samples.shape[1]] = samples[...]
        near_window[:, samples.shape[1] :] = jnp.zeros((own, width), BF16)
        far_window[:, : halo.shape[1]] = halo[...]
        far_window[:, halo.shape[1] :] = jnp.zeros((own, width), BF16)

    for rr in range(rows_step):

        def local(k):
            return columns[k, step * rows_step + rr] - place[0] * count

        def near(k):
            return jnp.where((local(k) >= 0) & (local(k) < count), local(k), count)

        def far(k):
            return far_position(local(k), count, odd)

        left = jnp.concatenate(
            [taken(near_window, near, slots, width), taken(far_window, far, slots, width)], axis=0
        )
        both = dot(left, block_row(blocks, rr), NT)
        lanes = slice(rr * width, (rr + 1) * width)
        products[:, lanes] = both[:own] + both[own:]
        z_high[:, lanes], z_low[:, lanes] = split_two(both[own:])


def others_kernel(parts, place, columns, blocks, *refs):
    halos = refs[: parts - 1]
    own_high, own_low, z_high, z_low, packed, window, gram, cross = refs[parts - 1 :]
    step = pl.program_id(0)
    rows_step, slots, width, _ = blocks.shape
    count = rows_step * pl.num_programs(0)
    own = own_high.shape[0]
    odd = lax.rem(place[0], 2) == 1
    rows = [
        pl.ds(pl.multiple_of(lax.rem(place[1] + parts - d, parts) * own, own), own) for d in range(parts)
    ]

    @pl.when(step == 0)
    def _():
        for d in range(1, parts):
            window[(d - 1) * own : d * own, : 2 * HB * width] = halos[d - 1][...]
        window[:, 2 * HB * width :] = jnp.zeros((window.shape[0], width), BF16)
        gram[...] = jnp.zeros_like(gram)
        cross[...] = jnp.zeros_like(cross)

    z_high[rows[0], :] = own_high[...]
    z_low[rows[0], :] = own_low[...]
    for rr in range(rows_step):

        def far(k):
            return far_position(columns[k, step * rows_step + rr] - place[0] * count, count, odd)

        remote = dot(taken(window, far, slots, width), block_row(blocks, rr), NT)
        high, low = split_two(remote)
        lanes = slice(rr * width, (rr + 1) * width)
        for d in range(1, parts):
            z_high[rows[d], lanes] = high[(d - 1) * own : d * own]
            z_low[rows[d], lanes] = low[(d - 1) * own : d * own]
        if rr % 2 == 1:
            pair = slice((rr - 1) * width, (rr + 1) * width)
            high, low = z_high[:, pair], z_low[:, pair]
            gram[...] += dot(high, high, NT)
            cross[...] += dot(high, low, NT)

    @pl.when(step == pl.num_programs(0) - 1)
    def _():
        pack_symmetric(packed, gram[...] + (cross[...] + cross[...].T))


def square_iota(n):
    return lax.broadcasted_iota(jnp.int32, (n, n), 0), lax.broadcasted_iota(jnp.int32, (n, n), 1)


def pack_symmetric(packed, full):
    h = full.shape[0] // 2
    row, col = square_iota(h)
    first = full[:h, :h]
    packed[:h, :] = full[:h, h:]
    packed[h : 2 * h, :] = jnp.where(row > col, first, full[h:, h:])
    diagonal = jnp.sum(jnp.where(row == col, first, 0.0), axis=0, keepdims=True)
    packed[2 * h :, :] = jnp.broadcast_to(diagonal, (GROUP, h))


def unpack_symmetric(packed, full, b):
    h = packed.shape[1]
    row, col = square_iota(h)
    shared = packed[h : 2 * h, :]
    lower = jnp.where(row > col, shared, 0.0)
    diagonal = jnp.where(row == col, jnp.broadcast_to(packed[2 * h : 2 * h + 1, :], (h, h)), 0.0)
    upper = jnp.where(row <= col, shared, 0.0)
    full[b, :h, :h] = lower + lower.T + diagonal
    full[b, h:, h:] = upper + jnp.where(row < col, upper, 0.0).T
    full[b, :h, h:] = packed[:h, :]


def row_of(x, j):
    return jnp.broadcast_to(x[:, j : j + 1, :], x.shape)


def start_inverse(m):
    batch, n, _ = m.shape
    row, col = square_iota(LANES)
    for b in range(batch):
        for c in range(0, n, LANES):
            for e in range(0, n, LANES):
                m[b, c : c + LANES, e : e + LANES] = (
                    (row == col).astype(F32) if e == c else jnp.zeros((LANES, LANES), F32)
                )


def clear_lower(a):
    batch, n, _ = a.shape
    for b in range(batch):
        for c in range(LANES, n, LANES):
            a[b, c : c + LANES, :c] = jnp.zeros((LANES, c), F32)


def factor(a, m, first, last):
    batch, n, _ = a.shape
    chunks = n // LANES
    groups = PANEL // GROUP
    tile = (batch, GROUP, LANES)
    sub = lax.broadcasted_iota(jnp.int32, tile, 1)
    lane = lax.broadcasted_iota(jnp.int32, tile, 2)
    for p in range(first, last, PANEL):
        ch = p // LANES
        parts = [(a, c) for c in range(ch, chunks)] + [(m, c) for c in range(ch + 1)]
        rows = [slice(p + GROUP * g, p + GROUP * (g + 1)) for g in range(groups)]
        r = [[ref[:, rows[g], c * LANES : (c + 1) * LANES] for ref, c in parts] for g in range(groups)]
        for g0 in range(groups):
            at = p - ch * LANES + GROUP * g0
            v = [
                [jnp.broadcast_to(r[g][0][:, :, at + k : at + k + 1], tile) for k in range(GROUP)]
                if g >= g0
                else None
                for g in range(groups)
            ]
            head, top = v[g0], r[g0]
            recips, v_rows, r_rows = [], [], []
            pivots = None
            for j in range(GROUP):
                d = row_of(head[j], j)
                rc = invert(d)
                recips.append(rc)
                pivots = d if pivots is None else jnp.where(sub == j, d, pivots)
                v_rows.append([row_of(head[k], j) if k > j else None for k in range(GROUP)])
                r_rows.append([row_of(x, j) for x in top])
                if j < GROUP - 1:
                    below = jnp.where(sub > j, head[j], 0.0)
                    scaled = below * rc
                    for k in range(j + 1, GROUP):
                        if k == j + 1:
                            head[k] = head[k] - (below * v_rows[j][k]) * rc
                        else:
                            head[k] = head[k] - scaled * v_rows[j][k]
                    for x in range(len(top)):
                        top[x] = top[x] - scaled * r_rows[j][x]
            for g in range(g0 + 1, groups):
                for j in range(GROUP):
                    scaled = v[g][j] * recips[j]
                    for k in range(j + 1, GROUP):
                        v[g][k] = v[g][k] - scaled * v_rows[j][k]
                    for x in range(len(top)):
                        r[g][x] = r[g][x] - scaled * r_rows[j][x]
            scale = lax.rsqrt(pivots)
            for x, (ref, c) in enumerate(parts):
                done = top[x] * scale
                if ref is a and c == ch:
                    done = jnp.where(lane >= sub + at, done, 0.0)
                r[g0][x] = done
                ref[:, rows[g0], c * LANES : (c + 1) * LANES] = done
        if p + PANEL == n:
            break
        for b in range(batch):
            panel = jnp.concatenate(
                [jnp.concatenate([r[g][x][b] for g in range(groups)], axis=0) for x in range(len(parts))], axis=1
            )
            h, mid, low = split_three(panel)
            left = jnp.concatenate([h, h, mid, mid, h, low], axis=0)
            right = jnp.concatenate([h, mid, h, mid, low, h], axis=0)
            for c in range(ch, chunks):
                start = max(p + PANEL, c * LANES)
                stop = (c + 1) * LANES
                if start >= stop:
                    continue
                x0 = c - ch
                update = dot(left[:, x0 * LANES : (x0 + 1) * LANES], right, TN)[start - c * LANES :, :]
                for x, (ref, e) in enumerate(parts):
                    if ref is a and e < c:
                        continue
                    lanes = slice(e * LANES, (e + 1) * LANES)
                    ref[b, start:stop, lanes] = ref[b, start:stop, lanes] - update[:, x * LANES : (x + 1) * LANES]


def invert(x):
    guess = pl.reciprocal(x, approx=True)
    return guess * (2.0 - x * guess)


def own_rows(place, own):
    return pl.ds(pl.multiple_of(place[1] * own, own), own)


def first_kernel(packed_zero, packed_one, a, m):
    unpack_symmetric(packed_zero, a, 0)
    unpack_symmetric(packed_one, a, 1)
    start_inverse(m)
    factor(a, m, 0, a.shape[1] // 2)


def second_kernel(scale, place, a_in, m_in, z_high, z_low, bases, transfer, upper_own, a, m):
    del a_in, m_in
    n = a.shape[1]
    factor(a, m, n // 2, n)
    clear_lower(a)
    own = upper_own.shape[0]
    rows = own_rows(place, own)
    upper_own[...] = a[1, rows, :]
    transfer[...] = dot_split(split_two(m[1]), split_two(a[0, rows, :]), NT)
    inverse = split_two(m[0, rows, :] * scale)
    for c in range(0, z_high.shape[1], 512):
        lanes = slice(c, c + 512)
        bases[:, lanes] = dot_split(inverse, (z_high[:, lanes], z_low[:, lanes]), NN)


def tree_kernel(top_scale, place, upper_own, *refs):
    levels = (len(refs) - 3) // 2
    packed = refs[:levels]
    transfers = refs[levels : 2 * levels]
    top, a, m = refs[2 * levels :]
    for b in range(levels):
        unpack_symmetric(packed[b], a, b)
    start_inverse(m)
    factor(a, m, 0, a.shape[1])
    clear_lower(a)
    own = upper_own.shape[0]
    rows = own_rows(place, own)
    for b in range(levels):
        child = upper_own[...] if b == 0 else a[b - 1, rows, :]
        transfers[b][...] = dot_split(split_two(m[b]), split_two(child), NT)
    top[...] = (a[levels - 1, rows, :] * top_scale).T


def whole():
    return pl.BlockSpec(memory_space=pltpu.VMEM)


def params():
    return pltpu.CompilerParams(vmem_limit_bytes=VMEM_LIMIT)


def from_partner(block, axis, bit):
    count = lax.axis_size(axis)
    route = []
    for low in range(count):
        high = low | 1 << bit
        if high != low and high < count:
            route += [(low, high), (high, low)]
    return lax.ppermute(block, axis, route)


def swap_across(block, odd_start):
    count = lax.axis_size("leaf")
    route = []
    for low in range(odd_start, count - 1, 2):
        route += [(low, low + 1), (low + 1, low)]
    return lax.ppermute(block, "leaf", route)


def sample_shift(block, d):
    count = lax.axis_size("samp")
    return lax.ppermute(block, "samp", [(i, (i + d) % count) for i in range(count)])


def shards(stiffness, columns, samples):
    blocks_here, slots, width, _ = stiffness.shape
    own, row_count = samples.shape
    parts = lax.axis_size("samp")
    total = own * parts
    reach = HB * width
    leaf = lax.axis_index("leaf")
    place = jnp.stack([leaf, lax.axis_index("samp")]).astype(jnp.int32)
    steps = blocks_here // ROWS_A_STEP
    step_lanes = ROWS_A_STEP * width
    shape = jax.ShapeDtypeStruct
    columns = columns.T

    far_end = row_count - reach
    even = leaf % 2 == 0
    first = lax.dynamic_slice_in_dim(samples, jnp.where(even, far_end, 0), reach, 1)
    second = lax.dynamic_slice_in_dim(samples, jnp.where(even, 0, far_end), reach, 1)
    halo = jnp.concatenate([swap_across(first, 0), swap_across(second, 1)], axis=1)
    other_halos = [sample_shift(halo, d) for d in range(1, parts)]

    block_spec = pl.BlockSpec((ROWS_A_STEP, slots, width, width), lambda i, *_: (i, 0, 0, 0))
    own_spec = pl.BlockSpec((own, step_lanes), lambda i, *_: (0, i))
    all_spec = pl.BlockSpec((total, step_lanes), lambda i, *_: (0, i))

    def fixed(*dims):
        return pl.BlockSpec(dims, lambda i, *_: (0,) * len(dims))

    products, own_high, own_low = pl.pallas_call(
        own_kernel,
        grid_spec=pltpu.PrefetchScalarGridSpec(
            num_scalar_prefetch=2,
            grid=(steps,),
            in_specs=[block_spec, fixed(own, row_count), fixed(own, 2 * reach)],
            out_specs=[own_spec] * 3,
            scratch_shapes=[pltpu.VMEM((own, row_count + width), BF16), pltpu.VMEM((own, 2 * reach + width), BF16)],
        ),
        out_shape=[shape((own, row_count), F32), shape((own, row_count), BF16), shape((own, row_count), BF16)],
        compiler_params=params(),
        cost_estimate=pl.CostEstimate(
            flops=4 * own * slots * width * row_count, bytes_accessed=7 * 1024 * 1024, transcendentals=0
        ),
        name="own",
    )(place, columns, stiffness, samples, halo)

    packed_shape = (total + GROUP, total // 2)
    z_high, z_low, packed = pl.pallas_call(
        functools.partial(others_kernel, parts),
        grid_spec=pltpu.PrefetchScalarGridSpec(
            num_scalar_prefetch=2,
            grid=(steps,),
            in_specs=[block_spec] + [fixed(own, 2 * reach)] * (parts - 1) + [own_spec] * 2,
            out_specs=[all_spec, all_spec, fixed(*packed_shape)],
            scratch_shapes=[
                pltpu.VMEM((total - own, 2 * reach + width), BF16),
                pltpu.VMEM((total, total), F32),
                pltpu.VMEM((total, total), F32),
            ],
        ),
        out_shape=[shape((total, row_count), BF16), shape((total, row_count), BF16), shape(packed_shape, F32)],
        compiler_params=params(),
        name="others",
    )(place, columns, stiffness, *other_halos, own_high, own_low)

    smem = pl.BlockSpec(memory_space=pltpu.SMEM)
    square = shape((2, total, total), F32)
    transfer_shape = shape((total, own), F32)
    gram_one = packed + from_partner(packed, "leaf", 0)
    gram_two = gram_one + from_partner(gram_one, "leaf", 1)
    a, m = pl.pallas_call(
        first_kernel,
        in_specs=[whole()] * 2,
        out_specs=[whole()] * 2,
        out_shape=[square] * 2,
        compiler_params=params(),
        cost_estimate=pl.CostEstimate(flops=3 * 10**9, bytes_accessed=1024 * 1024, transcendentals=0),
        name="first",
    )(packed, gram_one)
    gram_three = gram_two + from_partner(gram_two, "leaf", 2)
    bases, transfer_one, upper_own, _, _ = pl.pallas_call(
        functools.partial(second_kernel, math.sqrt(row_count)),
        in_specs=[smem] + [whole()] * 4,
        out_specs=[whole()] * 5,
        out_shape=[shape((own, row_count), F32), transfer_shape, shape((own, total), F32), square, square],
        input_output_aliases={1: 3, 2: 4},
        compiler_params=params(),
        cost_estimate=pl.CostEstimate(flops=3 * 10**9, bytes_accessed=1024 * 1024, transcendentals=0),
        name="second",
    )(place, a, m, z_high, z_low)
    transfer_two, transfer_three, top_factor = pl.pallas_call(
        functools.partial(tree_kernel, 1.0 / math.sqrt(2**LEVELS * row_count)),
        in_specs=[smem] + [whole()] * 3,
        out_specs=[whole()] * 3,
        out_shape=[transfer_shape] * 3,
        scratch_shapes=[pltpu.VMEM((2, total, total), F32)] * 2,
        compiler_params=params(),
        name="tree",
    )(place, upper_own, gram_two, gram_three)
    return (products, bases, transfer_one, transfer_two, transfer_three, top_factor)


def solution(mesh):
    return jax.shard_map(
        shards,
        mesh=mesh,
        in_specs=(P("leaf", None, None, None), P("leaf", None), P("samp", "leaf")),
        out_specs=(
            P("samp", "leaf"),
            P("samp", "leaf"),
            P("leaf", "samp"),
            P("leaf", "samp"),
            P("leaf", "samp"),
            P("leaf", "samp"),
        ),
        check_vma=False,
    )
```

time: 63.1 us -> 54.9 us (0.87)
  waiting for transfers between devices: 4.9 us -> 1.32 us
  starting transfers between devices: 16.9 us -> 13.4 us
  Pallas kernels: 35 us -> 34 us
    ppermute x4 -> x3, starting transfers between devices: 11.7 us -> 4.09 us  [the longest x1 2.91 us: sample_shift(): lax.ppermute(block, 'samp', [(i, (i + d) % count) for i in range(count)])]
    ppermute x3, starting transfers between devices: 5.2 us -> 9.34 us  [from_partner(): return lax.ppermute(block, axis, route)]
    ppermute x3, waiting for transfers between devices: 4.89 us -> 1 us  [from_partner(): return lax.ppermute(block, axis, route)]
    pallas_call x1, Pallas kernels: 12.7 us -> 11.4 us  [shards(): pl.pallas_call(functools.partial(tree_kernel, 1.0 / math.sqrt(2 ** LEVELS...]
    dynamic_slice x0 -> x1, local copies, waits for them, and re-layouts: none -> 0.99 us  [shards(): lax.dynamic_slice_in_dim(samples, jnp.where(even, 0, far_end), reach, 1)]
    slice x1 -> x0, local copies, waits for them, and re-layouts: 0.99 us -> none  [halo_pieces(): head = samples[:, :reach]]
    pallas_call x3 -> x4, Pallas kernels: 22.3 us -> 22.6 us  [the longest x1 6.78 us: shards(): pl.pallas_call(functools.partial(second_kernel, math.sqrt(row_count)), in...]
    unnamed x5 -> x7, local copies, waits for them, and re-layouts: 3.99 us -> 3.92 us
  transfers between devices with their start and end apart: 7 -> 6, of which waited for: 2 -> 2; matrix products, arithmetic and copies ran while one was open for 1% -> 0% of each run, Pallas kernels for 21% -> 30%
where the time goes in v2:
time: 54.9 us; the launch traced here: 54.6 us
  Pallas kernels  34 us (62%)
  starting transfers between devices  13.4 us (24%)
  local copies, waits for them, and re-layouts  4.93 us (9%)
  waiting for transfers between devices  1.32 us (2%)
  between operations  0.72 us (1%)
    pallas_call x1, Pallas kernels, shards(): pl.pallas_call(functools.partial(tree_kernel, 1.0 / math.sqrt(2 ** LEVELS...  11.4 us
    ppermute x3, starting transfers between devices, from_partner(): return lax.ppermute(block, axis, route)  9.34 us
    pallas_call x1, Pallas kernels, shards(): pl.pallas_call(functools.partial(second_kernel, math.sqrt(row_count)), in...  6.78 us
    pallas_call x1, Pallas kernels, shards(): pl.pallas_call(functools.partial(others_kernel, parts), grid_spec=pltpu.P...  6.38 us
    pallas_call x1, Pallas kernels, shards(): pl.pallas_call(first_kernel, in_specs=[whole()] * 2, out_specs=[whole()]...  5.06 us
    pallas_call x1, Pallas kernels, shards(): pl.pallas_call(own_kernel, grid_spec=pltpu.PrefetchScalarGridSpec(num_sca...  4.42 us
    unnamed x7, local copies, waits for them, and re-layouts  3.92 us
    ppermute x1, starting transfers between devices, sample_shift(): lax.ppermute(block, 'samp', [(i, (i + d) % count) for i in range(count)])  2.91 us
  transfers between devices with their start and end apart: 6, of which 2 were waited for; matrix products, arithmetic and copies ran while one was open for 0% of the time, Pallas kernels for 30%

profile of v2, /device:TPU:0, one launch (start us, length us, event | category | flops | bytes accessed | tf_op | source)
XLA Modules:
  0.0 54.6 jit_solution(9817311840884167101)
XLA Ops:
  0.6 1.0 %constant_dynamic-slice_fusion = (bf16[128,512]{1,0:T(8,128)(2,1)S(1)}, bf16[128,512]{1,0:T(8,128)(2,1)S(1)}) fusion(bf16[128,2048]{1,0:T(8,128)(2,1)} %samples.1, s32[]{:T(128)S(6)} %select_n.18, s32[]{:T(128)S(6)} %select_n.17), kind=kLoop, calls=%fused_computation.3 | loop fusion | bytes 524296 | tf_op jit(solution)/shard_map/dynamic_slice | solution.py:361
  1.6 0.5 collective-permute-start
  2.2 0.7 %collective-permute-start.1 = (bf16[128,512]{1,0:T(8,128)(2,1)S(1)}, bf16[128,512]{1,0:T(8,128)(2,1)S(1)}, u32[]{:S(2)}, u32[]{:S(2)}) collective-permute-start(bf16[128,512]{1,0:T(8,128)(2,1)S(1)} %get-tuple-element.34), channel_id=1, source_target_pairs={{2,4},{4,2},{6,8},{8,6},{10,12},{12,10},{14,16},{16,14},{18,20},{2... | collective-permute-start | bytes 393224 | tf_op jit(solution)/shard_map/ppermute | solution.py:337
  2.8 0.3 collective-permute-done
  3.2 0.0 collective-permute-done.1
  3.2 2.9 %collective-permute-start.2 = (bf16[128,1024]{1,0:T(8,128)(2,1)S(1)}, bf16[128,1024]{1,0:T(8,128)(2,1)S(1)}, u32[]{:S(2)}, u32[]{:S(2)}) collective-permute-start(bf16[128,1024]{1,0:T(8,128)(2,1)S(1)} %constant_dynamic-update-slice_fusion.halo), channel_id=1, source_target_pairs={{0,1},{1,0},{2,3},{3,2},{4,5},{5,4},{6,7},{7,6},{8,9},{9,8},{10,11... | collective-permute-start | bytes 786440 | tf_op jit(solution)/shard_map/ppermute | solution.py:342
  6.1 0.1 pad_add_fusion.place
  6.2 0.0 copy-start
  6.2 2.2 %copy-done = bf16[16,8,128,128]{3,2,1,0:T(8,128)(2,1)S(1)} copy-done((bf16[16,8,128,128]{3,2,1,0:T(8,128)(2,1)S(1)}, bf16[16,8,128,128]{3,2,1,0:T(8,128)(2,1)}, u32[]{:S(2)}) %copy-start) | copy-done | bytes 4194328
  8.4 0.0 copy-start.1
  8.4 1.0 %copy-done.1 = bf16[128,2048]{1,0:T(8,128)(2,1)S(1)} copy-done((bf16[128,2048]{1,0:T(8,128)(2,1)S(1)}, bf16[128,2048]{1,0:T(8,128)(2,1)}, u32[]{:S(2)}) %copy-start.1) | copy-done | bytes 524312
  9.4 0.0 copy-start.2
  9.4 0.7 %copy-done.2 = s32[16,8]{0,1:T(8,128)S(1)} copy-done((s32[16,8]{0,1:T(8,128)S(1)}, s32[16,8]{0,1:T(8,128)}, u32[]{:S(2)}) %copy-start.2) | copy-done | bytes 536
  10.1 4.4 %own.1 = (f32[128,2048]{1,0:T(8,128)}, bf16[128,2048]{1,0:T(8,128)(2,1)S(1)}, bf16[128,2048]{1,0:T(8,128)(2,1)S(1)}) custom-call(s32[2]{0:T(128)S(1)} %pad_add_fusion.place, s32[8,16]{1,0:T(8,128)S(1)} %bitcast.3, bf16[16,8,128,128]{3,2,1,0:T(8,128)(2,1)S(1)} %copy-done, bf16[128,2048]{1,0:T(8,128)(2,1)S(1)} %copy-done.1, ...), custom_call_target="tpu_custom_call" | custom-call | flops 1073741824 | bytes 7340032 | tf_op jit(solution)/shard_map/own/pallas_call | solution.py:372
  14.5 0.0 collective-permute-done.2.refs_0_
  14.5 6.4 %others.1 = (bf16[256,2048]{1,0:T(8,128)(2,1)S(1)}, bf16[256,2048]{1,0:T(8,128)(2,1)S(1)}, f32[264,128]{1,0:T(8,128)S(1)}) custom-call(s32[2]{0:T(128)S(1)} %pad_add_fusion.place, s32[8,16]{1,0:T(8,128)S(1)} %bitcast.4, bf16[16,8,128,128]{3,2,1,0:T(8,128)(2,1)} %blocks.3, bf16[128,1024]{1,0:T(8,128)(2,1)S(1)} %collective-permute-done.2.refs_0_, ...), custom_call_target="tpu_custom_call" | custom-call | tf_op jit(solution)/shard_map/others/pallas_call | solution.py:390
  20.9 5.5 %collective-permute-start.3 = (f32[264,128]{1,0:T(8,128)S(1)}, f32[264,128]{1,0:T(8,128)S(1)}, u32[]{:S(2)}, u32[]{:S(2)}) collective-permute-start(f32[264,128]{1,0:T(8,128)S(1)} %get-tuple-element.23.packed_zero), channel_id=1, source_target_pairs={{0,2},{2,0},{4,6},{6,4},{8,10},{10,8},{12,14},{14,12},{16,18},{18,... | collective-permute-start | bytes 405512 | tf_op jit(solution)/shard_map/ppermute | solution.py:329
  26.4 1.0 %collective-permute-done.3 = f32[264,128]{1,0:T(8,128)S(1)} collective-permute-done((f32[264,128]{1,0:T(8,128)S(1)}, f32[264,128]{1,0:T(8,128)S(1)}, u32[]{:S(2)}, u32[]{:S(2)}) %collective-permute-start.3) | collective-permute-done | bytes 135200 | tf_op jit(solution)/shard_map/ppermute | solution.py:329
  27.4 2.2 %collective-permute-start.4 = (f32[264,128]{1,0:T(8,128)S(1)}, f32[264,128]{1,0:T(8,128)S(1)}, u32[]{:S(2)}, u32[]{:S(2)}) collective-permute-start(f32[264,128]{1,0:T(8,128)S(1)} %add.16.packed_one), channel_id=1, source_target_pairs={{0,4},{4,0},{2,6},{6,2},{8,12},{12,8},{10,14},{14,10},{16,20},{20,... | collective-permute-start | bytes 405512 | tf_op jit(solution)/shard_map/ppermute | solution.py:329
  29.6 5.1 %first.1 = (f32[2,256,256]{2,1,0:T(8,128)S(1)}, f32[2,256,256]{2,1,0:T(8,128)S(1)}) custom-call(f32[264,128]{1,0:T(8,128)S(1)} %get-tuple-element.23.packed_zero, f32[264,128]{1,0:T(8,128)S(1)} %add.16.packed_one), custom_call_target="tpu_custom_call" | custom-call | flops 3000000000 | bytes 1048576 | tf_op jit(solution)/shard_map/first/pallas_call | solution.py:413
  34.7 0.0 collective-permute-done.4
  34.7 1.6 %collective-permute-start.5 = (f32[264,128]{1,0:T(8,128)S(1)}, f32[264,128]{1,0:T(8,128)S(1)}, u32[]{:S(2)}, u32[]{:S(2)}) collective-permute-start(f32[264,128]{1,0:T(8,128)S(1)} %add.17.refs_0_), channel_id=1, source_target_pairs={{0,8},{8,0},{2,10},{10,2},{4,12},{12,4},{6,14},{14,6},{16,24},{24,... | collective-permute-start | bytes 405512 | tf_op jit(solution)/shard_map/ppermute | solution.py:329
  36.4 6.8 %second.1 = (f32[128,2048]{1,0:T(8,128)}, f32[256,128]{1,0:T(8,128)}, f32[128,256]{1,0:T(8,128)S(1)}, f32[2,256,256]{2,1,0:T(8,128)S(1)}, f32[2,256,256]{2,1,0:T(8,128)S(1)}) custom-call(s32[2]{0:T(128)S(1)} %pad_add_fusion.place, f32[2,256,256]{2,1,0:T(8,128)S(1)} %get-tuple-element.24.a_in, ...), custom_call_target="tpu_custom_call", output_to_operand_aliasing={{3}: (1, {}), {4}: (2, {})} | custom-call | flops 3000000000 | bytes 1048576 | tf_op jit(solution)/shard_map/second/pallas_call | solution.py:423
  43.2 0.0 collective-permute-done.5
  43.2 11.4 %tree.1 = (f32[256,128]{1,0:T(8,128)}, f32[256,128]{1,0:T(8,128)}, f32[256,128]{1,0:T(8,128)}) custom-call(s32[2]{0:T(128)S(1)} %pad_add_fusion.place, f32[128,256]{1,0:T(8,128)S(1)} %get-tuple-element.30.upper_own, f32[264,128]{1,0:T(8,128)S(1)} %add.17.refs_0_, f32[264,128]{1,0:T(8,128)S(1)} %add.18.refs_1_), custom_call_target="tpu_custom_call" | custom-call | tf_op jit(solution)/shard_map/tree/pallas_call | solution.py:433
  (5 shorter events, 0.1 us)
Async XLA Ops:
  1.6 1.5 %collective-permute-start = (bf16[128,512]{1,0:T(8,128)(2,1)S(1)}, bf16[128,512]{1,0:T(8,128)(2,1)S(1)}, u32[]{:S(2)}, u32[]{:S(2)}) collective-permute-start(bf16[128,512]{1,0:T(8,128)(2,1)S(1)} %get-tuple-element.35), channel_id=1, source_target_pairs={{0,2},{2,0},{4,6},{6,4},{8,10},{10,8},{12,14},{14,12},{16,18},{18,... | collective-permute-start | bytes 393224 | tf_op jit(solution)/shard_map/ppermute | solution.py:337
  2.2 1.0 %collective-permute-start.1 = (bf16[128,512]{1,0:T(8,128)(2,1)S(1)}, bf16[128,512]{1,0:T(8,128)(2,1)S(1)}, u32[]{:S(2)}, u32[]{:S(2)}) collective-permute-start(bf16[128,512]{1,0:T(8,128)(2,1)S(1)} %get-tuple-element.34), channel_id=1, source_target_pairs={{2,4},{4,2},{6,8},{8,6},{10,12},{12,10},{14,16},{16,14},{18,20},{2... | collective-permute-start | bytes 393224 | tf_op jit(solution)/shard_map/ppermute | solution.py:337
  3.2 11.3 %collective-permute-start.2 = (bf16[128,1024]{1,0:T(8,128)(2,1)S(1)}, bf16[128,1024]{1,0:T(8,128)(2,1)S(1)}, u32[]{:S(2)}, u32[]{:S(2)}) collective-permute-start(bf16[128,1024]{1,0:T(8,128)(2,1)S(1)} %constant_dynamic-update-slice_fusion.halo), channel_id=1, source_target_pairs={{0,1},{1,0},{2,3},{3,2},{4,5},{5,4},{6,7},{7,6},{8,9},{9,8},{10,11... | collective-permute-start | bytes 786440 | tf_op jit(solution)/shard_map/ppermute | solution.py:342
  6.2 2.2 %copy-start = (bf16[16,8,128,128]{3,2,1,0:T(8,128)(2,1)S(1)}, bf16[16,8,128,128]{3,2,1,0:T(8,128)(2,1)}, u32[]{:S(2)}) copy-start(bf16[16,8,128,128]{3,2,1,0:T(8,128)(2,1)} %blocks.3) | copy-start | bytes 12582916
  8.4 1.0 %copy-start.1 = (bf16[128,2048]{1,0:T(8,128)(2,1)S(1)}, bf16[128,2048]{1,0:T(8,128)(2,1)}, u32[]{:S(2)}) copy-start(bf16[128,2048]{1,0:T(8,128)(2,1)} %samples.1) | copy-start | bytes 1572868
  9.4 0.7 %copy-start.2 = (s32[16,8]{0,1:T(8,128)S(1)}, s32[16,8]{0,1:T(8,128)}, u32[]{:S(2)}) copy-start(s32[16,8]{0,1:T(8,128)} %param.4) | copy-start | bytes 1540
  20.9 6.5 %collective-permute-start.3 = (f32[264,128]{1,0:T(8,128)S(1)}, f32[264,128]{1,0:T(8,128)S(1)}, u32[]{:S(2)}, u32[]{:S(2)}) collective-permute-start(f32[264,128]{1,0:T(8,128)S(1)} %get-tuple-element.23.packed_zero), channel_id=1, source_target_pairs={{0,2},{2,0},{4,6},{6,4},{8,10},{10,8},{12,14},{14,12},{16,18},{18,... | collective-permute-start | bytes 405512 | tf_op jit(solution)/shard_map/ppermute | solution.py:329
  27.4 7.3 %collective-permute-start.4 = (f32[264,128]{1,0:T(8,128)S(1)}, f32[264,128]{1,0:T(8,128)S(1)}, u32[]{:S(2)}, u32[]{:S(2)}) collective-permute-start(f32[264,128]{1,0:T(8,128)S(1)} %add.16.packed_one), channel_id=1, source_target_pairs={{0,4},{4,0},{2,6},{6,2},{8,12},{12,8},{10,14},{14,10},{16,20},{20,... | collective-permute-start | bytes 405512 | tf_op jit(solution)/shard_map/ppermute | solution.py:329
  34.7 8.4 %collective-permute-start.5 = (f32[264,128]{1,0:T(8,128)S(1)}, f32[264,128]{1,0:T(8,128)S(1)}, u32[]{:S(2)}, u32[]{:S(2)}) collective-permute-start(f32[264,128]{1,0:T(8,128)S(1)} %add.17.refs_0_), channel_id=1, source_target_pairs={{0,8},{8,0},{2,10},{10,2},{4,12},{12,4},{6,14},{14,6},{16,24},{24,... | collective-permute-start | bytes 405512 | tf_op jit(solution)/shard_map/ppermute | solution.py:329

commit v3 on v2

--- a/solution.py
+++ b/solution.py
@@ -15,6 +15,7 @@
 PANEL = 32
 ROWS_A_STEP = 4
 VMEM_LIMIT = 48 * 1024 * 1024
+VMEM_NEARLY_ALL = 61 * 1024 * 1024
 F32 = jnp.float32
 BF16 = jnp.bfloat16
 NN = (((1,), (0,)), ((), ()))
@@ -59,82 +60,96 @@
     return jnp.where(local < 0, below, jnp.where(local < count, 2 * HB, above))
 
 
-def own_kernel(place, columns, blocks, samples, halo, products, z_high, z_low, near_window, far_window):
-    step = pl.program_id(0)
+def local_column(place, columns, blocks, rr, k):
+    rows_step = blocks.shape[0]
+    steps = pl.num_programs(0)
+    return columns[k, pl.program_id(0) * rows_step + rr] - place[0] * (rows_step * steps)
+
+
+def near_kernel(place, columns, blocks, samples, near, window):
     rows_step, slots, width, _ = blocks.shape
     count = rows_step * pl.num_programs(0)
-    own = samples.shape[0]
+
+    @pl.when(pl.program_id(0) == 0)
+    def _():
+        window[:, : samples.shape[1]] = samples[...]
+        window[:, samples.shape[1] :] = jnp.zeros((samples.shape[0], width), BF16)
+
+    for rr in range(rows_step):
+
+        def chosen(k):
+            local = local_column(place, columns, blocks, rr, k)
+            return jnp.where((local >= 0) & (local < count), local, count)
+
+        lanes = slice(rr * width, (rr + 1) * width)
+        near[:, lanes] = dot(taken(window, chosen, slots, width), block_row(blocks, rr), NT)
+
+
+def fill_window(window, halos):
+    own, reach = halos[0].shape
+    for at in range(0, len(halos), 2):
+        rows = slice(at // 2 * own, (at // 2 + 1) * own)
+        window[rows, :reach] = halos[at][...]
+        window[rows, reach : 2 * reach] = halos[at + 1][...]
+    window[:, 2 * reach :] = jnp.zeros((window.shape[0], window.shape[1] - 2 * reach), BF16)
+
+
+def far_row(place, columns, blocks, window, rr):
+    rows_step, slots, width, _ = blocks.shape
+    count = rows_step * pl.num_programs(0)
     odd = lax.rem(place[0], 2) == 1
+
+    def chosen(k):
+        return far_position(local_column(place, columns, blocks, rr, k), count, odd)
+
+    return dot(taken(window, chosen, slots, width), block_row(blocks, rr), NT)
+
+
+def own_kernel(place, columns, blocks, first, second, near, products, z_high, z_low, gram, window):
+    rows_step, _, width, _ = blocks.shape
+    step = pl.program_id(0)
 
     @pl.when(step == 0)
     def _():
-        near_window[:, : samples.shape[1]] = samples[...]
-        near_window[:, samples.shape[1] :] = jnp.zeros((own, width), BF16)
-        far_window[:, : halo.shape[1]] = halo[...]
-        far_window[:, halo.shape[1] :] = jnp.zeros((own, width), BF16)
+        fill_window(window, (first, second))
+        gram[...] = jnp.zeros_like(gram)
 
     for rr in range(rows_step):
-
-        def local(k):
-            return columns[k, step * rows_step + rr] - place[0] * count
-
-        def near(k):
-            return jnp.where((local(k) >= 0) & (local(k) < count), local(k), count)
-
-        def far(k):
-            return far_position(local(k), count, odd)
-
-        left = jnp.concatenate(
-            [taken(near_window, near, slots, width), taken(far_window, far, slots, width)], axis=0
-        )
-        both = dot(left, block_row(blocks, rr), NT)
+        remote = far_row(place, columns, blocks, window, rr)
         lanes = slice(rr * width, (rr + 1) * width)
-        products[:, lanes] = both[:own] + both[own:]
-        z_high[:, lanes], z_low[:, lanes] = split_two(both[own:])
+        products[:, lanes] = near[:, lanes] + remote
+        z_high[:, lanes], z_low[:, lanes] = split_two(remote)
+    halves = z_high[...], z_low[...]
+    gram[...] += dot_split(halves, halves, NT)
 
 
 def others_kernel(parts, place, columns, blocks, *refs):
-    halos = refs[: parts - 1]
-    own_high, own_low, z_high, z_low, packed, window, gram, cross = refs[parts - 1 :]
+    halos = refs[: 2 * (parts - 1)]
+    own_high, own_low, own_gram, z_high, z_low, packed, window, gram_rows, full = refs[2 * (parts - 1) :]
+    rows_step, _, width, _ = blocks.shape
     step = pl.program_id(0)
-    rows_step, slots, width, _ = blocks.shape
-    count = rows_step * pl.num_programs(0)
     own = own_high.shape[0]
-    odd = lax.rem(place[0], 2) == 1
-    rows = [
-        pl.ds(pl.multiple_of(lax.rem(place[1] + parts - d, parts) * own, own), own) for d in range(parts)
-    ]
 
     @pl.when(step == 0)
     def _():
-        for d in range(1, parts):
-            window[(d - 1) * own : d * own, : 2 * HB * width] = halos[d - 1][...]
-        window[:, 2 * HB * width :] = jnp.zeros((window.shape[0], width), BF16)
-        gram[...] = jnp.zeros_like(gram)
-        cross[...] = jnp.zeros_like(cross)
-
-    z_high[rows[0], :] = own_high[...]
-    z_low[rows[0], :] = own_low[...]
+        fill_window(window, halos)
+        gram_rows[...] = jnp.zeros_like(gram_rows)
+
     for rr in range(rows_step):
-
-        def far(k):
-            return far_position(columns[k, step * rows_step + rr] - place[0] * count, count, odd)
-
-        remote = dot(taken(window, far, slots, width), block_row(blocks, rr), NT)
-        high, low = split_two(remote)
         lanes = slice(rr * width, (rr + 1) * width)
-        for d in range(1, parts):
-            z_high[rows[d], lanes] = high[(d - 1) * own : d * own]
-            z_low[rows[d], lanes] = low[(d - 1) * own : d * own]
-        if rr % 2 == 1:
-            pair = slice((rr - 1) * width, (rr + 1) * width)
-            high, low = z_high[:, pair], z_low[:, pair]
-            gram[...] += dot(high, high, NT)
-            cross[...] += dot(high, low, NT)
+        z_high[:, lanes], z_low[:, lanes] = split_two(far_row(place, columns, blocks, window, rr))
+    high, low = z_high[...], z_low[...]
+    all_high = jnp.concatenate([own_high[...], high], axis=0)
+    all_low = jnp.concatenate([own_low[...], low], axis=0)
+    gram_rows[...] += dot_split((high, low), (all_high, all_low), NT)
 
     @pl.when(step == pl.num_programs(0) - 1)
     def _():
-        pack_symmetric(packed, gram[...] + (cross[...] + cross[...].T))
+        full[:own, :own] = own_gram[...]
+        full[own:, :] = gram_rows[...]
+        full[:own, own:] = gram_rows[:, :own].T
+        shift = place[1] * own
+        pack_symmetric(packed, pltpu.roll(pltpu.roll(full[...], shift, 0), shift, 1))
 
 
 def square_iota(n):
@@ -278,7 +293,7 @@
     factor(a, m, 0, a.shape[1] // 2)
 
 
-def second_kernel(scale, place, a_in, m_in, z_high, z_low, bases, transfer, upper_own, a, m):
+def second_kernel(scale, place, a_in, m_in, own_high, own_low, rest_high, rest_low, bases, transfer, upper_own, a, m):
     del a_in, m_in
     n = a.shape[1]
     factor(a, m, n // 2, n)
@@ -287,10 +302,13 @@
     rows = own_rows(place, own)
     upper_own[...] = a[1, rows, :]
     transfer[...] = dot_split(split_two(m[1]), split_two(a[0, rows, :]), NT)
-    inverse = split_two(m[0, rows, :] * scale)
-    for c in range(0, z_high.shape[1], 512):
+    turned = pltpu.roll(m[0, rows, :] * scale, lax.rem(n - place[1] * own, n), 1)
+    inverse = split_two(turned)
+    for c in range(0, own_high.shape[1], 512):
         lanes = slice(c, c + 512)
-        bases[:, lanes] = dot_split(inverse, (z_high[:, lanes], z_low[:, lanes]), NN)
+        high = jnp.concatenate([own_high[:, lanes], rest_high[:, lanes]], axis=0)
+        low = jnp.concatenate([own_low[:, lanes], rest_low[:, lanes]], axis=0)
+        bases[:, lanes] = dot_split(inverse, (high, low), NN)
 
 
 def tree_kernel(top_scale, place, upper_own, *refs):
@@ -315,8 +333,8 @@
     return pl.BlockSpec(memory_space=pltpu.VMEM)
 
 
-def params():
-    return pltpu.CompilerParams(vmem_limit_bytes=VMEM_LIMIT)
+def params(limit=VMEM_LIMIT):
+    return pltpu.CompilerParams(vmem_limit_bytes=limit)
 
 
 def from_partner(block, axis, bit):
@@ -339,7 +357,7 @@
 
 def sample_shift(block, d):
     count = lax.axis_size("samp")
-    return lax.ppermute(block, "samp", [(i, (i + d) % count) for i in range(count)])
+    return lax.ppermute(block, "samp", [(i, (i - d) % count) for i in range(count)])
 
 
 def shards(stiffness, columns, samples):
@@ -359,51 +377,73 @@
     even = leaf % 2 == 0
     first = lax.dynamic_slice_in_dim(samples, jnp.where(even, far_end, 0), reach, 1)
     second = lax.dynamic_slice_in_dim(samples, jnp.where(even, 0, far_end), reach, 1)
-    halo = jnp.concatenate([swap_across(first, 0), swap_across(second, 1)], axis=1)
-    other_halos = [sample_shift(halo, d) for d in range(1, parts)]
+    halos = [swap_across(first, 0), swap_across(second, 1)]
+    other_halos = [sample_shift(halo, d) for d in range(1, parts) for halo in halos]
 
     block_spec = pl.BlockSpec((ROWS_A_STEP, slots, width, width), lambda i, *_: (i, 0, 0, 0))
     own_spec = pl.BlockSpec((own, step_lanes), lambda i, *_: (0, i))
-    all_spec = pl.BlockSpec((total, step_lanes), lambda i, *_: (0, i))
+    rest = total - own
+    rest_spec = pl.BlockSpec((rest, step_lanes), lambda i, *_: (0, i))
+    product_cost = pl.CostEstimate(
+        flops=2 * own * slots * width * row_count, bytes_accessed=6 * 1024 * 1024, transcendentals=0
+    )
 
     def fixed(*dims):
         return pl.BlockSpec(dims, lambda i, *_: (0,) * len(dims))
 
-    products, own_high, own_low = pl.pallas_call(
+    near = pl.pallas_call(
+        near_kernel,
+        grid_spec=pltpu.PrefetchScalarGridSpec(
+            num_scalar_prefetch=2,
+            grid=(steps,),
+            in_specs=[block_spec, fixed(own, row_count)],
+            out_specs=own_spec,
+            scratch_shapes=[pltpu.VMEM((own, row_count + width), BF16)],
+        ),
+        out_shape=shape((own, row_count), F32),
+        compiler_params=params(VMEM_NEARLY_ALL),
+        cost_estimate=product_cost,
+        name="near",
+    )(place, columns, stiffness, samples)
+
+    products, own_high, own_low, own_gram = pl.pallas_call(
         own_kernel,
         grid_spec=pltpu.PrefetchScalarGridSpec(
             num_scalar_prefetch=2,
             grid=(steps,),
-            in_specs=[block_spec, fixed(own, row_count), fixed(own, 2 * reach)],
-            out_specs=[own_spec] * 3,
-            scratch_shapes=[pltpu.VMEM((own, row_count + width), BF16), pltpu.VMEM((own, 2 * reach + width), BF16)],
+            in_specs=[block_spec] + [fixed(own, reach)] * 2 + [own_spec],
+            out_specs=[own_spec] * 3 + [fixed(own, own)],
+            scratch_shapes=[pltpu.VMEM((own, 2 * reach + width), BF16)],
         ),
-        out_shape=[shape((own, row_count), F32), shape((own, row_count), BF16), shape((own, row_count), BF16)],
+        out_shape=[
+            shape((own, row_count), F32),
+            shape((own, row_count), BF16),
+            shape((own, row_count), BF16),
+            shape((own, own), F32),
+        ],
         compiler_params=params(),
-        cost_estimate=pl.CostEstimate(
-            flops=4 * own * slots * width * row_count, bytes_accessed=7 * 1024 * 1024, transcendentals=0
-        ),
+        cost_estimate=product_cost,
         name="own",
-    )(place, columns, stiffness, samples, halo)
+    )(place, columns, stiffness, *halos, near)
 
     packed_shape = (total + GROUP, total // 2)
-    z_high, z_low, packed = pl.pallas_call(
+    rest_high, rest_low, packed = pl.pallas_call(
         functools.partial(others_kernel, parts),
         grid_spec=pltpu.PrefetchScalarGridSpec(
             num_scalar_prefetch=2,
             grid=(steps,),
-            in_specs=[block_spec] + [fixed(own, 2 * reach)] * (parts - 1) + [own_spec] * 2,
-            out_specs=[all_spec, all_spec, fixed(*packed_shape)],
+            in_specs=[block_spec] + [fixed(own, reach)] * (2 * (parts - 1)) + [own_spec] * 2 + [fixed(own, own)],
+            out_specs=[rest_spec, rest_spec, fixed(*packed_shape)],
             scratch_shapes=[
-                pltpu.VMEM((total - own, 2 * reach + width), BF16),
-                pltpu.VMEM((total, total), F32),
+                pltpu.VMEM((rest, 2 * reach + width), BF16),
+                pltpu.VMEM((rest, total), F32),
                 pltpu.VMEM((total, total), F32),
             ],
         ),
-        out_shape=[shape((total, row_count), BF16), shape((total, row_count), BF16), shape(packed_shape, F32)],
+        out_shape=[shape((rest, row_count), BF16), shape((rest, row_count), BF16), shape(packed_shape, F32)],
         compiler_params=params(),
         name="others",
-    )(place, columns, stiffness, *other_halos, own_high, own_low)
+    )(place, columns, stiffness, *other_halos, own_high, own_low, own_gram)
 
     smem = pl.BlockSpec(memory_space=pltpu.SMEM)
     square = shape((2, total, total), F32)
@@ -422,14 +462,14 @@
     gram_three = gram_two + from_partner(gram_two, "leaf", 2)
     bases, transfer_one, upper_own, _, _ = pl.pallas_call(
         functools.partial(second_kernel, math.sqrt(row_count)),
-        in_specs=[smem] + [whole()] * 4,
+        in_specs=[smem] + [whole()] * 6,
         out_specs=[whole()] * 5,
         out_shape=[shape((own, row_count), F32), transfer_shape, shape((own, total), F32), square, square],
         input_output_aliases={1: 3, 2: 4},
         compiler_params=params(),
         cost_estimate=pl.CostEstimate(flops=3 * 10**9, bytes_accessed=1024 * 1024, transcendentals=0),
         name="second",
-    )(place, a, m, z_high, z_low)
+    )(place, a, m, own_high, own_low, rest_high, rest_low)
     transfer_two, transfer_three, top_factor = pl.pallas_call(
         functools.partial(tree_kernel, 1.0 / math.sqrt(2**LEVELS * row_count)),
         in_specs=[smem] + [whole()] * 3,

time: 54.9 us -> 59.8 us (1.089)
  Pallas kernels: 34 us -> 41 us
  local copies, waits for them, and re-layouts: 4.93 us -> 2.22 us
    pallas_call x0 -> x1, Pallas kernels: none -> 5.85 us  [shards(): pl.pallas_call(near_kernel, grid_spec=pltpu.PrefetchScalarGridSpec(num_sc...]
    unnamed x7 -> x6, local copies, waits for them, and re-layouts: 3.92 us -> 1.23 us
    pallas_call x1, Pallas kernels: 4.42 us -> 5.88 us  [shards(): pl.pallas_call(own_kernel, grid_spec=pltpu.PrefetchScalarGridSpec(num_sca...]
    ppermute x1 -> x2, starting transfers between devices: 2.91 us -> 2.88 us  [sample_shift(): lax.ppermute(block, 'samp', [(i, (i - d) % count) for i in range(count)])]
  transfers between devices with their start and end apart: 6 -> 7, of which waited for: 2 -> 2; matrix products, arithmetic and copies ran while one was open for 0% -> 1% of each run, Pallas kernels for 30% -> 40%
where the time goes in v3:
time: 59.8 us; the launch traced here: 59.3 us
  Pallas kernels  41 us (69%)
  starting transfers between devices  13.4 us (22%)
  local copies, waits for them, and re-layouts  2.22 us (4%)
  waiting for transfers between devices  1.32 us (2%)
  between operations  0.71 us (1%)
  other arithmetic  0.65 us (1%)
    pallas_call x1, Pallas kernels, shards(): pl.pallas_call(functools.partial(tree_kernel, 1.0 / math.sqrt(2 ** LEVELS...  11.4 us
    ppermute x3, starting transfers between devices, from_partner(): return lax.ppermute(block, axis, route)  9.39 us
    pallas_call x1, Pallas kernels, shards(): pl.pallas_call(functools.partial(second_kernel, math.sqrt(row_count)), in...  6.83 us
    pallas_call x1, Pallas kernels, shards(): pl.pallas_call(functools.partial(others_kernel, parts), grid_spec=pltpu.P...  5.95 us
    pallas_call x1, Pallas kernels, shards(): pl.pallas_call(own_kernel, grid_spec=pltpu.PrefetchScalarGridSpec(num_sca...  5.88 us
    pallas_call x1, Pallas kernels, shards(): pl.pallas_call(near_kernel, grid_spec=pltpu.PrefetchScalarGridSpec(num_sc...  5.85 us
    pallas_call x1, Pallas kernels, shards(): pl.pallas_call(first_kernel, in_specs=[whole()] * 2, out_specs=[whole()]...  5.07 us
    ppermute x2, starting transfers between devices, sample_shift(): lax.ppermute(block, 'samp', [(i, (i - d) % count) for i in range(count)])  2.88 us
  transfers between devices with their start and end apart: 7, of which 2 were waited for; matrix products, arithmetic and copies ran while one was open for 1% of the time, Pallas kernels for 40%

profile of v3, /device:TPU:0, one launch (start us, length us, event | category | flops | bytes accessed | tf_op | source)
XLA Modules:
  0.0 59.3 jit_solution(13983050864644349657)
XLA Ops:
  0.6 0.0 copy-start.1
  0.7 1.0 %constant_dynamic-slice_fusion = (bf16[128,512]{1,0:T(8,128)(2,1)S(1)}, bf16[128,512]{1,0:T(8,128)(2,1)S(1)}) fusion(bf16[128,2048]{1,0:T(8,128)(2,1)} %samples.1, s32[]{:T(128)S(6)} %select_n.18, s32[]{:T(128)S(6)} %select_n.17), kind=kLoop, calls=%fused_computation.1 | loop fusion | bytes 524296 | tf_op jit(solution)/shard_map/dynamic_slice | solution.py:379
  1.7 0.5 collective-permute-start
  2.2 0.7 %collective-permute-start.1 = (bf16[128,512]{1,0:T(8,128)(2,1)S(1)}, bf16[128,512]{1,0:T(8,128)(2,1)S(1)}, u32[]{:S(2)}, u32[]{:S(2)}) collective-permute-start(bf16[128,512]{1,0:T(8,128)(2,1)S(1)} %get-tuple-element.36), channel_id=1, source_target_pairs={{2,4},{4,2},{6,8},{8,6},{10,12},{12,10},{14,16},{16,14},{18,20},{2... | collective-permute-start | bytes 393224 | tf_op jit(solution)/shard_map/ppermute | solution.py:355
  2.8 0.3 collective-permute-done.first
  3.2 2.8 %collective-permute-start.2 = (bf16[128,512]{1,0:T(8,128)(2,1)S(1)}, bf16[128,512]{1,0:T(8,128)(2,1)S(1)}, u32[]{:S(2)}, u32[]{:S(2)}) collective-permute-start(bf16[128,512]{1,0:T(8,128)(2,1)S(1)} %collective-permute-done.first), channel_id=1, source_target_pairs={{0,1},{1,0},{2,3},{3,2},{4,5},{5,4},{6,7},{7,6},{8,9},{9,8},{10,11... | collective-permute-start | bytes 393224 | tf_op jit(solution)/shard_map/ppermute | solution.py:360
  6.0 0.0 collective-permute-done.1.second
  6.0 0.0 collective-permute-start.3
  6.0 0.6 pad_add_fusion.place
  6.6 0.0 copy-start.2
  6.6 5.9 %near.1 = f32[128,2048]{1,0:T(8,128)} custom-call(s32[2]{0:T(128)} %pad_add_fusion.place, s32[8,16]{1,0:T(8,128)} %bitcast.3, bf16[16,8,128,128]{3,2,1,0:T(8,128)(2,1)} %blocks.5, bf16[128,2048]{1,0:T(8,128)(2,1)} %samples.1), custom_call_target="tpu_custom_call" | custom-call | flops 536870912 | bytes 6291456 | tf_op jit(solution)/shard_map/near/pallas_call | solution.py:394
  12.5 0.0 copy-done.1
  12.5 0.0 copy-done.2
  12.5 0.0 copy-start
  12.5 1.2 %copy-done = f32[128,2048]{1,0:T(8,128)S(1)} copy-done((f32[128,2048]{1,0:T(8,128)S(1)}, f32[128,2048]{1,0:T(8,128)}, u32[]{:S(2)}) %copy-start) | copy-done | bytes 1048600
  13.7 5.9 %own.1 = (f32[128,2048]{1,0:T(8,128)}, bf16[128,2048]{1,0:T(8,128)(2,1)S(1)}, bf16[128,2048]{1,0:T(8,128)(2,1)S(1)}, f32[128,128]{1,0:T(8,128)S(1)}) custom-call(s32[2]{0:T(128)S(1)} %copy-done.2, s32[8,16]{1,0:T(8,128)S(1)} %bitcast.4, bf16[16,8,128,128]{3,2,1,0:T(8,128)(2,1)} %blocks.5, bf16[128,512]{1,0:T(8,128)(2,1)S(1)} %collective-permute-done.first, ...), custom_call_target="tpu_custom_call" | custom-call | flops 536870912 | bytes 6291456 | tf_op jit(solution)/shard_map/own/pallas_call | solution.py:409
  19.6 0.0 collective-permute-done.2.refs_0_
  19.6 0.0 collective-permute-done.3.refs_1_
  19.6 6.0 %others.1 = (bf16[128,2048]{1,0:T(8,128)(2,1)S(1)}, bf16[128,2048]{1,0:T(8,128)(2,1)S(1)}, f32[264,128]{1,0:T(8,128)S(1)}) custom-call(s32[2]{0:T(128)S(1)} %copy-done.2, s32[8,16]{1,0:T(8,128)S(1)} %bitcast.5, bf16[16,8,128,128]{3,2,1,0:T(8,128)(2,1)} %blocks.5, bf16[128,512]{1,0:T(8,128)(2,1)S(1)} %collective-permute-done.2.refs_0_, ...), custom_call_target="tpu_custom_call" | custom-call | tf_op jit(solution)/shard_map/others/pallas_call | solution.py:430
  25.6 5.5 %collective-permute-start.4 = (f32[264,128]{1,0:T(8,128)S(1)}, f32[264,128]{1,0:T(8,128)S(1)}, u32[]{:S(2)}, u32[]{:S(2)}) collective-permute-start(f32[264,128]{1,0:T(8,128)S(1)} %get-tuple-element.25.packed_zero), channel_id=1, source_target_pairs={{0,2},{2,0},{4,6},{6,4},{8,10},{10,8},{12,14},{14,12},{16,18},{18,... | collective-permute-start | bytes 405512 | tf_op jit(solution)/shard_map/ppermute | solution.py:347
  31.1 1.0 %collective-permute-done.4 = f32[264,128]{1,0:T(8,128)S(1)} collective-permute-done((f32[264,128]{1,0:T(8,128)S(1)}, f32[264,128]{1,0:T(8,128)S(1)}, u32[]{:S(2)}, u32[]{:S(2)}) %collective-permute-start.4) | collective-permute-done | bytes 135200 | tf_op jit(solution)/shard_map/ppermute | solution.py:347
  32.1 2.2 %collective-permute-start.5 = (f32[264,128]{1,0:T(8,128)S(1)}, f32[264,128]{1,0:T(8,128)S(1)}, u32[]{:S(2)}, u32[]{:S(2)}) collective-permute-start(f32[264,128]{1,0:T(8,128)S(1)} %add.16.packed_one), channel_id=1, source_target_pairs={{0,4},{4,0},{2,6},{6,2},{8,12},{12,8},{10,14},{14,10},{16,20},{20,... | collective-permute-start | bytes 405512 | tf_op jit(solution)/shard_map/ppermute | solution.py:347
  34.3 5.1 %first.1 = (f32[2,256,256]{2,1,0:T(8,128)S(1)}, f32[2,256,256]{2,1,0:T(8,128)S(1)}) custom-call(f32[264,128]{1,0:T(8,128)S(1)} %get-tuple-element.25.packed_zero, f32[264,128]{1,0:T(8,128)S(1)} %add.16.packed_one), custom_call_target="tpu_custom_call" | custom-call | flops 3000000000 | bytes 1048576 | tf_op jit(solution)/shard_map/first/pallas_call | solution.py:453
  39.3 0.0 collective-permute-done.5
  39.4 1.7 %collective-permute-start.6 = (f32[264,128]{1,0:T(8,128)S(1)}, f32[264,128]{1,0:T(8,128)S(1)}, u32[]{:S(2)}, u32[]{:S(2)}) collective-permute-start(f32[264,128]{1,0:T(8,128)S(1)} %add.17.refs_0_), channel_id=1, source_target_pairs={{0,8},{8,0},{2,10},{10,2},{4,12},{12,4},{6,14},{14,6},{16,24},{24,... | collective-permute-start | bytes 405512 | tf_op jit(solution)/shard_map/ppermute | solution.py:347
  41.1 6.8 %second.1 = (f32[128,2048]{1,0:T(8,128)}, f32[256,128]{1,0:T(8,128)}, f32[128,256]{1,0:T(8,128)S(1)}, f32[2,256,256]{2,1,0:T(8,128)S(1)}, f32[2,256,256]{2,1,0:T(8,128)S(1)}) custom-call(s32[2]{0:T(128)S(1)} %copy-done.2, f32[2,256,256]{2,1,0:T(8,128)S(1)} %get-tuple-element.26.a_in, ...), custom_call_target="tpu_custom_call", output_to_operand_aliasing={{3}: (1, {}), {4}: (2, {})} | custom-call | flops 3000000000 | bytes 1048576 | tf_op jit(solution)/shard_map/second/pallas_call | solution.py:463
  47.9 0.0 collective-permute-done.6
  47.9 11.4 %tree.1 = (f32[256,128]{1,0:T(8,128)}, f32[256,128]{1,0:T(8,128)}, f32[256,128]{1,0:T(8,128)}) custom-call(s32[2]{0:T(128)S(1)} %copy-done.2, f32[128,256]{1,0:T(8,128)S(1)} %get-tuple-element.32.upper_own, f32[264,128]{1,0:T(8,128)S(1)} %add.17.refs_0_, f32[264,128]{1,0:T(8,128)S(1)} %add.18.refs_1_), custom_call_target="tpu_custom_call" | custom-call | tf_op jit(solution)/shard_map/tree/pallas_call | solution.py:473
  (3 shorter events, 0.1 us)
Async XLA Ops:
  0.6 11.9 %copy-start.1 = (s32[16,8]{0,1:T(8,128)S(1)}, s32[16,8]{0,1:T(8,128)}, u32[]{:S(2)}) copy-start(s32[16,8]{0,1:T(8,128)} %param.4) | copy-start | bytes 1540
  1.7 1.5 %collective-permute-start = (bf16[128,512]{1,0:T(8,128)(2,1)S(1)}, bf16[128,512]{1,0:T(8,128)(2,1)S(1)}, u32[]{:S(2)}, u32[]{:S(2)}) collective-permute-start(bf16[128,512]{1,0:T(8,128)(2,1)S(1)} %get-tuple-element.37), channel_id=1, source_target_pairs={{0,2},{2,0},{4,6},{6,4},{8,10},{10,8},{12,14},{14,12},{16,18},{18,... | collective-permute-start | bytes 393224 | tf_op jit(solution)/shard_map/ppermute | solution.py:355
  2.2 3.8 %collective-permute-start.1 = (bf16[128,512]{1,0:T(8,128)(2,1)S(1)}, bf16[128,512]{1,0:T(8,128)(2,1)S(1)}, u32[]{:S(2)}, u32[]{:S(2)}) collective-permute-start(bf16[128,512]{1,0:T(8,128)(2,1)S(1)} %get-tuple-element.36), channel_id=1, source_target_pairs={{2,4},{4,2},{6,8},{8,6},{10,12},{12,10},{14,16},{16,14},{18,20},{2... | collective-permute-start | bytes 393224 | tf_op jit(solution)/shard_map/ppermute | solution.py:355
  3.2 16.4 %collective-permute-start.2 = (bf16[128,512]{1,0:T(8,128)(2,1)S(1)}, bf16[128,512]{1,0:T(8,128)(2,1)S(1)}, u32[]{:S(2)}, u32[]{:S(2)}) collective-permute-start(bf16[128,512]{1,0:T(8,128)(2,1)S(1)} %collective-permute-done.first), channel_id=1, source_target_pairs={{0,1},{1,0},{2,3},{3,2},{4,5},{5,4},{6,7},{7,6},{8,9},{9,8},{10,11... | collective-permute-start | bytes 393224 | tf_op jit(solution)/shard_map/ppermute | solution.py:360
  6.0 13.6 %collective-permute-start.3 = (bf16[128,512]{1,0:T(8,128)(2,1)S(1)}, bf16[128,512]{1,0:T(8,128)(2,1)S(1)}, u32[]{:S(2)}, u32[]{:S(2)}) collective-permute-start(bf16[128,512]{1,0:T(8,128)(2,1)S(1)} %collective-permute-done.1.second), channel_id=1, source_target_pairs={{0,1},{1,0},{2,3},{3,2},{4,5},{5,4},{6,7},{7,6},{8,9},{9,8},{10,11... | collective-permute-start | bytes 393224 | tf_op jit(solution)/shard_map/ppermute | solution.py:360
  6.6 5.9 %copy-start.2 = (s32[2]{0:T(128)S(1)}, s32[2]{0:T(128)}, u32[]{:S(2)}) copy-start(s32[2]{0:T(128)} %pad_add_fusion.place) | copy-start | bytes 28
  12.5 1.2 %copy-start = (f32[128,2048]{1,0:T(8,128)S(1)}, f32[128,2048]{1,0:T(8,128)}, u32[]{:S(2)}) copy-start(f32[128,2048]{1,0:T(8,128)} %near.1) | copy-start | bytes 3145732
  25.6 6.5 %collective-permute-start.4 = (f32[264,128]{1,0:T(8,128)S(1)}, f32[264,128]{1,0:T(8,128)S(1)}, u32[]{:S(2)}, u32[]{:S(2)}) collective-permute-start(f32[264,128]{1,0:T(8,128)S(1)} %get-tuple-element.25.packed_zero), channel_id=1, source_target_pairs={{0,2},{2,0},{4,6},{6,4},{8,10},{10,8},{12,14},{14,12},{16,18},{18,... | collective-permute-start | bytes 405512 | tf_op jit(solution)/shard_map/ppermute | solution.py:347
  32.1 7.3 %collective-permute-start.5 = (f32[264,128]{1,0:T(8,128)S(1)}, f32[264,128]{1,0:T(8,128)S(1)}, u32[]{:S(2)}, u32[]{:S(2)}) collective-permute-start(f32[264,128]{1,0:T(8,128)S(1)} %add.16.packed_one), channel_id=1, source_target_pairs={{0,4},{4,0},{2,6},{6,2},{8,12},{12,8},{10,14},{14,10},{16,20},{20,... | collective-permute-start | bytes 405512 | tf_op jit(solution)/shard_map/ppermute | solution.py:347
  39.4 8.5 %collective-permute-start.6 = (f32[264,128]{1,0:T(8,128)S(1)}, f32[264,128]{1,0:T(8,128)S(1)}, u32[]{:S(2)}, u32[]{:S(2)}) collective-permute-start(f32[264,128]{1,0:T(8,128)S(1)} %add.17.refs_0_), channel_id=1, source_target_pairs={{0,8},{8,0},{2,10},{10,2},{4,12},{12,4},{6,14},{14,6},{16,24},{24,... | collective-permute-start | bytes 405512 | tf_op jit(solution)/shard_map/ppermute | solution.py:347

commit v4 on v3

--- a/solution.py
+++ b/solution.py
@@ -14,8 +14,8 @@
 GROUP = 8
 PANEL = 32
 ROWS_A_STEP = 4
-VMEM_LIMIT = 48 * 1024 * 1024
-VMEM_NEARLY_ALL = 61 * 1024 * 1024
+VMEM_LIMIT = 20 * 1024 * 1024
+VMEM_NEAR = 48 * 1024 * 1024
 F32 = jnp.float32
 BF16 = jnp.bfloat16
 NN = (((1,), (0,)), ((), ()))
@@ -44,15 +44,6 @@
     return dot(a_high, b_high, dims) + (dot(a_high, b_low, dims) + dot(a_low, b_high, dims))
 
 
-def taken(window, chosen, slots, width):
-    lanes = [pl.ds(pl.multiple_of(chosen(k) * width, LANES), width) for k in range(slots)]
-    return jnp.concatenate([window[:, at] for at in lanes], axis=1)
-
-
-def block_row(blocks, rr):
-    return jnp.concatenate([blocks[rr, k] for k in range(blocks.shape[1])], axis=1)
-
-
 def far_position(local, count, odd):
     lower = jnp.where(odd, 0, HB)
     below = jnp.clip(local + HB, 0, HB - 1) + lower
@@ -60,96 +51,91 @@
     return jnp.where(local < 0, below, jnp.where(local < count, 2 * HB, above))
 
 
-def local_column(place, columns, blocks, rr, k):
-    rows_step = blocks.shape[0]
-    steps = pl.num_programs(0)
-    return columns[k, pl.program_id(0) * rows_step + rr] - place[0] * (rows_step * steps)
-
-
-def near_kernel(place, columns, blocks, samples, near, window):
-    rows_step, slots, width, _ = blocks.shape
-    count = rows_step * pl.num_programs(0)
-
-    @pl.when(pl.program_id(0) == 0)
-    def _():
-        window[:, : samples.shape[1]] = samples[...]
-        window[:, samples.shape[1] :] = jnp.zeros((samples.shape[0], width), BF16)
-
-    for rr in range(rows_step):
-
-        def chosen(k):
-            local = local_column(place, columns, blocks, rr, k)
-            return jnp.where((local >= 0) & (local < count), local, count)
-
-        lanes = slice(rr * width, (rr + 1) * width)
-        near[:, lanes] = dot(taken(window, chosen, slots, width), block_row(blocks, rr), NT)
+def block_rows(place, columns, blocks, window, position, emit, before=None):
+    count, slots, width, _ = blocks.shape
+
+    def body(step, carry):
+        if before is not None:
+            before(step)
+        for rr in range(ROWS_A_STEP):
+            row = step * ROWS_A_STEP + rr
+            picked = []
+            for k in range(slots):
+                at = position(columns[k, row] - place[0] * count) * width
+                picked.append(window[:, pl.ds(pl.multiple_of(at, LANES), width)])
+            stored = jnp.concatenate([blocks[row, k] for k in range(slots)], axis=1)
+            product = dot(jnp.concatenate(picked, axis=1), stored, NT)
+            emit(pl.ds(pl.multiple_of(row * width, LANES), width), product)
+        return carry
+
+    lax.fori_loop(0, count // ROWS_A_STEP, body, 0)
+
+
+def near_kernel(place, columns, blocks_hbm, samples, near, blocks, window, arrived):
+    count, _, width, _ = blocks.shape
+
+    def chunk(step):
+        rows = pl.ds(step * ROWS_A_STEP, ROWS_A_STEP)
+        return pltpu.make_async_copy(blocks_hbm.at[rows], blocks.at[rows], arrived.at[step])
+
+    for step in range(count // ROWS_A_STEP):
+        chunk(step).start()
+    window[:, : samples.shape[1]] = samples[...]
+    window[:, samples.shape[1] :] = jnp.zeros((samples.shape[0], width), BF16)
+
+    def position(local):
+        return jnp.where((local >= 0) & (local < count), local, count)
+
+    def emit(lanes, product):
+        near[:, lanes] = product
+
+    block_rows(place, columns, blocks, window, position, emit, lambda step: chunk(step).wait())
 
 
 def fill_window(window, halos):
-    own, reach = halos[0].shape
-    for at in range(0, len(halos), 2):
-        rows = slice(at // 2 * own, (at // 2 + 1) * own)
-        window[rows, :reach] = halos[at][...]
-        window[rows, reach : 2 * reach] = halos[at + 1][...]
-    window[:, 2 * reach :] = jnp.zeros((window.shape[0], window.shape[1] - 2 * reach), BF16)
-
-
-def far_row(place, columns, blocks, window, rr):
-    rows_step, slots, width, _ = blocks.shape
-    count = rows_step * pl.num_programs(0)
+    own, lanes = halos[0].shape
+    for at, halo in enumerate(halos):
+        window[at * own : (at + 1) * own, :lanes] = halo[...]
+    window[:, lanes:] = jnp.zeros((window.shape[0], window.shape[1] - lanes), BF16)
+
+
+def far_rows(place, columns, blocks, window, emit):
     odd = lax.rem(place[0], 2) == 1
-
-    def chosen(k):
-        return far_position(local_column(place, columns, blocks, rr, k), count, odd)
-
-    return dot(taken(window, chosen, slots, width), block_row(blocks, rr), NT)
-
-
-def own_kernel(place, columns, blocks, first, second, near, products, z_high, z_low, gram, window):
-    rows_step, _, width, _ = blocks.shape
-    step = pl.program_id(0)
-
-    @pl.when(step == 0)
-    def _():
-        fill_window(window, (first, second))
-        gram[...] = jnp.zeros_like(gram)
-
-    for rr in range(rows_step):
-        remote = far_row(place, columns, blocks, window, rr)
-        lanes = slice(rr * width, (rr + 1) * width)
+    count = blocks.shape[0]
+    block_rows(place, columns, blocks, window, lambda local: far_position(local, count, odd), emit)
+
+
+def own_kernel(place, columns, blocks, halo, near, products, z_high, z_low, gram, window):
+    fill_window(window, (halo,))
+
+    def emit(lanes, remote):
         products[:, lanes] = near[:, lanes] + remote
         z_high[:, lanes], z_low[:, lanes] = split_two(remote)
+
+    far_rows(place, columns, blocks, window, emit)
     halves = z_high[...], z_low[...]
-    gram[...] += dot_split(halves, halves, NT)
+    gram[...] = dot_split(halves, halves, NT)
 
 
 def others_kernel(parts, place, columns, blocks, *refs):
-    halos = refs[: 2 * (parts - 1)]
-    own_high, own_low, own_gram, z_high, z_low, packed, window, gram_rows, full = refs[2 * (parts - 1) :]
-    rows_step, _, width, _ = blocks.shape
-    step = pl.program_id(0)
+    halos = refs[: parts - 1]
+    own_high, own_low, own_gram, z_high, z_low, packed, window, full = refs[parts - 1 :]
     own = own_high.shape[0]
-
-    @pl.when(step == 0)
-    def _():
-        fill_window(window, halos)
-        gram_rows[...] = jnp.zeros_like(gram_rows)
-
-    for rr in range(rows_step):
-        lanes = slice(rr * width, (rr + 1) * width)
-        z_high[:, lanes], z_low[:, lanes] = split_two(far_row(place, columns, blocks, window, rr))
+    fill_window(window, halos)
+
+    def emit(lanes, remote):
+        z_high[:, lanes], z_low[:, lanes] = split_two(remote)
+
+    far_rows(place, columns, blocks, window, emit)
     high, low = z_high[...], z_low[...]
     all_high = jnp.concatenate([own_high[...], high], axis=0)
     all_low = jnp.concatenate([own_low[...], low], axis=0)
-    gram_rows[...] += dot_split((high, low), (all_high, all_low), NT)
-
-    @pl.when(step == pl.num_programs(0) - 1)
-    def _():
-        full[:own, :own] = own_gram[...]
-        full[own:, :] = gram_rows[...]
-        full[:own, own:] = gram_rows[:, :own].T
-        shift = place[1] * own
-        pack_symmetric(packed, pltpu.roll(pltpu.roll(full[...], shift, 0), shift, 1))
+    gram_rows = dot_split((high, low), (all_high, all_low), NT)
+    full[:own, :own] = own_gram[...]
+    full[own:, :] = gram_rows
+    full[:own, own:] = gram_rows[:, :own].T
+    shift = place[1] * own
+    pack_symmetric(packed, pltpu.roll(pltpu.roll(full[...], shift, 0), shift, 1))
 
 
 def square_iota(n):
@@ -368,8 +354,6 @@
     reach = HB * width
     leaf = lax.axis_index("leaf")
     place = jnp.stack([leaf, lax.axis_index("samp")]).astype(jnp.int32)
-    steps = blocks_here // ROWS_A_STEP
-    step_lanes = ROWS_A_STEP * width
     shape = jax.ShapeDtypeStruct
     columns = columns.T
 
@@ -377,75 +361,58 @@
     even = leaf % 2 == 0
     first = lax.dynamic_slice_in_dim(samples, jnp.where(even, far_end, 0), reach, 1)
     second = lax.dynamic_slice_in_dim(samples, jnp.where(even, 0, far_end), reach, 1)
-    halos = [swap_across(first, 0), swap_across(second, 1)]
-    other_halos = [sample_shift(halo, d) for d in range(1, parts) for halo in halos]
-
-    block_spec = pl.BlockSpec((ROWS_A_STEP, slots, width, width), lambda i, *_: (i, 0, 0, 0))
-    own_spec = pl.BlockSpec((own, step_lanes), lambda i, *_: (0, i))
+    smem = pl.BlockSpec(memory_space=pltpu.SMEM)
     rest = total - own
-    rest_spec = pl.BlockSpec((rest, step_lanes), lambda i, *_: (0, i))
+    window_lanes = 2 * reach + width
     product_cost = pl.CostEstimate(
         flops=2 * own * slots * width * row_count, bytes_accessed=6 * 1024 * 1024, transcendentals=0
     )
 
-    def fixed(*dims):
-        return pl.BlockSpec(dims, lambda i, *_: (0,) * len(dims))
-
-    near = pl.pallas_call(
+    near, blocks = pl.pallas_call(
         near_kernel,
-        grid_spec=pltpu.PrefetchScalarGridSpec(
-            num_scalar_prefetch=2,
-            grid=(steps,),
-            in_specs=[block_spec, fixed(own, row_count)],
-            out_specs=own_spec,
-            scratch_shapes=[pltpu.VMEM((own, row_count + width), BF16)],
-        ),
-        out_shape=shape((own, row_count), F32),
-        compiler_params=params(VMEM_NEARLY_ALL),
+        in_specs=[smem, smem, pl.BlockSpec(memory_space=pltpu.HBM), whole()],
+        out_specs=[whole()] * 2,
+        out_shape=[shape((own, row_count), F32), shape(stiffness.shape, BF16)],
+        scratch_shapes=[
+            pltpu.VMEM((own, row_count + width), BF16),
+            pltpu.SemaphoreType.DMA((blocks_here // ROWS_A_STEP,)),
+        ],
+        compiler_params=params(VMEM_NEAR),
         cost_estimate=product_cost,
         name="near",
     )(place, columns, stiffness, samples)
 
+    second_halo, near = lax.optimization_barrier((swap_across(second, 1), near))
+    halo = jnp.concatenate([swap_across(first, 0), second_halo], axis=1)
+    other_halos = [sample_shift(halo, d) for d in range(1, parts)]
+
     products, own_high, own_low, own_gram = pl.pallas_call(
         own_kernel,
-        grid_spec=pltpu.PrefetchScalarGridSpec(
-            num_scalar_prefetch=2,
-            grid=(steps,),
-            in_specs=[block_spec] + [fixed(own, reach)] * 2 + [own_spec],
-            out_specs=[own_spec] * 3 + [fixed(own, own)],
-            scratch_shapes=[pltpu.VMEM((own, 2 * reach + width), BF16)],
-        ),
+        in_specs=[smem, smem] + [whole()] * 3,
+        out_specs=[whole()] * 4,
         out_shape=[
             shape((own, row_count), F32),
             shape((own, row_count), BF16),
             shape((own, row_count), BF16),
             shape((own, own), F32),
         ],
+        scratch_shapes=[pltpu.VMEM((own, window_lanes), BF16)],
         compiler_params=params(),
         cost_estimate=product_cost,
         name="own",
-    )(place, columns, stiffness, *halos, near)
+    )(place, columns, blocks, halo, near)
 
     packed_shape = (total + GROUP, total // 2)
     rest_high, rest_low, packed = pl.pallas_call(
         functools.partial(others_kernel, parts),
-        grid_spec=pltpu.PrefetchScalarGridSpec(
-            num_scalar_prefetch=2,
-            grid=(steps,),
-            in_specs=[block_spec] + [fixed(own, reach)] * (2 * (parts - 1)) + [own_spec] * 2 + [fixed(own, own)],
-            out_specs=[rest_spec, rest_spec, fixed(*packed_shape)],
-            scratch_shapes=[
-                pltpu.VMEM((rest, 2 * reach + width), BF16),
-                pltpu.VMEM((rest, total), F32),
-                pltpu.VMEM((total, total), F32),
-            ],
-        ),
+        in_specs=[smem, smem] + [whole()] * (parts + 3),
+        out_specs=[whole()] * 3,
         out_shape=[shape((rest, row_count), BF16), shape((rest, row_count), BF16), shape(packed_shape, F32)],
+        scratch_shapes=[pltpu.VMEM((rest, window_lanes), BF16), pltpu.VMEM((total, total), F32)],
         compiler_params=params(),
         name="others",
-    )(place, columns, stiffness, *other_halos, own_high, own_low, own_gram)
-
-    smem = pl.BlockSpec(memory_space=pltpu.SMEM)
+    )(place, columns, blocks, *other_halos, own_high, own_low, own_gram)
+
     square = shape((2, total, total), F32)
     transfer_shape = shape((total, own), F32)
     gram_one = packed + from_partner(packed, "leaf", 0)

time: 59.8 us -> 52.6 us (0.88)
  Pallas kernels: 41 us -> 34.6 us
  starting transfers between devices: 13.4 us -> 12.1 us
  waiting for transfers between devices: 1.32 us -> 1.94 us
    pallas_call x3, Pallas kernels: 17.7 us -> 11.4 us  [the longest x1 3.92 us: shards(): pl.pallas_call(functools.partial(others_kernel, parts), in_specs=[smem, s...]
    ppermute x3, starting transfers between devices: 9.39 us -> 8.4 us  [from_partner(): return lax.ppermute(block, axis, route)]
    ppermute x2 -> x1, waiting for transfers between devices: 0.01 us -> 0.94 us  [sample_shift(): lax.ppermute(block, 'samp', [(i, (i - d) % count) for i in range(count)])]
    unnamed x6 -> x5, local copies, waits for them, and re-layouts: 1.23 us -> 1.74 us
    ppermute x2 -> x1, starting transfers between devices: 2.88 us -> 2.58 us  [sample_shift(): lax.ppermute(block, 'samp', [(i, (i - d) % count) for i in range(count)])]
  transfers between devices with their start and end apart: 7 -> 6, of which waited for: 2 -> 2; matrix products, arithmetic and copies ran while one was open for 1% -> 0% of each run, Pallas kernels for 40% -> 37%
where the time goes in v4:
time: 52.6 us; the launch traced here: 52.3 us
  Pallas kernels  34.6 us (66%)
  starting transfers between devices  12.1 us (23%)
  local copies, waits for them, and re-layouts  2.74 us (5%)
  waiting for transfers between devices  1.94 us (4%)
  between operations  0.74 us (1%)
    pallas_call x1, Pallas kernels, shards(): pl.pallas_call(functools.partial(tree_kernel, 1.0 / math.sqrt(2 ** LEVELS...  11.4 us
    ppermute x3, starting transfers between devices, from_partner(): return lax.ppermute(block, axis, route)  8.4 us
    pallas_call x1, Pallas kernels, shards(): pl.pallas_call(functools.partial(second_kernel, math.sqrt(row_count)), in...  6.83 us
    pallas_call x1, Pallas kernels, shards(): pl.pallas_call(first_kernel, in_specs=[whole()] * 2, out_specs=[whole()]...  5.06 us
    pallas_call x1, Pallas kernels, shards(): pl.pallas_call(functools.partial(others_kernel, parts), in_specs=[smem, s...  3.92 us
    pallas_call x1, Pallas kernels, shards(): pl.pallas_call(own_kernel, in_specs=[smem, smem] + [whole()] * 3, out_spe...  3.79 us
    pallas_call x1, Pallas kernels, shards(): pl.pallas_call(near_kernel, in_specs=[smem, smem, pl.BlockSpec(memory_spa...  3.65 us
    ppermute x1, starting transfers between devices, sample_shift(): lax.ppermute(block, 'samp', [(i, (i - d) % count) for i in range(count)])  2.58 us
  transfers between devices with their start and end apart: 6, of which 2 were waited for; matrix products, arithmetic and copies ran while one was open for 0% of the time, Pallas kernels for 37%

profile of v4, /device:TPU:0, one launch (start us, length us, event | category | flops | bytes accessed | tf_op | source)
XLA Modules:
  0.0 52.3 jit_solution(16921430029914982709)
XLA Ops:
  0.6 1.0 %constant_dynamic-slice_fusion = (bf16[128,512]{1,0:T(8,128)(2,1)S(1)}, bf16[128,512]{1,0:T(8,128)(2,1)S(1)}) fusion(bf16[128,2048]{1,0:T(8,128)(2,1)} %samples.1, s32[]{:T(128)S(6)} %select_n.18, s32[]{:T(128)S(6)} %select_n.17), kind=kLoop, calls=%fused_computation.3 | loop fusion | bytes 524296 | tf_op jit(solution)/shard_map/dynamic_slice | solution.py:363
  1.6 0.5 collective-permute-start
  2.2 0.7 %collective-permute-start.1 = (bf16[128,512]{1,0:T(8,128)(2,1)S(1)}, bf16[128,512]{1,0:T(8,128)(2,1)S(1)}, u32[]{:S(2)}, u32[]{:S(2)}) collective-permute-start(bf16[128,512]{1,0:T(8,128)(2,1)S(1)} %get-tuple-element.44), channel_id=1, source_target_pairs={{2,4},{4,2},{6,8},{8,6},{10,12},{12,10},{14,16},{16,14},{18,20},{2... | collective-permute-start | bytes 393224 | tf_op jit(solution)/shard_map/ppermute | solution.py:341
  2.8 0.1 pad_add_fusion.place
  2.9 0.0 copy-start
  2.9 1.0 %copy-done = bf16[128,2048]{1,0:T(8,128)(2,1)S(1)} copy-done((bf16[128,2048]{1,0:T(8,128)(2,1)S(1)}, bf16[128,2048]{1,0:T(8,128)(2,1)}, u32[]{:S(2)}) %copy-start) | copy-done | bytes 524312
  4.0 0.0 copy-start.1
  4.0 0.7 %copy-done.1 = s32[16,8]{0,1:T(8,128)S(1)} copy-done((s32[16,8]{0,1:T(8,128)S(1)}, s32[16,8]{0,1:T(8,128)}, u32[]{:S(2)}) %copy-start.1) | copy-done | bytes 536
  4.6 3.6 %near.1 = (f32[128,2048]{1,0:T(8,128)S(1)}, bf16[16,8,128,128]{3,2,1,0:T(8,128)(2,1)S(1)}) custom-call(s32[2]{0:T(128)S(1)} %pad_add_fusion.place, s32[8,16]{1,0:T(8,128)S(1)} %bitcast.3, bf16[16,8,128,128]{3,2,1,0:T(8,128)(2,1)} %blocks_hbm.1, bf16[128,2048]{1,0:T(8,128)(2,1)S(1)} %copy-done), custom_call_target="tpu_custom_call" | custom-call | flops 536870912 | bytes 6291456 | tf_op jit(solution)/shard_map/near/pallas_call | solution.py:371
  8.3 0.0 collective-permute-done.1
  8.3 0.0 collective-permute-done
  8.4 2.6 %collective-permute-start.2 = (bf16[128,1024]{1,0:T(8,128)(2,1)S(1)}, bf16[128,1024]{1,0:T(8,128)(2,1)S(1)}, u32[]{:S(2)}, u32[]{:S(2)}) collective-permute-start(bf16[128,1024]{1,0:T(8,128)(2,1)S(1)} %constant_dynamic-update-slice_fusion.halo), channel_id=1, source_target_pairs={{0,1},{1,0},{2,3},{3,2},{4,5},{5,4},{6,7},{7,6},{8,9},{9,8},{10,11... | collective-permute-start | bytes 786440 | tf_op jit(solution)/shard_map/ppermute | solution.py:346
  10.9 3.8 %own.1 = (f32[128,2048]{1,0:T(8,128)}, bf16[128,2048]{1,0:T(8,128)(2,1)S(1)}, bf16[128,2048]{1,0:T(8,128)(2,1)S(1)}, f32[128,128]{1,0:T(8,128)S(1)}) custom-call(s32[2]{0:T(128)S(1)} %pad_add_fusion.place, s32[8,16]{1,0:T(8,128)S(1)} %bitcast.4, bf16[16,8,128,128]{3,2,1,0:T(8,128)(2,1)S(1)} %get-tuple-element.25.blocks, ...), custom_call_target="tpu_custom_call" | custom-call | flops 536870912 | bytes 6291456 | tf_op jit(solution)/shard_map/own/pallas_call | solution.py:389
  14.7 0.9 %collective-permute-done.2.refs_0_ = bf16[128,1024]{1,0:T(8,128)(2,1)S(1)} collective-permute-done((bf16[128,1024]{1,0:T(8,128)(2,1)S(1)}, bf16[128,1024]{1,0:T(8,128)(2,1)S(1)}, u32[]{:S(2)}, u32[]{:S(2)}) %collective-permute-start.2) | collective-permute-done | bytes 262176 | tf_op jit(solution)/shard_map/ppermute | solution.py:346
  15.7 3.9 %others.1 = (bf16[128,2048]{1,0:T(8,128)(2,1)S(1)}, bf16[128,2048]{1,0:T(8,128)(2,1)S(1)}, f32[264,128]{1,0:T(8,128)S(1)}) custom-call(s32[2]{0:T(128)S(1)} %pad_add_fusion.place, s32[8,16]{1,0:T(8,128)S(1)} %bitcast.5, bf16[16,8,128,128]{3,2,1,0:T(8,128)(2,1)S(1)} %get-tuple-element.25.blocks, bf16[128,1024]{1,0:T(8,128)(2,1)S(1)} %collective-permute-done.2.refs_0_, ...), custom_call_target="tpu_custom_call" | custom-call | tf_op jit(solution)/shard_map/others/pallas_call | solution.py:406
  19.6 2.3 %collective-permute-start.3 = (f32[264,128]{1,0:T(8,128)S(1)}, f32[264,128]{1,0:T(8,128)S(1)}, u32[]{:S(2)}, u32[]{:S(2)}) collective-permute-start(f32[264,128]{1,0:T(8,128)S(1)} %get-tuple-element.33.packed_zero), channel_id=1, source_target_pairs={{0,2},{2,0},{4,6},{6,4},{8,10},{10,8},{12,14},{14,12},{16,18},{18,... | collective-permute-start | bytes 405512 | tf_op jit(solution)/shard_map/ppermute | solution.py:333
  21.9 1.0 %collective-permute-done.3 = f32[264,128]{1,0:T(8,128)S(1)} collective-permute-done((f32[264,128]{1,0:T(8,128)S(1)}, f32[264,128]{1,0:T(8,128)S(1)}, u32[]{:S(2)}, u32[]{:S(2)}) %collective-permute-start.3) | collective-permute-done | bytes 135200 | tf_op jit(solution)/shard_map/ppermute | solution.py:333
  22.9 3.4 %collective-permute-start.4 = (f32[264,128]{1,0:T(8,128)S(1)}, f32[264,128]{1,0:T(8,128)S(1)}, u32[]{:S(2)}, u32[]{:S(2)}) collective-permute-start(f32[264,128]{1,0:T(8,128)S(1)} %add.16.packed_one), channel_id=1, source_target_pairs={{0,4},{4,0},{2,6},{6,2},{8,12},{12,8},{10,14},{14,10},{16,20},{20,... | collective-permute-start | bytes 405512 | tf_op jit(solution)/shard_map/ppermute | solution.py:333
  26.3 5.1 %first.1 = (f32[2,256,256]{2,1,0:T(8,128)S(1)}, f32[2,256,256]{2,1,0:T(8,128)S(1)}) custom-call(f32[264,128]{1,0:T(8,128)S(1)} %get-tuple-element.33.packed_zero, f32[264,128]{1,0:T(8,128)S(1)} %add.16.packed_one), custom_call_target="tpu_custom_call" | custom-call | flops 3000000000 | bytes 1048576 | tf_op jit(solution)/shard_map/first/pallas_call | solution.py:420
  31.4 0.0 collective-permute-done.4
  31.4 2.6 %collective-permute-start.5 = (f32[264,128]{1,0:T(8,128)S(1)}, f32[264,128]{1,0:T(8,128)S(1)}, u32[]{:S(2)}, u32[]{:S(2)}) collective-permute-start(f32[264,128]{1,0:T(8,128)S(1)} %add.17.refs_0_), channel_id=1, source_target_pairs={{0,8},{8,0},{2,10},{10,2},{4,12},{12,4},{6,14},{14,6},{16,24},{24,... | collective-permute-start | bytes 405512 | tf_op jit(solution)/shard_map/ppermute | solution.py:333
  34.1 6.8 %second.1 = (f32[128,2048]{1,0:T(8,128)}, f32[256,128]{1,0:T(8,128)}, f32[128,256]{1,0:T(8,128)S(1)}, f32[2,256,256]{2,1,0:T(8,128)S(1)}, f32[2,256,256]{2,1,0:T(8,128)S(1)}) custom-call(s32[2]{0:T(128)S(1)} %pad_add_fusion.place, f32[2,256,256]{2,1,0:T(8,128)S(1)} %get-tuple-element.34.a_in, ...), custom_call_target="tpu_custom_call", output_to_operand_aliasing={{3}: (1, {}), {4}: (2, {})} | custom-call | flops 3000000000 | bytes 1048576 | tf_op jit(solution)/shard_map/second/pallas_call | solution.py:430
  40.9 0.0 collective-permute-done.5
  40.9 11.4 %tree.1 = (f32[256,128]{1,0:T(8,128)}, f32[256,128]{1,0:T(8,128)}, f32[256,128]{1,0:T(8,128)}) custom-call(s32[2]{0:T(128)S(1)} %pad_add_fusion.place, f32[128,256]{1,0:T(8,128)S(1)} %get-tuple-element.40.upper_own, f32[264,128]{1,0:T(8,128)S(1)} %add.17.refs_0_, f32[264,128]{1,0:T(8,128)S(1)} %add.18.refs_1_), custom_call_target="tpu_custom_call" | custom-call | tf_op jit(solution)/shard_map/tree/pallas_call | solution.py:440
  (5 shorter events, 0.1 us)
Async XLA Ops:
  1.6 6.7 %collective-permute-start = (bf16[128,512]{1,0:T(8,128)(2,1)S(1)}, bf16[128,512]{1,0:T(8,128)(2,1)S(1)}, u32[]{:S(2)}, u32[]{:S(2)}) collective-permute-start(bf16[128,512]{1,0:T(8,128)(2,1)S(1)} %get-tuple-element.45), channel_id=1, source_target_pairs={{0,2},{2,0},{4,6},{6,4},{8,10},{10,8},{12,14},{14,12},{16,18},{18,... | collective-permute-start | bytes 393224 | tf_op jit(solution)/shard_map/ppermute | solution.py:341
  2.2 6.1 %collective-permute-start.1 = (bf16[128,512]{1,0:T(8,128)(2,1)S(1)}, bf16[128,512]{1,0:T(8,128)(2,1)S(1)}, u32[]{:S(2)}, u32[]{:S(2)}) collective-permute-start(bf16[128,512]{1,0:T(8,128)(2,1)S(1)} %get-tuple-element.44), channel_id=1, source_target_pairs={{2,4},{4,2},{6,8},{8,6},{10,12},{12,10},{14,16},{16,14},{18,20},{2... | collective-permute-start | bytes 393224 | tf_op jit(solution)/shard_map/ppermute | solution.py:341
  2.9 1.0 %copy-start = (bf16[128,2048]{1,0:T(8,128)(2,1)S(1)}, bf16[128,2048]{1,0:T(8,128)(2,1)}, u32[]{:S(2)}) copy-start(bf16[128,2048]{1,0:T(8,128)(2,1)} %samples.1) | copy-start | bytes 1572868
  4.0 0.7 %copy-start.1 = (s32[16,8]{0,1:T(8,128)S(1)}, s32[16,8]{0,1:T(8,128)}, u32[]{:S(2)}) copy-start(s32[16,8]{0,1:T(8,128)} %param.4) | copy-start | bytes 1540
  8.4 7.3 %collective-permute-start.2 = (bf16[128,1024]{1,0:T(8,128)(2,1)S(1)}, bf16[128,1024]{1,0:T(8,128)(2,1)S(1)}, u32[]{:S(2)}, u32[]{:S(2)}) collective-permute-start(bf16[128,1024]{1,0:T(8,128)(2,1)S(1)} %constant_dynamic-update-slice_fusion.halo), channel_id=1, source_target_pairs={{0,1},{1,0},{2,3},{3,2},{4,5},{5,4},{6,7},{7,6},{8,9},{9,8},{10,11... | collective-permute-start | bytes 786440 | tf_op jit(solution)/shard_map/ppermute | solution.py:346
  19.6 3.3 %collective-permute-start.3 = (f32[264,128]{1,0:T(8,128)S(1)}, f32[264,128]{1,0:T(8,128)S(1)}, u32[]{:S(2)}, u32[]{:S(2)}) collective-permute-start(f32[264,128]{1,0:T(8,128)S(1)} %get-tuple-element.33.packed_zero), channel_id=1, source_target_pairs={{0,2},{2,0},{4,6},{6,4},{8,10},{10,8},{12,14},{14,12},{16,18},{18,... | collective-permute-start | bytes 405512 | tf_op jit(solution)/shard_map/ppermute | solution.py:333
  22.9 8.5 %collective-permute-start.4 = (f32[264,128]{1,0:T(8,128)S(1)}, f32[264,128]{1,0:T(8,128)S(1)}, u32[]{:S(2)}, u32[]{:S(2)}) collective-permute-start(f32[264,128]{1,0:T(8,128)S(1)} %add.16.packed_one), channel_id=1, source_target_pairs={{0,4},{4,0},{2,6},{6,2},{8,12},{12,8},{10,14},{14,10},{16,20},{20,... | collective-permute-start | bytes 405512 | tf_op jit(solution)/shard_map/ppermute | solution.py:333
  31.4 9.5 %collective-permute-start.5 = (f32[264,128]{1,0:T(8,128)S(1)}, f32[264,128]{1,0:T(8,128)S(1)}, u32[]{:S(2)}, u32[]{:S(2)}) collective-permute-start(f32[264,128]{1,0:T(8,128)S(1)} %add.17.refs_0_), channel_id=1, source_target_pairs={{0,8},{8,0},{2,10},{10,2},{4,12},{12,4},{6,14},{14,6},{16,24},{24,... | collective-permute-start | bytes 405512 | tf_op jit(solution)/shard_map/ppermute | solution.py:333

commit v5 on v4

--- a/solution.py
+++ b/solution.py
@@ -92,50 +92,27 @@
     block_rows(place, columns, blocks, window, position, emit, lambda step: chunk(step).wait())
 
 
-def fill_window(window, halos):
-    own, lanes = halos[0].shape
-    for at, halo in enumerate(halos):
-        window[at * own : (at + 1) * own, :lanes] = halo[...]
-    window[:, lanes:] = jnp.zeros((window.shape[0], window.shape[1] - lanes), BF16)
-
-
-def far_rows(place, columns, blocks, window, emit):
+def far_kernel(place, columns, blocks, first, second, near, products, z_high, z_low, packed, window, total_own, leaving):
+    count, _, width, _ = blocks.shape
+    own = near.shape[0]
+    reach = first.shape[1]
     odd = lax.rem(place[0], 2) == 1
-    count = blocks.shape[0]
+    window[:, :reach] = first[...]
+    window[:, reach : 2 * reach] = second[...]
+    window[:, 2 * reach :] = jnp.zeros((window.shape[0], width), BF16)
+
+    def emit(lanes, remote):
+        total_own[:, lanes] = near[:, lanes] + remote[:own]
+        z_high[:, lanes], z_low[:, lanes] = split_two(remote)
+
     block_rows(place, columns, blocks, window, lambda local: far_position(local, count, odd), emit)
-
-
-def own_kernel(place, columns, blocks, halo, near, products, z_high, z_low, gram, window):
-    fill_window(window, (halo,))
-
-    def emit(lanes, remote):
-        products[:, lanes] = near[:, lanes] + remote
-        z_high[:, lanes], z_low[:, lanes] = split_two(remote)
-
-    far_rows(place, columns, blocks, window, emit)
+    leave = pltpu.make_async_copy(total_own, products, leaving)
+    leave.start()
     halves = z_high[...], z_low[...]
-    gram[...] = dot_split(halves, halves, NT)
-
-
-def others_kernel(parts, place, columns, blocks, *refs):
-    halos = refs[: parts - 1]
-    own_high, own_low, own_gram, z_high, z_low, packed, window, full = refs[parts - 1 :]
-    own = own_high.shape[0]
-    fill_window(window, halos)
-
-    def emit(lanes, remote):
-        z_high[:, lanes], z_low[:, lanes] = split_two(remote)
-
-    far_rows(place, columns, blocks, window, emit)
-    high, low = z_high[...], z_low[...]
-    all_high = jnp.concatenate([own_high[...], high], axis=0)
-    all_low = jnp.concatenate([own_low[...], low], axis=0)
-    gram_rows = dot_split((high, low), (all_high, all_low), NT)
-    full[:own, :own] = own_gram[...]
-    full[own:, :] = gram_rows
-    full[:own, own:] = gram_rows[:, :own].T
+    gram = dot_split(halves, halves, NT)
     shift = place[1] * own
-    pack_symmetric(packed, pltpu.roll(pltpu.roll(full[...], shift, 0), shift, 1))
+    pack_symmetric(packed, pltpu.roll(pltpu.roll(gram, shift, 0), shift, 1))
+    leave.wait()
 
 
 def square_iota(n):
@@ -279,7 +256,7 @@
     factor(a, m, 0, a.shape[1] // 2)
 
 
-def second_kernel(scale, place, a_in, m_in, own_high, own_low, rest_high, rest_low, bases, transfer, upper_own, a, m):
+def second_kernel(scale, place, a_in, m_in, z_high, z_low, bases, transfer, upper_own, a, m):
     del a_in, m_in
     n = a.shape[1]
     factor(a, m, n // 2, n)
@@ -290,11 +267,9 @@
     transfer[...] = dot_split(split_two(m[1]), split_two(a[0, rows, :]), NT)
     turned = pltpu.roll(m[0, rows, :] * scale, lax.rem(n - place[1] * own, n), 1)
     inverse = split_two(turned)
-    for c in range(0, own_high.shape[1], 512):
+    for c in range(0, z_high.shape[1], 512):
         lanes = slice(c, c + 512)
-        high = jnp.concatenate([own_high[:, lanes], rest_high[:, lanes]], axis=0)
-        low = jnp.concatenate([own_low[:, lanes], rest_low[:, lanes]], axis=0)
-        bases[:, lanes] = dot_split(inverse, (high, low), NN)
+        bases[:, lanes] = dot_split(inverse, (z_high[:, lanes], z_low[:, lanes]), NN)
 
 
 def tree_kernel(top_scale, place, upper_own, *refs):
@@ -341,9 +316,12 @@
     return lax.ppermute(block, "leaf", route)
 
 
-def sample_shift(block, d):
+def with_other_parts(block):
     count = lax.axis_size("samp")
-    return lax.ppermute(block, "samp", [(i, (i - d) % count) for i in range(count)])
+    rows = [block]
+    for d in range(1, count):
+        rows.append(lax.ppermute(block, "samp", [(i, (i - d) % count) for i in range(count)]))
+    return jnp.concatenate(rows, axis=0)
 
 
 def shards(stiffness, columns, samples):
@@ -362,12 +340,13 @@
     first = lax.dynamic_slice_in_dim(samples, jnp.where(even, far_end, 0), reach, 1)
     second = lax.dynamic_slice_in_dim(samples, jnp.where(even, 0, far_end), reach, 1)
     smem = pl.BlockSpec(memory_space=pltpu.SMEM)
-    rest = total - own
-    window_lanes = 2 * reach + width
     product_cost = pl.CostEstimate(
         flops=2 * own * slots * width * row_count, bytes_accessed=6 * 1024 * 1024, transcendentals=0
     )
 
+    second_all = with_other_parts(second)
+    first_all = with_other_parts(first)
+    second_all, place = lax.optimization_barrier((second_all, place))
     near, blocks = pl.pallas_call(
         near_kernel,
         in_specs=[smem, smem, pl.BlockSpec(memory_space=pltpu.HBM), whole()],
@@ -382,36 +361,29 @@
         name="near",
     )(place, columns, stiffness, samples)
 
-    second_halo, near = lax.optimization_barrier((swap_across(second, 1), near))
-    halo = jnp.concatenate([swap_across(first, 0), second_halo], axis=1)
-    other_halos = [sample_shift(halo, d) for d in range(1, parts)]
-
-    products, own_high, own_low, own_gram = pl.pallas_call(
-        own_kernel,
-        in_specs=[smem, smem] + [whole()] * 3,
-        out_specs=[whole()] * 4,
+    second_all = swap_across(second_all, 1)
+    first_all, near = lax.optimization_barrier((first_all, near))
+    first_all = swap_across(first_all, 0)
+
+    packed_shape = (total + GROUP, total // 2)
+    products, z_high, z_low, packed = pl.pallas_call(
+        far_kernel,
+        in_specs=[smem, smem] + [whole()] * 4,
+        out_specs=[pl.BlockSpec(memory_space=pltpu.HBM)] + [whole()] * 3,
         out_shape=[
             shape((own, row_count), F32),
-            shape((own, row_count), BF16),
-            shape((own, row_count), BF16),
-            shape((own, own), F32),
+            shape((total, row_count), BF16),
+            shape((total, row_count), BF16),
+            shape(packed_shape, F32),
         ],
-        scratch_shapes=[pltpu.VMEM((own, window_lanes), BF16)],
+        scratch_shapes=[
+            pltpu.VMEM((total, 2 * reach + width), BF16),
+            pltpu.VMEM((own, row_count), F32),
+            pltpu.SemaphoreType.DMA,
+        ],
         compiler_params=params(),
-        cost_estimate=product_cost,
-        name="own",
-    )(place, columns, blocks, halo, near)
-
-    packed_shape = (total + GROUP, total // 2)
-    rest_high, rest_low, packed = pl.pallas_call(
-        functools.partial(others_kernel, parts),
-        in_specs=[smem, smem] + [whole()] * (parts + 3),
-        out_specs=[whole()] * 3,
-        out_shape=[shape((rest, row_count), BF16), shape((rest, row_count), BF16), shape(packed_shape, F32)],
-        scratch_shapes=[pltpu.VMEM((rest, window_lanes), BF16), pltpu.VMEM((total, total), F32)],
-        compiler_params=params(),
-        name="others",
-    )(place, columns, blocks, *other_halos, own_high, own_low, own_gram)
+        name="far",
+    )(place, columns, blocks, first_all, second_all, near)
 
     square = shape((2, total, total), F32)
     transfer_shape = shape((total, own), F32)
@@ -429,14 +401,14 @@
     gram_three = gram_two + from_partner(gram_two, "leaf", 2)
     bases, transfer_one, upper_own, _, _ = pl.pallas_call(
         functools.partial(second_kernel, math.sqrt(row_count)),
-        in_specs=[smem] + [whole()] * 6,
+        in_specs=[smem] + [whole()] * 4,
         out_specs=[whole()] * 5,
         out_shape=[shape((own, row_count), F32), transfer_shape, shape((own, total), F32), square, square],
         input_output_aliases={1: 3, 2: 4},
         compiler_params=params(),
         cost_estimate=pl.CostEstimate(flops=3 * 10**9, bytes_accessed=1024 * 1024, transcendentals=0),
         name="second",
-    )(place, a, m, own_high, own_low, rest_high, rest_low)
+    )(place, a, m, z_high, z_low)
     transfer_two, transfer_three, top_factor = pl.pallas_call(
         functools.partial(tree_kernel, 1.0 / math.sqrt(2**LEVELS * row_count)),
         in_specs=[smem] + [whole()] * 3,

time: 52.6 us -> 53.2 us (1.011)
  waiting for transfers between devices: 1.94 us -> 6.33 us
  Pallas kernels: 34.6 us -> 31.8 us
  starting transfers between devices: 12.1 us -> 11.2 us
    ppermute x3, starting transfers between devices: 8.4 us -> 3.96 us  [from_partner(): return lax.ppermute(block, axis, route)]
    ppermute x1 -> x2, waiting for transfers between devices: 0.94 us -> 4.17 us  [with_other_parts(): lax.ppermute(block, 'samp', [(i, (i - d) % count) for i in range(count)])]
    ppermute x2, starting transfers between devices: 1.17 us -> 4.18 us  [swap_across(): return lax.ppermute(block, 'leaf', route)]
    pallas_call x2 -> x1, Pallas kernels: 7.7 us -> 4.89 us  [shards(): pl.pallas_call(far_kernel, in_specs=[smem, smem] + [whole()] * 4, out_spe...]
    ppermute x2, waiting for transfers between devices: 0.01 us -> 1.16 us  [swap_across(): return lax.ppermute(block, 'leaf', route)]
    ppermute x1 -> x2, starting transfers between devices: 2.58 us -> 3.08 us  [with_other_parts(): lax.ppermute(block, 'samp', [(i, (i - d) % count) for i in range(count)])]
    unnamed x5 -> x4, local copies, waits for them, and re-layouts: 1.74 us -> 1.72 us
  transfers between devices with their start and end apart: 6 -> 7, of which waited for: 2 -> 3; matrix products, arithmetic and copies ran while one was open for 0% -> 0% of each run, Pallas kernels for 37% -> 29%
where the time goes in v5:
time: 53.2 us; the launch traced here: 53 us
  Pallas kernels  31.8 us (60%)
  starting transfers between devices  11.2 us (21%)
  waiting for transfers between devices  6.33 us (12%)
  local copies, waits for them, and re-layouts  2.72 us (5%)
  between operations  0.73 us (1%)
    pallas_call x1, Pallas kernels, shards(): pl.pallas_call(functools.partial(tree_kernel, 1.0 / math.sqrt(2 ** LEVELS...  11.4 us
    pallas_call x1, Pallas kernels, shards(): pl.pallas_call(functools.partial(second_kernel, math.sqrt(row_count)), in...  6.82 us
    pallas_call x1, Pallas kernels, shards(): pl.pallas_call(first_kernel, in_specs=[whole()] * 2, out_specs=[whole()]...  5.07 us
    pallas_call x1, Pallas kernels, shards(): pl.pallas_call(far_kernel, in_specs=[smem, smem] + [whole()] * 4, out_spe...  4.89 us
    ppermute x2, starting transfers between devices, swap_across(): return lax.ppermute(block, 'leaf', route)  4.18 us
    ppermute x2, waiting for transfers between devices, with_other_parts(): lax.ppermute(block, 'samp', [(i, (i - d) % count) for i in range(count)])  4.17 us
    ppermute x3, starting transfers between devices, from_partner(): return lax.ppermute(block, axis, route)  3.96 us
    pallas_call x1, Pallas kernels, shards(): pl.pallas_call(near_kernel, in_specs=[smem, smem, pl.BlockSpec(memory_spa...  3.66 us
  transfers between devices with their start and end apart: 7, of which 3 were waited for; matrix products, arithmetic and copies ran while one was open for 0% of the time, Pallas kernels for 29%

profile of v5, /device:TPU:0, one launch (start us, length us, event | category | flops | bytes accessed | tf_op | source)
XLA Modules:
  0.0 53.0 jit_solution(2585944957929145050)
XLA Ops:
  0.6 1.0 %constant_dynamic-slice_fusion = (bf16[128,512]{1,0:T(8,128)(2,1)S(1)}, bf16[128,512]{1,0:T(8,128)(2,1)S(1)}) fusion(bf16[128,2048]{1,0:T(8,128)(2,1)} %samples.1, s32[]{:T(128)S(6)} %select_n.18, s32[]{:T(128)S(6)} %select_n.17), kind=kLoop, calls=%fused_computation.3 | loop fusion | bytes 524296 | tf_op jit(solution)/shard_map/dynamic_slice | solution.py:340
  1.6 3.0 %collective-permute-start = (bf16[128,512]{1,0:T(8,128)(2,1)S(1)}, bf16[128,512]{1,0:T(8,128)(2,1)S(1)}, u32[]{:S(2)}, u32[]{:S(2)}) collective-permute-start(bf16[128,512]{1,0:T(8,128)(2,1)S(1)} %get-tuple-element.43), channel_id=1, source_target_pairs={{0,1},{1,0},{2,3},{3,2},{4,5},{5,4},{6,7},{7,6},{8,9},{9,8},{10,11... | collective-permute-start | bytes 393224 | tf_op jit(solution)/shard_map/ppermute | solution.py:323
  4.6 0.1 collective-permute-start.1
  4.7 0.1 pad_add_fusion.place
  4.8 4.2 %collective-permute-done = bf16[128,512]{1,0:T(8,128)(2,1)S(1)} collective-permute-done((bf16[128,512]{1,0:T(8,128)(2,1)S(1)}, bf16[128,512]{1,0:T(8,128)(2,1)S(1)}, u32[]{:S(2)}, u32[]{:S(2)}) %collective-permute-start) | collective-permute-done | bytes 131104 | tf_op jit(solution)/shard_map/ppermute | solution.py:323
  9.0 0.7 %collective-permute-start.3 = (bf16[256,512]{1,0:T(8,128)(2,1)S(1)}, bf16[256,512]{1,0:T(8,128)(2,1)S(1)}, u32[]{:S(2)}, u32[]{:S(2)}) collective-permute-start(bf16[256,512]{1,0:T(8,128)(2,1)S(1)} %pad_maximum_fusion), channel_id=1, source_target_pairs={{2,4},{4,2},{6,8},{8,6},{10,12},{12,10},{14,16},{16,14},{18,20},{2... | collective-permute-start | bytes 786440 | tf_op jit(solution)/shard_map/ppermute | solution.py:316
  9.7 0.0 copy-start
  9.7 1.0 %copy-done = bf16[128,2048]{1,0:T(8,128)(2,1)S(1)} copy-done((bf16[128,2048]{1,0:T(8,128)(2,1)S(1)}, bf16[128,2048]{1,0:T(8,128)(2,1)}, u32[]{:S(2)}) %copy-start) | copy-done | bytes 524312
  10.7 0.0 copy-start.1
  10.7 0.7 %copy-done.1 = s32[16,8]{0,1:T(8,128)S(1)} copy-done((s32[16,8]{0,1:T(8,128)S(1)}, s32[16,8]{0,1:T(8,128)}, u32[]{:S(2)}) %copy-start.1) | copy-done | bytes 536
  11.4 3.7 %near.1 = (f32[128,2048]{1,0:T(8,128)S(1)}, bf16[16,8,128,128]{3,2,1,0:T(8,128)(2,1)S(1)}) custom-call(s32[2]{0:T(128)S(1)} %pad_add_fusion.place, s32[8,16]{1,0:T(8,128)S(1)} %bitcast.3, bf16[16,8,128,128]{3,2,1,0:T(8,128)(2,1)} %blocks_hbm.1, bf16[128,2048]{1,0:T(8,128)(2,1)S(1)} %copy-done), custom_call_target="tpu_custom_call" | custom-call | flops 536870912 | bytes 6291456 | tf_op jit(solution)/shard_map/near/pallas_call | solution.py:350
  15.1 0.0 collective-permute-done.1
  15.1 3.5 %collective-permute-start.2 = (bf16[256,512]{1,0:T(8,128)(2,1)S(1)}, bf16[256,512]{1,0:T(8,128)(2,1)S(1)}, u32[]{:S(2)}, u32[]{:S(2)}) collective-permute-start(bf16[256,512]{1,0:T(8,128)(2,1)S(1)} %pad_maximum_fusion.1), channel_id=1, source_target_pairs={{0,2},{2,0},{4,6},{6,4},{8,10},{10,8},{12,14},{14,12},{16,18},{18,... | collective-permute-start | bytes 786440 | tf_op jit(solution)/shard_map/ppermute | solution.py:316
  18.6 0.0 collective-permute-done.3.second
  18.6 1.2 %collective-permute-done.2.first = bf16[256,512]{1,0:T(8,128)(2,1)S(1)} collective-permute-done((bf16[256,512]{1,0:T(8,128)(2,1)S(1)}, bf16[256,512]{1,0:T(8,128)(2,1)S(1)}, u32[]{:S(2)}, u32[]{:S(2)}) %collective-permute-start.2) | collective-permute-done | bytes 262176 | tf_op jit(solution)/shard_map/ppermute | solution.py:316
  19.8 4.9 %far.1 = (f32[128,2048]{1,0:T(8,128)}, bf16[256,2048]{1,0:T(8,128)(2,1)S(1)}, bf16[256,2048]{1,0:T(8,128)(2,1)S(1)}, f32[264,128]{1,0:T(8,128)S(1)}) custom-call(s32[2]{0:T(128)S(1)} %pad_add_fusion.place, s32[8,16]{1,0:T(8,128)S(1)} %bitcast.4, bf16[16,8,128,128]{3,2,1,0:T(8,128)(2,1)S(1)} %get-tuple-element.25.blocks, ...), custom_call_target="tpu_custom_call" | custom-call | tf_op jit(solution)/shard_map/far/pallas_call | solution.py:369
  24.7 0.4 collective-permute-start.4
  25.1 1.0 %collective-permute-done.4 = f32[264,128]{1,0:T(8,128)S(1)} collective-permute-done((f32[264,128]{1,0:T(8,128)S(1)}, f32[264,128]{1,0:T(8,128)S(1)}, u32[]{:S(2)}, u32[]{:S(2)}) %collective-permute-start.4) | collective-permute-done | bytes 135200 | tf_op jit(solution)/shard_map/ppermute | solution.py:308
  26.1 1.9 %collective-permute-start.5 = (f32[264,128]{1,0:T(8,128)S(1)}, f32[264,128]{1,0:T(8,128)S(1)}, u32[]{:S(2)}, u32[]{:S(2)}) collective-permute-start(f32[264,128]{1,0:T(8,128)S(1)} %add.16.packed_one), channel_id=1, source_target_pairs={{0,4},{4,0},{2,6},{6,2},{8,12},{12,8},{10,14},{14,10},{16,20},{20,... | collective-permute-start | bytes 405512 | tf_op jit(solution)/shard_map/ppermute | solution.py:308
  28.0 5.1 %first.1 = (f32[2,256,256]{2,1,0:T(8,128)S(1)}, f32[2,256,256]{2,1,0:T(8,128)S(1)}) custom-call(f32[264,128]{1,0:T(8,128)S(1)} %get-tuple-element.31.packed_zero, f32[264,128]{1,0:T(8,128)S(1)} %add.16.packed_one), custom_call_target="tpu_custom_call" | custom-call | flops 3000000000 | bytes 1048576 | tf_op jit(solution)/shard_map/first/pallas_call | solution.py:392
  33.1 0.0 collective-permute-done.5
  33.1 1.6 %collective-permute-start.6 = (f32[264,128]{1,0:T(8,128)S(1)}, f32[264,128]{1,0:T(8,128)S(1)}, u32[]{:S(2)}, u32[]{:S(2)}) collective-permute-start(f32[264,128]{1,0:T(8,128)S(1)} %add.17.refs_0_), channel_id=1, source_target_pairs={{0,8},{8,0},{2,10},{10,2},{4,12},{12,4},{6,14},{14,6},{16,24},{24,... | collective-permute-start | bytes 405512 | tf_op jit(solution)/shard_map/ppermute | solution.py:308
  34.7 6.8 %second.1 = (f32[128,2048]{1,0:T(8,128)}, f32[256,128]{1,0:T(8,128)}, f32[128,256]{1,0:T(8,128)S(1)}, f32[2,256,256]{2,1,0:T(8,128)S(1)}, f32[2,256,256]{2,1,0:T(8,128)S(1)}) custom-call(s32[2]{0:T(128)S(1)} %pad_add_fusion.place, f32[2,256,256]{2,1,0:T(8,128)S(1)} %get-tuple-element.32.a_in, ...), custom_call_target="tpu_custom_call", output_to_operand_aliasing={{3}: (1, {}), {4}: (2, {})} | custom-call | flops 3000000000 | bytes 1048576 | tf_op jit(solution)/shard_map/second/pallas_call | solution.py:402
  41.6 0.0 collective-permute-done.6
  41.6 11.4 %tree.1 = (f32[256,128]{1,0:T(8,128)}, f32[256,128]{1,0:T(8,128)}, f32[256,128]{1,0:T(8,128)}) custom-call(s32[2]{0:T(128)S(1)} %pad_add_fusion.place, f32[128,256]{1,0:T(8,128)S(1)} %get-tuple-element.38.upper_own, f32[264,128]{1,0:T(8,128)S(1)} %add.17.refs_0_, f32[264,128]{1,0:T(8,128)S(1)} %add.18.refs_1_), custom_call_target="tpu_custom_call" | custom-call | tf_op jit(solution)/shard_map/tree/pallas_call | solution.py:412
  (5 shorter events, 0.1 us)
Async XLA Ops:
  1.6 7.3 %collective-permute-start = (bf16[128,512]{1,0:T(8,128)(2,1)S(1)}, bf16[128,512]{1,0:T(8,128)(2,1)S(1)}, u32[]{:S(2)}, u32[]{:S(2)}) collective-permute-start(bf16[128,512]{1,0:T(8,128)(2,1)S(1)} %get-tuple-element.43), channel_id=1, source_target_pairs={{0,1},{1,0},{2,3},{3,2},{4,5},{5,4},{6,7},{7,6},{8,9},{9,8},{10,11... | collective-permute-start | bytes 393224 | tf_op jit(solution)/shard_map/ppermute | solution.py:323
  4.6 10.4 %collective-permute-start.1 = (bf16[128,512]{1,0:T(8,128)(2,1)S(1)}, bf16[128,512]{1,0:T(8,128)(2,1)S(1)}, u32[]{:S(2)}, u32[]{:S(2)}) collective-permute-start(bf16[128,512]{1,0:T(8,128)(2,1)S(1)} %get-tuple-element.42), channel_id=1, source_target_pairs={{0,1},{1,0},{2,3},{3,2},{4,5},{5,4},{6,7},{7,6},{8,9},{9,8},{10,11... | collective-permute-start | bytes 393224 | tf_op jit(solution)/shard_map/ppermute | solution.py:323
  9.0 9.6 %collective-permute-start.3 = (bf16[256,512]{1,0:T(8,128)(2,1)S(1)}, bf16[256,512]{1,0:T(8,128)(2,1)S(1)}, u32[]{:S(2)}, u32[]{:S(2)}) collective-permute-start(bf16[256,512]{1,0:T(8,128)(2,1)S(1)} %pad_maximum_fusion), channel_id=1, source_target_pairs={{2,4},{4,2},{6,8},{8,6},{10,12},{12,10},{14,16},{16,14},{18,20},{2... | collective-permute-start | bytes 786440 | tf_op jit(solution)/shard_map/ppermute | solution.py:316
  9.7 1.0 %copy-start = (bf16[128,2048]{1,0:T(8,128)(2,1)S(1)}, bf16[128,2048]{1,0:T(8,128)(2,1)}, u32[]{:S(2)}) copy-start(bf16[128,2048]{1,0:T(8,128)(2,1)} %samples.1) | copy-start | bytes 1572868
  10.7 0.7 %copy-start.1 = (s32[16,8]{0,1:T(8,128)S(1)}, s32[16,8]{0,1:T(8,128)}, u32[]{:S(2)}) copy-start(s32[16,8]{0,1:T(8,128)} %param.4) | copy-start | bytes 1540
  15.1 4.7 %collective-permute-start.2 = (bf16[256,512]{1,0:T(8,128)(2,1)S(1)}, bf16[256,512]{1,0:T(8,128)(2,1)S(1)}, u32[]{:S(2)}, u32[]{:S(2)}) collective-permute-start(bf16[256,512]{1,0:T(8,128)(2,1)S(1)} %pad_maximum_fusion.1), channel_id=1, source_target_pairs={{0,2},{2,0},{4,6},{6,4},{8,10},{10,8},{12,14},{14,12},{16,18},{18,... | collective-permute-start | bytes 786440 | tf_op jit(solution)/shard_map/ppermute | solution.py:316
  24.7 1.4 %collective-permute-start.4 = (f32[264,128]{1,0:T(8,128)S(1)}, f32[264,128]{1,0:T(8,128)S(1)}, u32[]{:S(2)}, u32[]{:S(2)}) collective-permute-start(f32[264,128]{1,0:T(8,128)S(1)} %get-tuple-element.31.packed_zero), channel_id=1, source_target_pairs={{0,2},{2,0},{4,6},{6,4},{8,10},{10,8},{12,14},{14,12},{16,18},{18,... | collective-permute-start | bytes 405512 | tf_op jit(solution)/shard_map/ppermute | solution.py:308
  26.1 6.9 %collective-permute-start.5 = (f32[264,128]{1,0:T(8,128)S(1)}, f32[264,128]{1,0:T(8,128)S(1)}, u32[]{:S(2)}, u32[]{:S(2)}) collective-permute-start(f32[264,128]{1,0:T(8,128)S(1)} %add.16.packed_one), channel_id=1, source_target_pairs={{0,4},{4,0},{2,6},{6,2},{8,12},{12,8},{10,14},{14,10},{16,20},{20,... | collective-permute-start | bytes 405512 | tf_op jit(solution)/shard_map/ppermute | solution.py:308
  33.1 8.5 %collective-permute-start.6 = (f32[264,128]{1,0:T(8,128)S(1)}, f32[264,128]{1,0:T(8,128)S(1)}, u32[]{:S(2)}, u32[]{:S(2)}) collective-permute-start(f32[264,128]{1,0:T(8,128)S(1)} %add.17.refs_0_), channel_id=1, source_target_pairs={{0,8},{8,0},{2,10},{10,2},{4,12},{12,4},{6,14},{14,6},{16,24},{24,... | collective-permute-start | bytes 405512 | tf_op jit(solution)/shard_map/ppermute | solution.py:308

commit v6 on v4

--- a/solution.py
+++ b/solution.py
@@ -51,7 +51,7 @@
     return jnp.where(local < 0, below, jnp.where(local < count, 2 * HB, above))
 
 
-def block_rows(place, columns, blocks, window, position, emit, before=None):
+def block_rows(place, columns, blocks, windows, emit, before=None):
     count, slots, width, _ = blocks.shape
 
     def body(step, carry):
@@ -59,20 +59,53 @@
             before(step)
         for rr in range(ROWS_A_STEP):
             row = step * ROWS_A_STEP + rr
+            local = [columns[k, row] - place[0] * count for k in range(slots)]
             picked = []
-            for k in range(slots):
-                at = position(columns[k, row] - place[0] * count) * width
-                picked.append(window[:, pl.ds(pl.multiple_of(at, LANES), width)])
+            for window, position in windows:
+                ats = [pl.multiple_of(position(at) * width, LANES) for at in local]
+                picked.append(jnp.concatenate([window[:, pl.ds(at, width)] for at in ats], axis=1))
             stored = jnp.concatenate([blocks[row, k] for k in range(slots)], axis=1)
-            product = dot(jnp.concatenate(picked, axis=1), stored, NT)
+            product = dot(jnp.concatenate(picked, axis=0), stored, NT)
             emit(pl.ds(pl.multiple_of(row * width, LANES), width), product)
         return carry
 
     lax.fori_loop(0, count // ROWS_A_STEP, body, 0)
 
 
-def near_kernel(place, columns, blocks_hbm, samples, near, blocks, window, arrived):
+def prepare_kernel(at, samples, copied, first, second, arrived):
+    reach = first.shape[1]
+    copies = [
+        pltpu.make_async_copy(samples.at[:, pl.ds(pl.multiple_of(at[0], LANES), reach)], first, arrived.at[0]),
+        pltpu.make_async_copy(samples.at[:, pl.ds(pl.multiple_of(at[1], LANES), reach)], second, arrived.at[1]),
+        pltpu.make_async_copy(samples, copied, arrived.at[2]),
+    ]
+    for copy in copies:
+        copy.start()
+    for copy in copies:
+        copy.wait()
+
+
+def fill_window(window, halos):
+    own, reach = halos[0].shape
+    for at in range(0, len(halos), 2):
+        rows = slice(at // 2 * own, (at // 2 + 1) * own)
+        window[rows, :reach] = halos[at][...]
+        window[rows, reach : 2 * reach] = halos[at + 1][...]
+    window[:, 2 * reach :] = jnp.zeros((window.shape[0], window.shape[1] - 2 * reach), BF16)
+
+
+def far_pick(place, blocks, window):
+    odd = lax.rem(place[0], 2) == 1
+    count = blocks.shape[0]
+    return window, lambda local: far_position(local, count, odd)
+
+
+def own_kernel(
+    place, columns, blocks_hbm, samples, first, second,
+    products, blocks, z_high, z_low, gram, near_window, far_window, sums, arrived, leaving,
+):
     count, _, width, _ = blocks.shape
+    own = samples.shape[0]
 
     def chunk(step):
         rows = pl.ds(step * ROWS_A_STEP, ROWS_A_STEP)
@@ -80,53 +113,37 @@
 
     for step in range(count // ROWS_A_STEP):
         chunk(step).start()
-    window[:, : samples.shape[1]] = samples[...]
-    window[:, samples.shape[1] :] = jnp.zeros((samples.shape[0], width), BF16)
-
-    def position(local):
+    near_window[:, : samples.shape[1]] = samples[...]
+    near_window[:, samples.shape[1] :] = jnp.zeros((own, width), BF16)
+    fill_window(far_window, (first, second))
+
+    def near_position(local):
         return jnp.where((local >= 0) & (local < count), local, count)
 
-    def emit(lanes, product):
-        near[:, lanes] = product
-
-    block_rows(place, columns, blocks, window, position, emit, lambda step: chunk(step).wait())
-
-
-def fill_window(window, halos):
-    own, lanes = halos[0].shape
-    for at, halo in enumerate(halos):
-        window[at * own : (at + 1) * own, :lanes] = halo[...]
-    window[:, lanes:] = jnp.zeros((window.shape[0], window.shape[1] - lanes), BF16)
-
-
-def far_rows(place, columns, blocks, window, emit):
-    odd = lax.rem(place[0], 2) == 1
-    count = blocks.shape[0]
-    block_rows(place, columns, blocks, window, lambda local: far_position(local, count, odd), emit)
-
-
-def own_kernel(place, columns, blocks, halo, near, products, z_high, z_low, gram, window):
-    fill_window(window, (halo,))
-
-    def emit(lanes, remote):
-        products[:, lanes] = near[:, lanes] + remote
+    def emit(lanes, both):
+        remote = both[own:]
+        sums[:, lanes] = both[:own] + remote
         z_high[:, lanes], z_low[:, lanes] = split_two(remote)
 
-    far_rows(place, columns, blocks, window, emit)
+    windows = [(near_window, near_position), far_pick(place, blocks, far_window)]
+    block_rows(place, columns, blocks, windows, emit, lambda step: chunk(step).wait())
+    leave = pltpu.make_async_copy(sums, products, leaving)
+    leave.start()
     halves = z_high[...], z_low[...]
     gram[...] = dot_split(halves, halves, NT)
+    leave.wait()
 
 
 def others_kernel(parts, place, columns, blocks, *refs):
-    halos = refs[: parts - 1]
-    own_high, own_low, own_gram, z_high, z_low, packed, window, full = refs[parts - 1 :]
+    halos = refs[: 2 * (parts - 1)]
+    own_high, own_low, own_gram, z_high, z_low, packed, window, full = refs[2 * (parts - 1) :]
     own = own_high.shape[0]
     fill_window(window, halos)
 
     def emit(lanes, remote):
         z_high[:, lanes], z_low[:, lanes] = split_two(remote)
 
-    far_rows(place, columns, blocks, window, emit)
+    block_rows(place, columns, blocks, [far_pick(place, blocks, window)], emit)
     high, low = z_high[...], z_low[...]
     all_high = jnp.concatenate([own_high[...], high], axis=0)
     all_low = jnp.concatenate([own_low[...], low], axis=0)
@@ -357,55 +374,55 @@
     shape = jax.ShapeDtypeStruct
     columns = columns.T
 
-    far_end = row_count - reach
-    even = leaf % 2 == 0
-    first = lax.dynamic_slice_in_dim(samples, jnp.where(even, far_end, 0), reach, 1)
-    second = lax.dynamic_slice_in_dim(samples, jnp.where(even, 0, far_end), reach, 1)
     smem = pl.BlockSpec(memory_space=pltpu.SMEM)
+    hbm = pl.BlockSpec(memory_space=pltpu.HBM)
     rest = total - own
     window_lanes = 2 * reach + width
-    product_cost = pl.CostEstimate(
-        flops=2 * own * slots * width * row_count, bytes_accessed=6 * 1024 * 1024, transcendentals=0
-    )
-
-    near, blocks = pl.pallas_call(
-        near_kernel,
-        in_specs=[smem, smem, pl.BlockSpec(memory_space=pltpu.HBM), whole()],
-        out_specs=[whole()] * 2,
-        out_shape=[shape((own, row_count), F32), shape(stiffness.shape, BF16)],
-        scratch_shapes=[
-            pltpu.VMEM((own, row_count + width), BF16),
-            pltpu.SemaphoreType.DMA((blocks_here // ROWS_A_STEP,)),
-        ],
+    far_end = row_count - reach
+    odd = lax.rem(leaf, 2)
+    reach_shape = shape((own, reach), BF16)
+    samples, first, second = pl.pallas_call(
+        prepare_kernel,
+        in_specs=[smem, hbm],
+        out_specs=[whole()] * 3,
+        out_shape=[shape(samples.shape, BF16), reach_shape, reach_shape],
+        scratch_shapes=[pltpu.SemaphoreType.DMA((3,))],
         compiler_params=params(VMEM_NEAR),
-        cost_estimate=product_cost,
-        name="near",
-    )(place, columns, stiffness, samples)
-
-    second_halo, near = lax.optimization_barrier((swap_across(second, 1), near))
-    halo = jnp.concatenate([swap_across(first, 0), second_halo], axis=1)
-    other_halos = [sample_shift(halo, d) for d in range(1, parts)]
-
-    products, own_high, own_low, own_gram = pl.pallas_call(
+        name="prepare",
+    )(jnp.stack([far_end * (1 - odd), far_end * odd]).astype(jnp.int32), samples)
+
+    halos = [swap_across(first, 0), swap_across(second, 1)]
+    other_halos = [sample_shift(halo, d) for d in range(1, parts) for halo in halos]
+
+    products, blocks, own_high, own_low, own_gram = pl.pallas_call(
         own_kernel,
-        in_specs=[smem, smem] + [whole()] * 3,
-        out_specs=[whole()] * 4,
+        in_specs=[smem, smem, hbm] + [whole()] * 3,
+        out_specs=[hbm] + [whole()] * 4,
         out_shape=[
             shape((own, row_count), F32),
+            shape(stiffness.shape, BF16),
             shape((own, row_count), BF16),
             shape((own, row_count), BF16),
             shape((own, own), F32),
         ],
-        scratch_shapes=[pltpu.VMEM((own, window_lanes), BF16)],
-        compiler_params=params(),
-        cost_estimate=product_cost,
+        scratch_shapes=[
+            pltpu.VMEM((own, row_count + width), BF16),
+            pltpu.VMEM((own, window_lanes), BF16),
+            pltpu.VMEM((own, row_count), F32),
+            pltpu.SemaphoreType.DMA((blocks_here // ROWS_A_STEP,)),
+            pltpu.SemaphoreType.DMA,
+        ],
+        compiler_params=params(VMEM_NEAR),
+        cost_estimate=pl.CostEstimate(
+            flops=4 * own * slots * width * row_count, bytes_accessed=6 * 1024 * 1024, transcendentals=0
+        ),
         name="own",
-    )(place, columns, blocks, halo, near)
+    )(place, columns, stiffness, samples, *halos)
 
     packed_shape = (total + GROUP, total // 2)
     rest_high, rest_low, packed = pl.pallas_call(
         functools.partial(others_kernel, parts),
-        in_specs=[smem, smem] + [whole()] * (parts + 3),
+        in_specs=[smem, smem] + [whole()] * (2 * parts + 2),
         out_specs=[whole()] * 3,
         out_shape=[shape((rest, row_count), BF16), shape((rest, row_count), BF16), shape(packed_shape, F32)],
         scratch_shapes=[pltpu.VMEM((rest, window_lanes), BF16), pltpu.VMEM((total, total), F32)],

time: 52.6 us -> 51.5 us (0.979)
  starting transfers between devices: 12.1 us -> 13.4 us
  local copies, waits for them, and re-layouts: 2.74 us -> 1.73 us
  Pallas kernels: 34.6 us -> 33.9 us
  waiting for transfers between devices: 1.94 us -> 1.32 us
    dynamic_slice x1 -> x0, local copies, waits for them, and re-layouts: 0.99 us -> none  [shards(): lax.dynamic_slice_in_dim(samples, jnp.where(even, 0, far_end), reach, 1)]
    ppermute x3, starting transfers between devices: 8.4 us -> 9.36 us  [from_partner(): return lax.ppermute(block, axis, route)]
    ppermute x1 -> x2, waiting for transfers between devices: 0.94 us -> 0.01 us  [sample_shift(): lax.ppermute(block, 'samp', [(i, (i - d) % count) for i in range(count)])]
    pallas_call x2, Pallas kernels: 7.44 us -> 6.71 us  [the longest x1 6.06 us: shards(): pl.pallas_call(own_kernel, in_specs=[smem, smem, hbm] + [whole()] * 3, ou...]
    ppermute x1 -> x2, starting transfers between devices: 2.58 us -> 2.88 us  [sample_shift(): lax.ppermute(block, 'samp', [(i, (i - d) % count) for i in range(count)])]
    unnamed x5 -> x4, local copies, waits for them, and re-layouts: 1.74 us -> 1.73 us
  transfers between devices with their start and end apart: 6 -> 7, of which waited for: 2 -> 2; matrix products, arithmetic and copies ran while one was open for 0% -> 0% of each run, Pallas kernels for 37% -> 35%
where the time goes in v6:
time: 51.5 us; the launch traced here: 51.3 us
  Pallas kernels  33.9 us (66%)
  starting transfers between devices  13.4 us (26%)
  local copies, waits for them, and re-layouts  1.73 us (3%)
  waiting for transfers between devices  1.32 us (3%)
  between operations  0.72 us (1%)
    pallas_call x1, Pallas kernels, shards(): pl.pallas_call(functools.partial(tree_kernel, 1.0 / math.sqrt(2 ** LEVELS...  11.4 us
    ppermute x3, starting transfers between devices, from_partner(): return lax.ppermute(block, axis, route)  9.36 us
    pallas_call x1, Pallas kernels, shards(): pl.pallas_call(functools.partial(second_kernel, math.sqrt(row_count)), in...  6.83 us
    pallas_call x1, Pallas kernels, shards(): pl.pallas_call(own_kernel, in_specs=[smem, smem, hbm] + [whole()] * 3, ou...  6.06 us
    pallas_call x1, Pallas kernels, shards(): pl.pallas_call(first_kernel, in_specs=[whole()] * 2, out_specs=[whole()]...  5.06 us
    pallas_call x1, Pallas kernels, shards(): pl.pallas_call(functools.partial(others_kernel, parts), in_specs=[smem, s...  3.92 us
    ppermute x2, starting transfers between devices, sample_shift(): lax.ppermute(block, 'samp', [(i, (i - d) % count) for i in range(count)])  2.88 us
    unnamed x4, local copies, waits for them, and re-layouts  1.73 us
  transfers between devices with their start and end apart: 7, of which 2 were waited for; matrix products, arithmetic and copies ran while one was open for 0% of the time, Pallas kernels for 35%

profile of v6, /device:TPU:0, one launch (start us, length us, event | category | flops | bytes accessed | tf_op | source)
XLA Modules:
  0.0 51.3 jit_solution(1016560213633951767)
XLA Ops:
  0.6 0.1 pad_add_fusion.1.at
  0.7 0.0 copy-start
  0.7 1.0 %copy-done = bf16[128,2048]{1,0:T(8,128)(2,1)S(1)} copy-done((bf16[128,2048]{1,0:T(8,128)(2,1)S(1)}, bf16[128,2048]{1,0:T(8,128)(2,1)}, u32[]{:S(2)}) %copy-start) | copy-done | bytes 524312
  1.8 0.7 %prepare.1 = (bf16[128,2048]{1,0:T(8,128)(2,1)S(1)}, bf16[128,512]{1,0:T(8,128)(2,1)S(1)}, bf16[128,512]{1,0:T(8,128)(2,1)S(1)}) custom-call(s32[2]{0:T(128)S(1)} %pad_add_fusion.1.at, bf16[128,2048]{1,0:T(8,128)(2,1)S(1)} %copy-done), custom_call_target="tpu_custom_call" | custom-call | tf_op jit(solution)/shard_map/prepare/pallas_call | solution.py:384
  2.4 0.5 %collective-permute-start = (bf16[128,512]{1,0:T(8,128)(2,1)S(1)}, bf16[128,512]{1,0:T(8,128)(2,1)S(1)}, u32[]{:S(2)}, u32[]{:S(2)}) collective-permute-start(bf16[128,512]{1,0:T(8,128)(2,1)S(1)} %get-tuple-element.26), channel_id=1, source_target_pairs={{0,2},{2,0},{4,6},{6,4},{8,10},{10,8},{12,14},{14,12},{16,18},{18,... | collective-permute-start | bytes 393224 | tf_op jit(solution)/shard_map/ppermute | solution.py:358
  2.9 0.7 %collective-permute-start.1 = (bf16[128,512]{1,0:T(8,128)(2,1)S(1)}, bf16[128,512]{1,0:T(8,128)(2,1)S(1)}, u32[]{:S(2)}, u32[]{:S(2)}) collective-permute-start(bf16[128,512]{1,0:T(8,128)(2,1)S(1)} %get-tuple-element.27), channel_id=1, source_target_pairs={{2,4},{4,2},{6,8},{8,6},{10,12},{12,10},{14,16},{16,14},{18,20},{2... | collective-permute-start | bytes 393224 | tf_op jit(solution)/shard_map/ppermute | solution.py:358
  3.6 0.3 collective-permute-done.first
  3.9 2.8 %collective-permute-start.2 = (bf16[128,512]{1,0:T(8,128)(2,1)S(1)}, bf16[128,512]{1,0:T(8,128)(2,1)S(1)}, u32[]{:S(2)}, u32[]{:S(2)}) collective-permute-start(bf16[128,512]{1,0:T(8,128)(2,1)S(1)} %collective-permute-done.first), channel_id=1, source_target_pairs={{0,1},{1,0},{2,3},{3,2},{4,5},{5,4},{6,7},{7,6},{8,9},{9,8},{10,11... | collective-permute-start | bytes 393224 | tf_op jit(solution)/shard_map/ppermute | solution.py:363
  6.8 0.0 collective-permute-done.1.second
  6.8 0.0 collective-permute-start.3
  6.8 0.1 pad_add_fusion.place
  6.9 0.0 copy-start.1
  6.9 0.7 %copy-done.1 = s32[16,8]{0,1:T(8,128)S(1)} copy-done((s32[16,8]{0,1:T(8,128)S(1)}, s32[16,8]{0,1:T(8,128)}, u32[]{:S(2)}) %copy-start.1) | copy-done | bytes 536
  7.6 6.1 %own.1 = (f32[128,2048]{1,0:T(8,128)}, bf16[16,8,128,128]{3,2,1,0:T(8,128)(2,1)S(1)}, bf16[128,2048]{1,0:T(8,128)(2,1)S(1)}, bf16[128,2048]{1,0:T(8,128)(2,1)S(1)}, f32[128,128]{1,0:T(8,128)S(1)}) custom-call(s32[2]{0:T(128)S(1)} %pad_add_fusion.place, s32[8,16]{1,0:T(8,128)S(1)} %bitcast.5, bf16[16,8,128,128]{3,2,1,0:T(8,128)(2,1)} %blocks_hbm.1, ...), custom_call_target="tpu_custom_call" | custom-call | flops 1073741824 | bytes 6291456 | tf_op jit(solution)/shard_map/own/pallas_call | solution.py:397
  13.6 0.0 collective-permute-done.2.refs_0_
  13.6 0.0 collective-permute-done.3.refs_1_
  13.7 3.9 %others.1 = (bf16[128,2048]{1,0:T(8,128)(2,1)S(1)}, bf16[128,2048]{1,0:T(8,128)(2,1)S(1)}, f32[264,128]{1,0:T(8,128)S(1)}) custom-call(s32[2]{0:T(128)S(1)} %pad_add_fusion.place, s32[8,16]{1,0:T(8,128)S(1)} %bitcast.6, bf16[16,8,128,128]{3,2,1,0:T(8,128)(2,1)S(1)} %get-tuple-element.29.blocks, bf16[128,512]{1,0:T(8,128)(2,1)S(1)} %collective-permute-done.2.refs_0_, ...), custom_call_target="tpu_custom_call" | custom-call | tf_op jit(solution)/shard_map/others/pallas_call | solution.py:423
  17.6 5.5 %collective-permute-start.4 = (f32[264,128]{1,0:T(8,128)S(1)}, f32[264,128]{1,0:T(8,128)S(1)}, u32[]{:S(2)}, u32[]{:S(2)}) collective-permute-start(f32[264,128]{1,0:T(8,128)S(1)} %get-tuple-element.33.packed_zero), channel_id=1, source_target_pairs={{0,2},{2,0},{4,6},{6,4},{8,10},{10,8},{12,14},{14,12},{16,18},{18,... | collective-permute-start | bytes 405512 | tf_op jit(solution)/shard_map/ppermute | solution.py:350
  23.1 1.0 %collective-permute-done.4 = f32[264,128]{1,0:T(8,128)S(1)} collective-permute-done((f32[264,128]{1,0:T(8,128)S(1)}, f32[264,128]{1,0:T(8,128)S(1)}, u32[]{:S(2)}, u32[]{:S(2)}) %collective-permute-start.4) | collective-permute-done | bytes 135200 | tf_op jit(solution)/shard_map/ppermute | solution.py:350
  24.1 2.2 %collective-permute-start.5 = (f32[264,128]{1,0:T(8,128)S(1)}, f32[264,128]{1,0:T(8,128)S(1)}, u32[]{:S(2)}, u32[]{:S(2)}) collective-permute-start(f32[264,128]{1,0:T(8,128)S(1)} %add.9.packed_one), channel_id=1, source_target_pairs={{0,4},{4,0},{2,6},{6,2},{8,12},{12,8},{10,14},{14,10},{16,20},{20,... | collective-permute-start | bytes 405512 | tf_op jit(solution)/shard_map/ppermute | solution.py:350
  26.3 5.1 %first.1 = (f32[2,256,256]{2,1,0:T(8,128)S(1)}, f32[2,256,256]{2,1,0:T(8,128)S(1)}) custom-call(f32[264,128]{1,0:T(8,128)S(1)} %get-tuple-element.33.packed_zero, f32[264,128]{1,0:T(8,128)S(1)} %add.9.packed_one), custom_call_target="tpu_custom_call" | custom-call | flops 3000000000 | bytes 1048576 | tf_op jit(solution)/shard_map/first/pallas_call | solution.py:437
  31.3 0.0 collective-permute-done.5
  31.4 1.7 %collective-permute-start.6 = (f32[264,128]{1,0:T(8,128)S(1)}, f32[264,128]{1,0:T(8,128)S(1)}, u32[]{:S(2)}, u32[]{:S(2)}) collective-permute-start(f32[264,128]{1,0:T(8,128)S(1)} %add.10.refs_0_), channel_id=1, source_target_pairs={{0,8},{8,0},{2,10},{10,2},{4,12},{12,4},{6,14},{14,6},{16,24},{24,... | collective-permute-start | bytes 405512 | tf_op jit(solution)/shard_map/ppermute | solution.py:350
  33.1 6.8 %second.1 = (f32[128,2048]{1,0:T(8,128)}, f32[256,128]{1,0:T(8,128)}, f32[128,256]{1,0:T(8,128)S(1)}, f32[2,256,256]{2,1,0:T(8,128)S(1)}, f32[2,256,256]{2,1,0:T(8,128)S(1)}) custom-call(s32[2]{0:T(128)S(1)} %pad_add_fusion.place, f32[2,256,256]{2,1,0:T(8,128)S(1)} %get-tuple-element.34.a_in, ...), custom_call_target="tpu_custom_call", output_to_operand_aliasing={{3}: (1, {}), {4}: (2, {})} | custom-call | flops 3000000000 | bytes 1048576 | tf_op jit(solution)/shard_map/second/pallas_call | solution.py:447
  39.9 0.0 collective-permute-done.6
  39.9 11.4 %tree.1 = (f32[256,128]{1,0:T(8,128)}, f32[256,128]{1,0:T(8,128)}, f32[256,128]{1,0:T(8,128)}) custom-call(s32[2]{0:T(128)S(1)} %pad_add_fusion.place, f32[128,256]{1,0:T(8,128)S(1)} %get-tuple-element.40.upper_own, f32[264,128]{1,0:T(8,128)S(1)} %add.10.refs_0_, f32[264,128]{1,0:T(8,128)S(1)} %add.11.refs_1_), custom_call_target="tpu_custom_call" | custom-call | tf_op jit(solution)/shard_map/tree/pallas_call | solution.py:457
  (3 shorter events, 0.1 us)
Async XLA Ops:
  0.7 1.0 %copy-start = (bf16[128,2048]{1,0:T(8,128)(2,1)S(1)}, bf16[128,2048]{1,0:T(8,128)(2,1)}, u32[]{:S(2)}) copy-start(bf16[128,2048]{1,0:T(8,128)(2,1)} %samples.1) | copy-start | bytes 1572868
  2.4 1.5 %collective-permute-start = (bf16[128,512]{1,0:T(8,128)(2,1)S(1)}, bf16[128,512]{1,0:T(8,128)(2,1)S(1)}, u32[]{:S(2)}, u32[]{:S(2)}) collective-permute-start(bf16[128,512]{1,0:T(8,128)(2,1)S(1)} %get-tuple-element.26), channel_id=1, source_target_pairs={{0,2},{2,0},{4,6},{6,4},{8,10},{10,8},{12,14},{14,12},{16,18},{18,... | collective-permute-start | bytes 393224 | tf_op jit(solution)/shard_map/ppermute | solution.py:358
  2.9 3.8 %collective-permute-start.1 = (bf16[128,512]{1,0:T(8,128)(2,1)S(1)}, bf16[128,512]{1,0:T(8,128)(2,1)S(1)}, u32[]{:S(2)}, u32[]{:S(2)}) collective-permute-start(bf16[128,512]{1,0:T(8,128)(2,1)S(1)} %get-tuple-element.27), channel_id=1, source_target_pairs={{2,4},{4,2},{6,8},{8,6},{10,12},{12,10},{14,16},{16,14},{18,20},{2... | collective-permute-start | bytes 393224 | tf_op jit(solution)/shard_map/ppermute | solution.py:358
  3.9 9.7 %collective-permute-start.2 = (bf16[128,512]{1,0:T(8,128)(2,1)S(1)}, bf16[128,512]{1,0:T(8,128)(2,1)S(1)}, u32[]{:S(2)}, u32[]{:S(2)}) collective-permute-start(bf16[128,512]{1,0:T(8,128)(2,1)S(1)} %collective-permute-done.first), channel_id=1, source_target_pairs={{0,1},{1,0},{2,3},{3,2},{4,5},{5,4},{6,7},{7,6},{8,9},{9,8},{10,11... | collective-permute-start | bytes 393224 | tf_op jit(solution)/shard_map/ppermute | solution.py:363
  6.8 6.9 %collective-permute-start.3 = (bf16[128,512]{1,0:T(8,128)(2,1)S(1)}, bf16[128,512]{1,0:T(8,128)(2,1)S(1)}, u32[]{:S(2)}, u32[]{:S(2)}) collective-permute-start(bf16[128,512]{1,0:T(8,128)(2,1)S(1)} %collective-permute-done.1.second), channel_id=1, source_target_pairs={{0,1},{1,0},{2,3},{3,2},{4,5},{5,4},{6,7},{7,6},{8,9},{9,8},{10,11... | collective-permute-start | bytes 393224 | tf_op jit(solution)/shard_map/ppermute | solution.py:363
  6.9 0.7 %copy-start.1 = (s32[16,8]{0,1:T(8,128)S(1)}, s32[16,8]{0,1:T(8,128)}, u32[]{:S(2)}) copy-start(s32[16,8]{0,1:T(8,128)} %param.4) | copy-start | bytes 1540
  17.6 6.5 %collective-permute-start.4 = (f32[264,128]{1,0:T(8,128)S(1)}, f32[264,128]{1,0:T(8,128)S(1)}, u32[]{:S(2)}, u32[]{:S(2)}) collective-permute-start(f32[264,128]{1,0:T(8,128)S(1)} %get-tuple-element.33.packed_zero), channel_id=1, source_target_pairs={{0,2},{2,0},{4,6},{6,4},{8,10},{10,8},{12,14},{14,12},{16,18},{18,... | collective-permute-start | bytes 405512 | tf_op jit(solution)/shard_map/ppermute | solution.py:350
  24.1 7.3 %collective-permute-start.5 = (f32[264,128]{1,0:T(8,128)S(1)}, f32[264,128]{1,0:T(8,128)S(1)}, u32[]{:S(2)}, u32[]{:S(2)}) collective-permute-start(f32[264,128]{1,0:T(8,128)S(1)} %add.9.packed_one), channel_id=1, source_target_pairs={{0,4},{4,0},{2,6},{6,2},{8,12},{12,8},{10,14},{14,10},{16,20},{20,... | collective-permute-start | bytes 405512 | tf_op jit(solution)/shard_map/ppermute | solution.py:350
  31.4 8.5 %collective-permute-start.6 = (f32[264,128]{1,0:T(8,128)S(1)}, f32[264,128]{1,0:T(8,128)S(1)}, u32[]{:S(2)}, u32[]{:S(2)}) collective-permute-start(f32[264,128]{1,0:T(8,128)S(1)} %add.10.refs_0_), channel_id=1, source_target_pairs={{0,8},{8,0},{2,10},{10,2},{4,12},{12,4},{6,14},{14,6},{16,24},{24,... | collective-permute-start | bytes 405512 | tf_op jit(solution)/shard_map/ppermute | solution.py:350

commit v7 on v6

--- a/solution.py
+++ b/solution.py
@@ -13,6 +13,7 @@
 LANES = 128
 GROUP = 8
 PANEL = 32
+FIRST_EIGHTHS = 5
 ROWS_A_STEP = 4
 VMEM_LIMIT = 20 * 1024 * 1024
 VMEM_NEAR = 48 * 1024 * 1024
@@ -169,16 +170,25 @@
     packed[2 * h :, :] = jnp.broadcast_to(diagonal, (GROUP, h))
 
 
+def largest(packed):
+    h = packed.shape[1]
+    row, col = square_iota(h)
+    on_diagonal = jnp.where(row == col, packed[h : 2 * h, :], 0.0)
+    rows = jnp.maximum(jnp.max(on_diagonal, axis=0, keepdims=True), packed[2 * h : 2 * h + 1, :])
+    return jnp.max(rows, axis=1, keepdims=True)
+
+
 def unpack_symmetric(packed, full, b):
     h = packed.shape[1]
     row, col = square_iota(h)
-    shared = packed[h : 2 * h, :]
+    over = 1.0 / largest(packed)
+    shared = packed[h : 2 * h, :] * over
     lower = jnp.where(row > col, shared, 0.0)
-    diagonal = jnp.where(row == col, jnp.broadcast_to(packed[2 * h : 2 * h + 1, :], (h, h)), 0.0)
+    diagonal = jnp.where(row == col, jnp.broadcast_to(packed[2 * h : 2 * h + 1, :] * over, (h, h)), 0.0)
     upper = jnp.where(row <= col, shared, 0.0)
     full[b, :h, :h] = lower + lower.T + diagonal
     full[b, h:, h:] = upper + jnp.where(row < col, upper, 0.0).T
-    full[b, :h, h:] = packed[:h, :]
+    full[b, :h, h:] = packed[:h, :] * over
 
 
 def row_of(x, j):
@@ -224,35 +234,50 @@
                 for g in range(groups)
             ]
             head, top = v[g0], r[g0]
-            recips, v_rows, r_rows = [], [], []
-            pivots = None
-            for j in range(GROUP):
-                d = row_of(head[j], j)
-                rc = invert(d)
-                recips.append(rc)
-                pivots = d if pivots is None else jnp.where(sub == j, d, pivots)
-                v_rows.append([row_of(head[k], j) if k > j else None for k in range(GROUP)])
-                r_rows.append([row_of(x, j) for x in top])
-                if j < GROUP - 1:
-                    below = jnp.where(sub > j, head[j], 0.0)
-                    scaled = below * rc
-                    for k in range(j + 1, GROUP):
-                        if k == j + 1:
-                            head[k] = head[k] - (below * v_rows[j][k]) * rc
-                        else:
-                            head[k] = head[k] - scaled * v_rows[j][k]
+            steps, leading = [], [None] * len(top)
+            pivots = cross = dets = None
+            for j in range(0, GROUP, 2):
+                p00, p10, p11 = row_of(head[j], j), row_of(head[j], j + 1), row_of(head[j + 1], j + 1)
+                det = p00 * p11 - p10 * p10
+                guess = pl.reciprocal(det, approx=True)
+                refine = 2.0 - det * guess
+                later = range(j + 2, GROUP)
+                v_rows = {k: (row_of(head[k], j), row_of(head[k], j + 1)) for k in later}
+                r_rows = [(row_of(x, j), row_of(x, j + 1)) for x in top]
+                here = sub >= j
+                pivots = p00 if j == 0 else jnp.where(here, p00, pivots)
+                cross = p10 if j == 0 else jnp.where(here, p10, cross)
+                dets = det if j == 0 else jnp.where(here, det, dets)
+                leading = [x0 if j == 0 else jnp.where(here, x0, old) for (x0, _), old in zip(r_rows, leading)]
+                c0 = jnp.where(sub > j + 1, head[j], 0.0)
+                c1 = jnp.where(sub > j + 1, head[j + 1], 0.0)
+                for k in later[:2]:
+                    x0, x1 = v_rows[k]
+                    term = c0 * (p11 * x0 - p10 * x1) + c1 * (p00 * x1 - p10 * x0)
+                    head[k] = head[k] - (term * guess) * refine
+                inverse = guess * refine
+                q00, q10, q11 = p11 * inverse, p10 * inverse, p00 * inverse
+                steps.append((j, q00, q10, q11, v_rows, r_rows))
+                if j + 2 < GROUP:
+                    w0, w1 = c0 * q00 - c1 * q10, c1 * q11 - c0 * q10
+                    for k in later[2:]:
+                        head[k] = head[k] - w0 * v_rows[k][0] - w1 * v_rows[k][1]
                     for x in range(len(top)):
-                        top[x] = top[x] - scaled * r_rows[j][x]
+                        top[x] = top[x] - w0 * r_rows[x][0] - w1 * r_rows[x][1]
             for g in range(g0 + 1, groups):
-                for j in range(GROUP):
-                    scaled = v[g][j] * recips[j]
-                    for k in range(j + 1, GROUP):
-                        v[g][k] = v[g][k] - scaled * v_rows[j][k]
+                for j, q00, q10, q11, v_rows, r_rows in steps:
+                    c0, c1 = v[g][j], v[g][j + 1]
+                    w0, w1 = c0 * q00 - c1 * q10, c1 * q11 - c0 * q10
+                    for k in range(j + 2, GROUP):
+                        v[g][k] = v[g][k] - w0 * v_rows[k][0] - w1 * v_rows[k][1]
                     for x in range(len(top)):
-                        r[g][x] = r[g][x] - scaled * r_rows[j][x]
-            scale = lax.rsqrt(pivots)
+                        r[g][x] = r[g][x] - w0 * r_rows[x][0] - w1 * r_rows[x][1]
+            second_row = sub % 2 == 1
+            over = invert(pivots)
+            ratio = jnp.where(second_row, cross * over, 0.0)
+            scale = lax.rsqrt(jnp.where(second_row, dets * over, pivots))
             for x, (ref, c) in enumerate(parts):
-                done = top[x] * scale
+                done = (top[x] - ratio * leading[x]) * scale
                 if ref is a and c == ch:
                     done = jnp.where(lane >= sub + at, done, 0.0)
                 r[g0][x] = done
@@ -289,23 +314,26 @@
     return pl.ds(pl.multiple_of(place[1] * own, own), own)
 
 
-def first_kernel(packed_zero, packed_one, a, m):
+def first_kernel(stop, packed_zero, packed_one, a, m):
     unpack_symmetric(packed_zero, a, 0)
     unpack_symmetric(packed_one, a, 1)
     start_inverse(m)
-    factor(a, m, 0, a.shape[1] // 2)
-
-
-def second_kernel(scale, place, a_in, m_in, own_high, own_low, rest_high, rest_low, bases, transfer, upper_own, a, m):
+    factor(a, m, 0, stop)
+
+
+def second_kernel(start, scale, place, packed_zero, packed_one, a_in, m_in, own_high, own_low, rest_high, rest_low,
+                  bases, transfer, upper_own, a, m):
     del a_in, m_in
     n = a.shape[1]
-    factor(a, m, n // 2, n)
+    factor(a, m, start, n)
     clear_lower(a)
     own = upper_own.shape[0]
     rows = own_rows(place, own)
-    upper_own[...] = a[1, rows, :]
-    transfer[...] = dot_split(split_two(m[1]), split_two(a[0, rows, :]), NT)
-    turned = pltpu.roll(m[0, rows, :] * scale, lax.rem(n - place[1] * own, n), 1)
+    size_zero, size_one = largest(packed_zero), largest(packed_one)
+    upper_own[...] = a[1, rows, :] * jnp.sqrt(size_one)
+    child = a[0, rows, :] * (jnp.sqrt(size_zero) * lax.rsqrt(size_one))
+    transfer[...] = dot_split(split_two(m[1]), split_two(child), NT)
+    turned = pltpu.roll(m[0, rows, :] * (lax.rsqrt(size_zero) * scale), lax.rem(n - place[1] * own, n), 1)
     inverse = split_two(turned)
     for c in range(0, own_high.shape[1], 512):
         lanes = slice(c, c + 512)
@@ -326,10 +354,13 @@
     clear_lower(a)
     own = upper_own.shape[0]
     rows = own_rows(place, own)
+    sizes = [largest(ref) for ref in packed]
+    child = upper_own[...]
     for b in range(levels):
-        child = upper_own[...] if b == 0 else a[b - 1, rows, :]
+        child = child * lax.rsqrt(sizes[b])
         transfers[b][...] = dot_split(split_two(m[b]), split_two(child), NT)
-    top[...] = (a[levels - 1, rows, :] * top_scale).T
+        child = a[b, rows, :] * jnp.sqrt(sizes[b])
+    top[...] = (child * top_scale).T
 
 
 def whole():
@@ -431,11 +462,12 @@
     )(place, columns, blocks, *other_halos, own_high, own_low, own_gram)
 
     square = shape((2, total, total), F32)
+    split_row = total * FIRST_EIGHTHS // 8 // PANEL * PANEL
     transfer_shape = shape((total, own), F32)
     gram_one = packed + from_partner(packed, "leaf", 0)
     gram_two = gram_one + from_partner(gram_one, "leaf", 1)
     a, m = pl.pallas_call(
-        first_kernel,
+        functools.partial(first_kernel, split_row),
         in_specs=[whole()] * 2,
         out_specs=[whole()] * 2,
         out_shape=[square] * 2,
@@ -445,15 +477,15 @@
     )(packed, gram_one)
     gram_three = gram_two + from_partner(gram_two, "leaf", 2)
     bases, transfer_one, upper_own, _, _ = pl.pallas_call(
-        functools.partial(second_kernel, math.sqrt(row_count)),
-        in_specs=[smem] + [whole()] * 6,
+        functools.partial(second_kernel, split_row, math.sqrt(row_count)),
+        in_specs=[smem] + [whole()] * 8,
         out_specs=[whole()] * 5,
         out_shape=[shape((own, row_count), F32), transfer_shape, shape((own, total), F32), square, square],
-        input_output_aliases={1: 3, 2: 4},
+        input_output_aliases={3: 3, 4: 4},
         compiler_params=params(),
         cost_estimate=pl.CostEstimate(flops=3 * 10**9, bytes_accessed=1024 * 1024, transcendentals=0),
         name="second",
-    )(place, a, m, own_high, own_low, rest_high, rest_low)
+    )(place, packed, gram_one, a, m, own_high, own_low, rest_high, rest_low)
     transfer_two, transfer_three, top_factor = pl.pallas_call(
         functools.partial(tree_kernel, 1.0 / math.sqrt(2**LEVELS * row_count)),
         in_specs=[smem] + [whole()] * 3,

time: 51.5 us -> 51.5 us (level)
  no operation moved by 1% of the time
where the time goes in v7:
time: 51.5 us; the launch traced here: 51.3 us
  Pallas kernels  34 us (66%)
  starting transfers between devices  13.4 us (26%)
  local copies, waits for them, and re-layouts  1.73 us (3%)
  waiting for transfers between devices  1.32 us (3%)
  between operations  0.73 us (1%)
    pallas_call x1, Pallas kernels, shards(): pl.pallas_call(functools.partial(tree_kernel, 1.0 / math.sqrt(2 ** LEVELS...  11.4 us
    ppermute x3, starting transfers between devices, from_partner(): return lax.ppermute(block, axis, route)  9.31 us
    pallas_call x1, Pallas kernels, shards(): pl.pallas_call(functools.partial(first_kernel, split_row), in_specs=[whol...  6.34 us
    pallas_call x1, Pallas kernels, shards(): pl.pallas_call(own_kernel, in_specs=[smem, smem, hbm] + [whole()] * 3, ou...  6.05 us
    pallas_call x1, Pallas kernels, shards(): pl.pallas_call(functools.partial(second_kernel, split_row, math.sqrt(row_...  5.61 us
    pallas_call x1, Pallas kernels, shards(): pl.pallas_call(functools.partial(others_kernel, parts), in_specs=[smem, s...  3.93 us
    ppermute x2, starting transfers between devices, sample_shift(): lax.ppermute(block, 'samp', [(i, (i - d) % count) for i in range(count)])  2.88 us
    unnamed x4, local copies, waits for them, and re-layouts  1.73 us
  transfers between devices with their start and end apart: 7, of which 2 were waited for; matrix products, arithmetic and copies ran while one was open for 0% of the time, Pallas kernels for 35%

profile of v7, /device:TPU:0, one launch (start us, length us, event | category | flops | bytes accessed | tf_op | source)
XLA Modules:
  0.0 51.3 jit_solution(2992750979439013068)
XLA Ops:
  0.6 0.1 pad_add_fusion.1.at
  0.7 0.0 copy-start
  0.7 1.0 %copy-done = bf16[128,2048]{1,0:T(8,128)(2,1)S(1)} copy-done((bf16[128,2048]{1,0:T(8,128)(2,1)S(1)}, bf16[128,2048]{1,0:T(8,128)(2,1)}, u32[]{:S(2)}) %copy-start) | copy-done | bytes 524312
  1.8 0.7 %prepare.1 = (bf16[128,2048]{1,0:T(8,128)(2,1)S(1)}, bf16[128,512]{1,0:T(8,128)(2,1)S(1)}, bf16[128,512]{1,0:T(8,128)(2,1)S(1)}) custom-call(s32[2]{0:T(128)S(1)} %pad_add_fusion.1.at, bf16[128,2048]{1,0:T(8,128)(2,1)S(1)} %copy-done), custom_call_target="tpu_custom_call" | custom-call | tf_op jit(solution)/shard_map/prepare/pallas_call | solution.py:415
  2.4 0.5 %collective-permute-start = (bf16[128,512]{1,0:T(8,128)(2,1)S(1)}, bf16[128,512]{1,0:T(8,128)(2,1)S(1)}, u32[]{:S(2)}, u32[]{:S(2)}) collective-permute-start(bf16[128,512]{1,0:T(8,128)(2,1)S(1)} %get-tuple-element.26), channel_id=1, source_target_pairs={{0,2},{2,0},{4,6},{6,4},{8,10},{10,8},{12,14},{14,12},{16,18},{18,... | collective-permute-start | bytes 393224 | tf_op jit(solution)/shard_map/ppermute | solution.py:389
  2.9 0.7 %collective-permute-start.1 = (bf16[128,512]{1,0:T(8,128)(2,1)S(1)}, bf16[128,512]{1,0:T(8,128)(2,1)S(1)}, u32[]{:S(2)}, u32[]{:S(2)}) collective-permute-start(bf16[128,512]{1,0:T(8,128)(2,1)S(1)} %get-tuple-element.27), channel_id=1, source_target_pairs={{2,4},{4,2},{6,8},{8,6},{10,12},{12,10},{14,16},{16,14},{18,20},{2... | collective-permute-start | bytes 393224 | tf_op jit(solution)/shard_map/ppermute | solution.py:389
  3.6 0.3 collective-permute-done.first
  3.9 2.8 %collective-permute-start.2 = (bf16[128,512]{1,0:T(8,128)(2,1)S(1)}, bf16[128,512]{1,0:T(8,128)(2,1)S(1)}, u32[]{:S(2)}, u32[]{:S(2)}) collective-permute-start(bf16[128,512]{1,0:T(8,128)(2,1)S(1)} %collective-permute-done.first), channel_id=1, source_target_pairs={{0,1},{1,0},{2,3},{3,2},{4,5},{5,4},{6,7},{7,6},{8,9},{9,8},{10,11... | collective-permute-start | bytes 393224 | tf_op jit(solution)/shard_map/ppermute | solution.py:394
  6.8 0.0 collective-permute-done.1.second
  6.8 0.0 collective-permute-start.3
  6.8 0.1 pad_add_fusion.place
  6.9 0.0 copy-start.1
  6.9 0.7 %copy-done.1 = s32[16,8]{0,1:T(8,128)S(1)} copy-done((s32[16,8]{0,1:T(8,128)S(1)}, s32[16,8]{0,1:T(8,128)}, u32[]{:S(2)}) %copy-start.1) | copy-done | bytes 536
  7.6 6.1 %own.1 = (f32[128,2048]{1,0:T(8,128)}, bf16[16,8,128,128]{3,2,1,0:T(8,128)(2,1)S(1)}, bf16[128,2048]{1,0:T(8,128)(2,1)S(1)}, bf16[128,2048]{1,0:T(8,128)(2,1)S(1)}, f32[128,128]{1,0:T(8,128)S(1)}) custom-call(s32[2]{0:T(128)S(1)} %pad_add_fusion.place, s32[8,16]{1,0:T(8,128)S(1)} %bitcast.5, bf16[16,8,128,128]{3,2,1,0:T(8,128)(2,1)} %blocks_hbm.1, ...), custom_call_target="tpu_custom_call" | custom-call | flops 1073741824 | bytes 6291456 | tf_op jit(solution)/shard_map/own/pallas_call | solution.py:428
  13.6 0.0 collective-permute-done.2.refs_0_
  13.6 0.0 collective-permute-done.3.refs_1_
  13.6 3.9 %others.1 = (bf16[128,2048]{1,0:T(8,128)(2,1)S(1)}, bf16[128,2048]{1,0:T(8,128)(2,1)S(1)}, f32[264,128]{1,0:T(8,128)S(1)}) custom-call(s32[2]{0:T(128)S(1)} %pad_add_fusion.place, s32[8,16]{1,0:T(8,128)S(1)} %bitcast.6, bf16[16,8,128,128]{3,2,1,0:T(8,128)(2,1)S(1)} %get-tuple-element.29.blocks, bf16[128,512]{1,0:T(8,128)(2,1)S(1)} %collective-permute-done.2.refs_0_, ...), custom_call_target="tpu_custom_call" | custom-call | tf_op jit(solution)/shard_map/others/pallas_call | solution.py:454
  17.6 5.5 %collective-permute-start.4 = (f32[264,128]{1,0:T(8,128)S(1)}, f32[264,128]{1,0:T(8,128)S(1)}, u32[]{:S(2)}, u32[]{:S(2)}) collective-permute-start(f32[264,128]{1,0:T(8,128)S(1)} %get-tuple-element.33.packed_zero), channel_id=1, source_target_pairs={{0,2},{2,0},{4,6},{6,4},{8,10},{10,8},{12,14},{14,12},{16,18},{18,... | collective-permute-start | bytes 405512 | tf_op jit(solution)/shard_map/ppermute | solution.py:381
  23.1 1.0 %collective-permute-done.4 = f32[264,128]{1,0:T(8,128)S(1)} collective-permute-done((f32[264,128]{1,0:T(8,128)S(1)}, f32[264,128]{1,0:T(8,128)S(1)}, u32[]{:S(2)}, u32[]{:S(2)}) %collective-permute-start.4) | collective-permute-done | bytes 135200 | tf_op jit(solution)/shard_map/ppermute | solution.py:381
  24.1 2.2 %collective-permute-start.5 = (f32[264,128]{1,0:T(8,128)S(1)}, f32[264,128]{1,0:T(8,128)S(1)}, u32[]{:S(2)}, u32[]{:S(2)}) collective-permute-start(f32[264,128]{1,0:T(8,128)S(1)} %add.9.packed_one), channel_id=1, source_target_pairs={{0,4},{4,0},{2,6},{6,2},{8,12},{12,8},{10,14},{14,10},{16,20},{20,... | collective-permute-start | bytes 405512 | tf_op jit(solution)/shard_map/ppermute | solution.py:381
  26.3 6.3 %first.1 = (f32[2,256,256]{2,1,0:T(8,128)S(1)}, f32[2,256,256]{2,1,0:T(8,128)S(1)}) custom-call(f32[264,128]{1,0:T(8,128)S(1)} %get-tuple-element.33.packed_zero, f32[264,128]{1,0:T(8,128)S(1)} %add.9.packed_one), custom_call_target="tpu_custom_call" | custom-call | flops 3000000000 | bytes 1048576 | tf_op jit(solution)/shard_map/first/pallas_call | solution.py:469
  32.6 0.0 collective-permute-done.5
  32.6 1.6 %collective-permute-start.6 = (f32[264,128]{1,0:T(8,128)S(1)}, f32[264,128]{1,0:T(8,128)S(1)}, u32[]{:S(2)}, u32[]{:S(2)}) collective-permute-start(f32[264,128]{1,0:T(8,128)S(1)} %add.10.refs_0_), channel_id=1, source_target_pairs={{0,8},{8,0},{2,10},{10,2},{4,12},{12,4},{6,14},{14,6},{16,24},{24,... | collective-permute-start | bytes 405512 | tf_op jit(solution)/shard_map/ppermute | solution.py:381
  34.3 5.6 %second.1 = (f32[128,2048]{1,0:T(8,128)}, f32[256,128]{1,0:T(8,128)}, f32[128,256]{1,0:T(8,128)S(1)}, f32[2,256,256]{2,1,0:T(8,128)S(1)}, f32[2,256,256]{2,1,0:T(8,128)S(1)}) custom-call(s32[2]{0:T(128)S(1)} %pad_add_fusion.place, f32[264,128]{1,0:T(8,128)S(1)} %get-tuple-element.33.packed_zero, ...), custom_call_target="tpu_custom_call", output_to_operand_aliasing={{3}: (3, {}), {4}: (4, {})} | custom-call | flops 3000000000 | bytes 1048576 | tf_op jit(solution)/shard_map/second/pallas_call | solution.py:479
  39.9 0.0 collective-permute-done.6
  39.9 11.4 %tree.1 = (f32[256,128]{1,0:T(8,128)}, f32[256,128]{1,0:T(8,128)}, f32[256,128]{1,0:T(8,128)}) custom-call(s32[2]{0:T(128)S(1)} %pad_add_fusion.place, f32[128,256]{1,0:T(8,128)S(1)} %get-tuple-element.40.upper_own, f32[264,128]{1,0:T(8,128)S(1)} %add.10.refs_0_, f32[264,128]{1,0:T(8,128)S(1)} %add.11.refs_1_), custom_call_target="tpu_custom_call" | custom-call | tf_op jit(solution)/shard_map/tree/pallas_call | solution.py:489
  (3 shorter events, 0.1 us)
Async XLA Ops:
  0.7 1.0 %copy-start = (bf16[128,2048]{1,0:T(8,128)(2,1)S(1)}, bf16[128,2048]{1,0:T(8,128)(2,1)}, u32[]{:S(2)}) copy-start(bf16[128,2048]{1,0:T(8,128)(2,1)} %samples.1) | copy-start | bytes 1572868
  2.4 1.5 %collective-permute-start = (bf16[128,512]{1,0:T(8,128)(2,1)S(1)}, bf16[128,512]{1,0:T(8,128)(2,1)S(1)}, u32[]{:S(2)}, u32[]{:S(2)}) collective-permute-start(bf16[128,512]{1,0:T(8,128)(2,1)S(1)} %get-tuple-element.26), channel_id=1, source_target_pairs={{0,2},{2,0},{4,6},{6,4},{8,10},{10,8},{12,14},{14,12},{16,18},{18,... | collective-permute-start | bytes 393224 | tf_op jit(solution)/shard_map/ppermute | solution.py:389
  2.9 3.8 %collective-permute-start.1 = (bf16[128,512]{1,0:T(8,128)(2,1)S(1)}, bf16[128,512]{1,0:T(8,128)(2,1)S(1)}, u32[]{:S(2)}, u32[]{:S(2)}) collective-permute-start(bf16[128,512]{1,0:T(8,128)(2,1)S(1)} %get-tuple-element.27), channel_id=1, source_target_pairs={{2,4},{4,2},{6,8},{8,6},{10,12},{12,10},{14,16},{16,14},{18,20},{2... | collective-permute-start | bytes 393224 | tf_op jit(solution)/shard_map/ppermute | solution.py:389
  3.9 9.7 %collective-permute-start.2 = (bf16[128,512]{1,0:T(8,128)(2,1)S(1)}, bf16[128,512]{1,0:T(8,128)(2,1)S(1)}, u32[]{:S(2)}, u32[]{:S(2)}) collective-permute-start(bf16[128,512]{1,0:T(8,128)(2,1)S(1)} %collective-permute-done.first), channel_id=1, source_target_pairs={{0,1},{1,0},{2,3},{3,2},{4,5},{5,4},{6,7},{7,6},{8,9},{9,8},{10,11... | collective-permute-start | bytes 393224 | tf_op jit(solution)/shard_map/ppermute | solution.py:394
  6.8 6.9 %collective-permute-start.3 = (bf16[128,512]{1,0:T(8,128)(2,1)S(1)}, bf16[128,512]{1,0:T(8,128)(2,1)S(1)}, u32[]{:S(2)}, u32[]{:S(2)}) collective-permute-start(bf16[128,512]{1,0:T(8,128)(2,1)S(1)} %collective-permute-done.1.second), channel_id=1, source_target_pairs={{0,1},{1,0},{2,3},{3,2},{4,5},{5,4},{6,7},{7,6},{8,9},{9,8},{10,11... | collective-permute-start | bytes 393224 | tf_op jit(solution)/shard_map/ppermute | solution.py:394
  6.9 0.7 %copy-start.1 = (s32[16,8]{0,1:T(8,128)S(1)}, s32[16,8]{0,1:T(8,128)}, u32[]{:S(2)}) copy-start(s32[16,8]{0,1:T(8,128)} %param.4) | copy-start | bytes 1540
  17.6 6.5 %collective-permute-start.4 = (f32[264,128]{1,0:T(8,128)S(1)}, f32[264,128]{1,0:T(8,128)S(1)}, u32[]{:S(2)}, u32[]{:S(2)}) collective-permute-start(f32[264,128]{1,0:T(8,128)S(1)} %get-tuple-element.33.packed_zero), channel_id=1, source_target_pairs={{0,2},{2,0},{4,6},{6,4},{8,10},{10,8},{12,14},{14,12},{16,18},{18,... | collective-permute-start | bytes 405512 | tf_op jit(solution)/shard_map/ppermute | solution.py:381
  24.1 8.5 %collective-permute-start.5 = (f32[264,128]{1,0:T(8,128)S(1)}, f32[264,128]{1,0:T(8,128)S(1)}, u32[]{:S(2)}, u32[]{:S(2)}) collective-permute-start(f32[264,128]{1,0:T(8,128)S(1)} %add.9.packed_one), channel_id=1, source_target_pairs={{0,4},{4,0},{2,6},{6,2},{8,12},{12,8},{10,14},{14,10},{16,20},{20,... | collective-permute-start | bytes 405512 | tf_op jit(solution)/shard_map/ppermute | solution.py:381
  32.6 7.3 %collective-permute-start.6 = (f32[264,128]{1,0:T(8,128)S(1)}, f32[264,128]{1,0:T(8,128)S(1)}, u32[]{:S(2)}, u32[]{:S(2)}) collective-permute-start(f32[264,128]{1,0:T(8,128)S(1)} %add.10.refs_0_), channel_id=1, source_target_pairs={{0,8},{8,0},{2,10},{10,2},{4,12},{12,4},{6,14},{14,6},{16,24},{24,... | collective-permute-start | bytes 405512 | tf_op jit(solution)/shard_map/ppermute | solution.py:381

commit v8 on v7

--- a/solution.py
+++ b/solution.py
@@ -33,13 +33,6 @@
     return high, (x - high.astype(F32)).astype(BF16)
 
 
-def split_three(x):
-    high = x.astype(BF16)
-    rest = x - high.astype(F32)
-    middle = rest.astype(BF16)
-    return high, middle, (rest - middle.astype(F32)).astype(BF16)
-
-
 def dot_split(a, b, dims):
     (a_high, a_low), (b_high, b_low) = a, b
     return dot(a_high, b_high, dims) + (dot(a_high, b_low, dims) + dot(a_low, b_high, dims))
@@ -215,14 +208,13 @@
 
 def factor(a, m, first, last):
     batch, n, _ = a.shape
-    chunks = n // LANES
     groups = PANEL // GROUP
     tile = (batch, GROUP, LANES)
     sub = lax.broadcasted_iota(jnp.int32, tile, 1)
     lane = lax.broadcasted_iota(jnp.int32, tile, 2)
     for p in range(first, last, PANEL):
         ch = p // LANES
-        parts = [(a, c) for c in range(ch, chunks)] + [(m, c) for c in range(ch + 1)]
+        parts = [(a, ch), (m, ch)]
         rows = [slice(p + GROUP * g, p + GROUP * (g + 1)) for g in range(groups)]
         r = [[ref[:, rows[g], c * LANES : (c + 1) * LANES] for ref, c in parts] for g in range(groups)]
         for g0 in range(groups):
@@ -282,27 +274,42 @@
                     done = jnp.where(lane >= sub + at, done, 0.0)
                 r[g0][x] = done
                 ref[:, rows[g0], c * LANES : (c + 1) * LANES] = done
-        if p + PANEL == n:
-            break
+        end = (ch + 1) * LANES
+        if p + PANEL == end:
+            join_chunks(a, m, ch)
+            continue
         for b in range(batch):
             panel = jnp.concatenate(
                 [jnp.concatenate([r[g][x][b] for g in range(groups)], axis=0) for x in range(len(parts))], axis=1
             )
-            h, mid, low = split_three(panel)
-            left = jnp.concatenate([h, h, mid, mid, h, low], axis=0)
-            right = jnp.concatenate([h, mid, h, mid, low, h], axis=0)
-            for c in range(ch, chunks):
-                start = max(p + PANEL, c * LANES)
-                stop = (c + 1) * LANES
-                if start >= stop:
-                    continue
-                x0 = c - ch
-                update = dot(left[:, x0 * LANES : (x0 + 1) * LANES], right, TN)[start - c * LANES :, :]
-                for x, (ref, e) in enumerate(parts):
-                    if ref is a and e < c:
-                        continue
-                    lanes = slice(e * LANES, (e + 1) * LANES)
-                    ref[b, start:stop, lanes] = ref[b, start:stop, lanes] - update[:, x * LANES : (x + 1) * LANES]
+            high, low = split_two(panel)
+            left = jnp.concatenate([high[:, :LANES], high[:, :LANES], low[:, :LANES]], axis=0)
+            right = jnp.concatenate([high, low, high], axis=0)
+            update = dot(left, right, TN)[p + PANEL - ch * LANES :, :]
+            for x, (ref, e) in enumerate(parts):
+                lanes = slice(e * LANES, (e + 1) * LANES)
+                ref[b, p + PANEL : end, lanes] = ref[b, p + PANEL : end, lanes] - update[:, x * LANES : (x + 1) * LANES]
+
+
+def join_chunks(a, m, ch):
+    batch, n, _ = a.shape
+    here = slice(ch * LANES, (ch + 1) * LANES)
+    for b in range(batch):
+        inverse = split_two(m[b, here, here])
+        if ch > 0:
+            before = slice(0, ch * LANES)
+            m[b, here, before] = -dot_split(inverse, split_two(m[b, here, before]), NN)
+        later = slice((ch + 1) * LANES, n)
+        if later.start == n:
+            continue
+        upper = dot_split(inverse, split_two(a[b, here, later]), NN)
+        a[b, here, later] = upper
+        upper = split_two(upper)
+        done = split_two(m[b, here, : (ch + 1) * LANES])
+        both = tuple(jnp.concatenate(pair, axis=1) for pair in zip(upper, done))
+        update = dot_split(upper, both, TN)
+        a[b, later, later] = a[b, later, later] - update[:, : n - later.start]
+        m[b, later, : later.start] = m[b, later, : later.start] + update[:, n - later.start :]
 
 
 def invert(x):

time: 51.5 us -> 50.9 us (0.988)
  Pallas kernels: 34 us -> 33.3 us
where the time goes in v8:
time: 50.9 us; the launch traced here: 50.6 us
  Pallas kernels  33.3 us (65%)
  starting transfers between devices  13.4 us (26%)
  local copies, waits for them, and re-layouts  1.73 us (3%)
  waiting for transfers between devices  1.32 us (3%)
  between operations  0.73 us (1%)
    pallas_call x1, Pallas kernels, shards(): pl.pallas_call(functools.partial(tree_kernel, 1.0 / math.sqrt(2 ** LEVELS...  11.1 us
    ppermute x3, starting transfers between devices, from_partner(): return lax.ppermute(block, axis, route)  9.32 us
    pallas_call x1, Pallas kernels, shards(): pl.pallas_call(own_kernel, in_specs=[smem, smem, hbm] + [whole()] * 3, ou...  6.05 us
    pallas_call x1, Pallas kernels, shards(): pl.pallas_call(functools.partial(first_kernel, split_row), in_specs=[whol...  6.03 us
    pallas_call x1, Pallas kernels, shards(): pl.pallas_call(functools.partial(second_kernel, split_row, math.sqrt(row_...  5.56 us
    pallas_call x1, Pallas kernels, shards(): pl.pallas_call(functools.partial(others_kernel, parts), in_specs=[smem, s...  3.92 us
    ppermute x2, starting transfers between devices, sample_shift(): lax.ppermute(block, 'samp', [(i, (i - d) % count) for i in range(count)])  2.88 us
    unnamed x4, local copies, waits for them, and re-layouts  1.73 us
  transfers between devices with their start and end apart: 7, of which 2 were waited for; matrix products, arithmetic and copies ran while one was open for 0% of the time, Pallas kernels for 35%

profile of v8, /device:TPU:0, one launch (start us, length us, event | category | flops | bytes accessed | tf_op | source)
XLA Modules:
  0.0 50.6 jit_solution(7742209587747505261)
XLA Ops:
  0.6 0.1 pad_add_fusion.1.at
  0.7 0.0 copy-start
  0.7 1.0 %copy-done = bf16[128,2048]{1,0:T(8,128)(2,1)S(1)} copy-done((bf16[128,2048]{1,0:T(8,128)(2,1)S(1)}, bf16[128,2048]{1,0:T(8,128)(2,1)}, u32[]{:S(2)}) %copy-start) | copy-done | bytes 524312
  1.8 0.7 %prepare.1 = (bf16[128,2048]{1,0:T(8,128)(2,1)S(1)}, bf16[128,512]{1,0:T(8,128)(2,1)S(1)}, bf16[128,512]{1,0:T(8,128)(2,1)S(1)}) custom-call(s32[2]{0:T(128)S(1)} %pad_add_fusion.1.at, bf16[128,2048]{1,0:T(8,128)(2,1)S(1)} %copy-done), custom_call_target="tpu_custom_call" | custom-call | tf_op jit(solution)/shard_map/prepare/pallas_call | solution.py:422
  2.4 0.5 %collective-permute-start = (bf16[128,512]{1,0:T(8,128)(2,1)S(1)}, bf16[128,512]{1,0:T(8,128)(2,1)S(1)}, u32[]{:S(2)}, u32[]{:S(2)}) collective-permute-start(bf16[128,512]{1,0:T(8,128)(2,1)S(1)} %get-tuple-element.26), channel_id=1, source_target_pairs={{0,2},{2,0},{4,6},{6,4},{8,10},{10,8},{12,14},{14,12},{16,18},{18,... | collective-permute-start | bytes 393224 | tf_op jit(solution)/shard_map/ppermute | solution.py:396
  2.9 0.7 %collective-permute-start.1 = (bf16[128,512]{1,0:T(8,128)(2,1)S(1)}, bf16[128,512]{1,0:T(8,128)(2,1)S(1)}, u32[]{:S(2)}, u32[]{:S(2)}) collective-permute-start(bf16[128,512]{1,0:T(8,128)(2,1)S(1)} %get-tuple-element.27), channel_id=1, source_target_pairs={{2,4},{4,2},{6,8},{8,6},{10,12},{12,10},{14,16},{16,14},{18,20},{2... | collective-permute-start | bytes 393224 | tf_op jit(solution)/shard_map/ppermute | solution.py:396
  3.6 0.3 collective-permute-done.first
  3.9 2.8 %collective-permute-start.2 = (bf16[128,512]{1,0:T(8,128)(2,1)S(1)}, bf16[128,512]{1,0:T(8,128)(2,1)S(1)}, u32[]{:S(2)}, u32[]{:S(2)}) collective-permute-start(bf16[128,512]{1,0:T(8,128)(2,1)S(1)} %collective-permute-done.first), channel_id=1, source_target_pairs={{0,1},{1,0},{2,3},{3,2},{4,5},{5,4},{6,7},{7,6},{8,9},{9,8},{10,11... | collective-permute-start | bytes 393224 | tf_op jit(solution)/shard_map/ppermute | solution.py:401
  6.8 0.0 collective-permute-done.1.second
  6.8 0.0 collective-permute-start.3
  6.8 0.1 pad_add_fusion.place
  6.9 0.0 copy-start.1
  6.9 0.7 %copy-done.1 = s32[16,8]{0,1:T(8,128)S(1)} copy-done((s32[16,8]{0,1:T(8,128)S(1)}, s32[16,8]{0,1:T(8,128)}, u32[]{:S(2)}) %copy-start.1) | copy-done | bytes 536
  7.6 6.1 %own.1 = (f32[128,2048]{1,0:T(8,128)}, bf16[16,8,128,128]{3,2,1,0:T(8,128)(2,1)S(1)}, bf16[128,2048]{1,0:T(8,128)(2,1)S(1)}, bf16[128,2048]{1,0:T(8,128)(2,1)S(1)}, f32[128,128]{1,0:T(8,128)S(1)}) custom-call(s32[2]{0:T(128)S(1)} %pad_add_fusion.place, s32[8,16]{1,0:T(8,128)S(1)} %bitcast.5, bf16[16,8,128,128]{3,2,1,0:T(8,128)(2,1)} %blocks_hbm.1, ...), custom_call_target="tpu_custom_call" | custom-call | flops 1073741824 | bytes 6291456 | tf_op jit(solution)/shard_map/own/pallas_call | solution.py:435
  13.6 0.0 collective-permute-done.2.refs_0_
  13.6 0.0 collective-permute-done.3.refs_1_
  13.6 3.9 %others.1 = (bf16[128,2048]{1,0:T(8,128)(2,1)S(1)}, bf16[128,2048]{1,0:T(8,128)(2,1)S(1)}, f32[264,128]{1,0:T(8,128)S(1)}) custom-call(s32[2]{0:T(128)S(1)} %pad_add_fusion.place, s32[8,16]{1,0:T(8,128)S(1)} %bitcast.6, bf16[16,8,128,128]{3,2,1,0:T(8,128)(2,1)S(1)} %get-tuple-element.29.blocks, bf16[128,512]{1,0:T(8,128)(2,1)S(1)} %collective-permute-done.2.refs_0_, ...), custom_call_target="tpu_custom_call" | custom-call | tf_op jit(solution)/shard_map/others/pallas_call | solution.py:461
  17.6 5.5 %collective-permute-start.4 = (f32[264,128]{1,0:T(8,128)S(1)}, f32[264,128]{1,0:T(8,128)S(1)}, u32[]{:S(2)}, u32[]{:S(2)}) collective-permute-start(f32[264,128]{1,0:T(8,128)S(1)} %get-tuple-element.33.packed_zero), channel_id=1, source_target_pairs={{0,2},{2,0},{4,6},{6,4},{8,10},{10,8},{12,14},{14,12},{16,18},{18,... | collective-permute-start | bytes 405512 | tf_op jit(solution)/shard_map/ppermute | solution.py:388
  23.0 1.0 %collective-permute-done.4 = f32[264,128]{1,0:T(8,128)S(1)} collective-permute-done((f32[264,128]{1,0:T(8,128)S(1)}, f32[264,128]{1,0:T(8,128)S(1)}, u32[]{:S(2)}, u32[]{:S(2)}) %collective-permute-start.4) | collective-permute-done | bytes 135200 | tf_op jit(solution)/shard_map/ppermute | solution.py:388
  24.1 2.2 %collective-permute-start.5 = (f32[264,128]{1,0:T(8,128)S(1)}, f32[264,128]{1,0:T(8,128)S(1)}, u32[]{:S(2)}, u32[]{:S(2)}) collective-permute-start(f32[264,128]{1,0:T(8,128)S(1)} %add.9.packed_one), channel_id=1, source_target_pairs={{0,4},{4,0},{2,6},{6,2},{8,12},{12,8},{10,14},{14,10},{16,20},{20,... | collective-permute-start | bytes 405512 | tf_op jit(solution)/shard_map/ppermute | solution.py:388
  26.3 6.0 %first.1 = (f32[2,256,256]{2,1,0:T(8,128)S(1)}, f32[2,256,256]{2,1,0:T(8,128)S(1)}) custom-call(f32[264,128]{1,0:T(8,128)S(1)} %get-tuple-element.33.packed_zero, f32[264,128]{1,0:T(8,128)S(1)} %add.9.packed_one), custom_call_target="tpu_custom_call" | custom-call | flops 3000000000 | bytes 1048576 | tf_op jit(solution)/shard_map/first/pallas_call | solution.py:476
  32.3 0.0 collective-permute-done.5
  32.3 1.6 %collective-permute-start.6 = (f32[264,128]{1,0:T(8,128)S(1)}, f32[264,128]{1,0:T(8,128)S(1)}, u32[]{:S(2)}, u32[]{:S(2)}) collective-permute-start(f32[264,128]{1,0:T(8,128)S(1)} %add.10.refs_0_), channel_id=1, source_target_pairs={{0,8},{8,0},{2,10},{10,2},{4,12},{12,4},{6,14},{14,6},{16,24},{24,... | collective-permute-start | bytes 405512 | tf_op jit(solution)/shard_map/ppermute | solution.py:388
  34.0 5.6 %second.1 = (f32[128,2048]{1,0:T(8,128)}, f32[256,128]{1,0:T(8,128)}, f32[128,256]{1,0:T(8,128)S(1)}, f32[2,256,256]{2,1,0:T(8,128)S(1)}, f32[2,256,256]{2,1,0:T(8,128)S(1)}) custom-call(s32[2]{0:T(128)S(1)} %pad_add_fusion.place, f32[264,128]{1,0:T(8,128)S(1)} %get-tuple-element.33.packed_zero, ...), custom_call_target="tpu_custom_call", output_to_operand_aliasing={{3}: (3, {}), {4}: (4, {})} | custom-call | flops 3000000000 | bytes 1048576 | tf_op jit(solution)/shard_map/second/pallas_call | solution.py:486
  39.5 0.0 collective-permute-done.6
  39.6 11.1 %tree.1 = (f32[256,128]{1,0:T(8,128)}, f32[256,128]{1,0:T(8,128)}, f32[256,128]{1,0:T(8,128)}) custom-call(s32[2]{0:T(128)S(1)} %pad_add_fusion.place, f32[128,256]{1,0:T(8,128)S(1)} %get-tuple-element.40.upper_own, f32[264,128]{1,0:T(8,128)S(1)} %add.10.refs_0_, f32[264,128]{1,0:T(8,128)S(1)} %add.11.refs_1_), custom_call_target="tpu_custom_call" | custom-call | tf_op jit(solution)/shard_map/tree/pallas_call | solution.py:496
  (3 shorter events, 0.1 us)
Async XLA Ops:
  0.7 1.0 %copy-start = (bf16[128,2048]{1,0:T(8,128)(2,1)S(1)}, bf16[128,2048]{1,0:T(8,128)(2,1)}, u32[]{:S(2)}) copy-start(bf16[128,2048]{1,0:T(8,128)(2,1)} %samples.1) | copy-start | bytes 1572868
  2.4 1.5 %collective-permute-start = (bf16[128,512]{1,0:T(8,128)(2,1)S(1)}, bf16[128,512]{1,0:T(8,128)(2,1)S(1)}, u32[]{:S(2)}, u32[]{:S(2)}) collective-permute-start(bf16[128,512]{1,0:T(8,128)(2,1)S(1)} %get-tuple-element.26), channel_id=1, source_target_pairs={{0,2},{2,0},{4,6},{6,4},{8,10},{10,8},{12,14},{14,12},{16,18},{18,... | collective-permute-start | bytes 393224 | tf_op jit(solution)/shard_map/ppermute | solution.py:396
  2.9 3.8 %collective-permute-start.1 = (bf16[128,512]{1,0:T(8,128)(2,1)S(1)}, bf16[128,512]{1,0:T(8,128)(2,1)S(1)}, u32[]{:S(2)}, u32[]{:S(2)}) collective-permute-start(bf16[128,512]{1,0:T(8,128)(2,1)S(1)} %get-tuple-element.27), channel_id=1, source_target_pairs={{2,4},{4,2},{6,8},{8,6},{10,12},{12,10},{14,16},{16,14},{18,20},{2... | collective-permute-start | bytes 393224 | tf_op jit(solution)/shard_map/ppermute | solution.py:396
  3.9 9.7 %collective-permute-start.2 = (bf16[128,512]{1,0:T(8,128)(2,1)S(1)}, bf16[128,512]{1,0:T(8,128)(2,1)S(1)}, u32[]{:S(2)}, u32[]{:S(2)}) collective-permute-start(bf16[128,512]{1,0:T(8,128)(2,1)S(1)} %collective-permute-done.first), channel_id=1, source_target_pairs={{0,1},{1,0},{2,3},{3,2},{4,5},{5,4},{6,7},{7,6},{8,9},{9,8},{10,11... | collective-permute-start | bytes 393224 | tf_op jit(solution)/shard_map/ppermute | solution.py:401
  6.8 6.9 %collective-permute-start.3 = (bf16[128,512]{1,0:T(8,128)(2,1)S(1)}, bf16[128,512]{1,0:T(8,128)(2,1)S(1)}, u32[]{:S(2)}, u32[]{:S(2)}) collective-permute-start(bf16[128,512]{1,0:T(8,128)(2,1)S(1)} %collective-permute-done.1.second), channel_id=1, source_target_pairs={{0,1},{1,0},{2,3},{3,2},{4,5},{5,4},{6,7},{7,6},{8,9},{9,8},{10,11... | collective-permute-start | bytes 393224 | tf_op jit(solution)/shard_map/ppermute | solution.py:401
  6.9 0.7 %copy-start.1 = (s32[16,8]{0,1:T(8,128)S(1)}, s32[16,8]{0,1:T(8,128)}, u32[]{:S(2)}) copy-start(s32[16,8]{0,1:T(8,128)} %param.4) | copy-start | bytes 1540
  17.6 6.5 %collective-permute-start.4 = (f32[264,128]{1,0:T(8,128)S(1)}, f32[264,128]{1,0:T(8,128)S(1)}, u32[]{:S(2)}, u32[]{:S(2)}) collective-permute-start(f32[264,128]{1,0:T(8,128)S(1)} %get-tuple-element.33.packed_zero), channel_id=1, source_target_pairs={{0,2},{2,0},{4,6},{6,4},{8,10},{10,8},{12,14},{14,12},{16,18},{18,... | collective-permute-start | bytes 405512 | tf_op jit(solution)/shard_map/ppermute | solution.py:388
  24.1 8.2 %collective-permute-start.5 = (f32[264,128]{1,0:T(8,128)S(1)}, f32[264,128]{1,0:T(8,128)S(1)}, u32[]{:S(2)}, u32[]{:S(2)}) collective-permute-start(f32[264,128]{1,0:T(8,128)S(1)} %add.9.packed_one), channel_id=1, source_target_pairs={{0,4},{4,0},{2,6},{6,2},{8,12},{12,8},{10,14},{14,10},{16,20},{20,... | collective-permute-start | bytes 405512 | tf_op jit(solution)/shard_map/ppermute | solution.py:388
  32.3 7.2 %collective-permute-start.6 = (f32[264,128]{1,0:T(8,128)S(1)}, f32[264,128]{1,0:T(8,128)S(1)}, u32[]{:S(2)}, u32[]{:S(2)}) collective-permute-start(f32[264,128]{1,0:T(8,128)S(1)} %add.10.refs_0_), channel_id=1, source_target_pairs={{0,8},{8,0},{2,10},{10,2},{4,12},{12,4},{6,14},{14,6},{16,24},{24,... | collective-permute-start | bytes 405512 | tf_op jit(solution)/shard_map/ppermute | solution.py:388

commit v9 on v8

--- a/solution.py
+++ b/solution.py
@@ -212,15 +212,18 @@
     tile = (batch, GROUP, LANES)
     sub = lax.broadcasted_iota(jnp.int32, tile, 1)
     lane = lax.broadcasted_iota(jnp.int32, tile, 2)
-    for p in range(first, last, PANEL):
-        ch = p // LANES
-        parts = [(a, ch), (m, ch)]
-        rows = [slice(p + GROUP * g, p + GROUP * (g + 1)) for g in range(groups)]
-        r = [[ref[:, rows[g], c * LANES : (c + 1) * LANES] for ref, c in parts] for g in range(groups)]
+
+    def panel(p, ch):
+        at = p - ch * LANES
+        parts = [(a, slice(ch * LANES, (ch + 1) * LANES)), (m, slice(ch * LANES, (ch + 1) * LANES))]
+        rows = [pl.ds(pl.multiple_of(p + GROUP * g, GROUP), GROUP) for g in range(groups)]
+        r = [[ref[:, rows[g], lanes] for ref, lanes in parts] for g in range(groups)]
+        for g in range(groups):
+            r[g][0] = turn(r[g][0], lax.rem(LANES - at, LANES))
         for g0 in range(groups):
-            at = p - ch * LANES + GROUP * g0
+            base = GROUP * g0
             v = [
-                [jnp.broadcast_to(r[g][0][:, :, at + k : at + k + 1], tile) for k in range(GROUP)]
+                [jnp.broadcast_to(r[g][0][:, :, base + k : base + k + 1], tile) for k in range(GROUP)]
                 if g >= g0
                 else None
                 for g in range(groups)
@@ -268,27 +271,39 @@
             over = invert(pivots)
             ratio = jnp.where(second_row, cross * over, 0.0)
             scale = lax.rsqrt(jnp.where(second_row, dets * over, pivots))
-            for x, (ref, c) in enumerate(parts):
+            for x, (ref, lanes) in enumerate(parts):
                 done = (top[x] - ratio * leading[x]) * scale
-                if ref is a and c == ch:
-                    done = jnp.where(lane >= sub + at, done, 0.0)
+                if x == 0:
+                    done = jnp.where(lane >= sub + (at + base), turn(done, at), 0.0)
                 r[g0][x] = done
-                ref[:, rows[g0], c * LANES : (c + 1) * LANES] = done
-        end = (ch + 1) * LANES
-        if p + PANEL == end:
-            join_chunks(a, m, ch)
-            continue
+                ref[:, rows[g0], lanes] = done
         for b in range(batch):
-            panel = jnp.concatenate(
+            wide = jnp.concatenate(
                 [jnp.concatenate([r[g][x][b] for g in range(groups)], axis=0) for x in range(len(parts))], axis=1
             )
-            high, low = split_two(panel)
+            high, low = split_two(wide)
             left = jnp.concatenate([high[:, :LANES], high[:, :LANES], low[:, :LANES]], axis=0)
             right = jnp.concatenate([high, low, high], axis=0)
-            update = dot(left, right, TN)[p + PANEL - ch * LANES :, :]
-            for x, (ref, e) in enumerate(parts):
-                lanes = slice(e * LANES, (e + 1) * LANES)
-                ref[b, p + PANEL : end, lanes] = ref[b, p + PANEL : end, lanes] - update[:, x * LANES : (x + 1) * LANES]
+            update = dot(left, right, TN)
+            below = lax.broadcasted_iota(jnp.int32, (LANES, LANES), 0) >= at + PANEL
+            for x, (ref, lanes) in enumerate(parts):
+                rest = ref[b, lanes, lanes]
+                ref[b, lanes, lanes] = rest - jnp.where(below, update[:, x * LANES : (x + 1) * LANES], 0.0)
+
+    for ch in range(first // LANES, -(-last // LANES)):
+        start, stop = max(first, ch * LANES), min(last, (ch + 1) * LANES)
+
+        def step(i, carry, start=start, ch=ch):
+            panel(pl.multiple_of(start + i * PANEL, PANEL), ch)
+            return carry
+
+        lax.fori_loop(0, (stop - start) // PANEL, step, 0)
+        if stop == (ch + 1) * LANES:
+            join_chunks(a, m, ch)
+
+
+def turn(x, shift):
+    return pltpu.roll(x.reshape(-1, x.shape[-1]), shift, 1).reshape(x.shape)
 
 
 def join_chunks(a, m, ch):

time: 50.9 us -> 54.2 us (1.065)
  Pallas kernels: 33.3 us -> 36.7 us
    pallas_call x1, Pallas kernels: 11.1 us -> 12.8 us  [shards(): pl.pallas_call(functools.partial(tree_kernel, 1.0 / math.sqrt(2 ** LEVELS...]
    pallas_call x1, Pallas kernels: 6.03 us -> 6.99 us  [shards(): pl.pallas_call(functools.partial(first_kernel, split_row), in_specs=[whol...]
    pallas_call x1, Pallas kernels: 5.56 us -> 6.3 us  [shards(): pl.pallas_call(functools.partial(second_kernel, split_row, math.sqrt(row_...]
  transfers between devices with their start and end apart: 7 -> 7, of which waited for: 2 -> 2; matrix products, arithmetic and copies ran while one was open for 0% -> 0% of each run, Pallas kernels for 35% -> 36%
where the time goes in v9:
time: 54.2 us; the launch traced here: 54 us
  Pallas kernels  36.7 us (68%)
  starting transfers between devices  13.4 us (25%)
  local copies, waits for them, and re-layouts  1.73 us (3%)
  waiting for transfers between devices  1.32 us (2%)
  between operations  0.73 us (1%)
    pallas_call x1, Pallas kernels, shards(): pl.pallas_call(functools.partial(tree_kernel, 1.0 / math.sqrt(2 ** LEVELS...  12.8 us
    ppermute x3, starting transfers between devices, from_partner(): return lax.ppermute(block, axis, route)  9.31 us
    pallas_call x1, Pallas kernels, shards(): pl.pallas_call(functools.partial(first_kernel, split_row), in_specs=[whol...  6.99 us
    pallas_call x1, Pallas kernels, shards(): pl.pallas_call(functools.partial(second_kernel, split_row, math.sqrt(row_...  6.3 us
    pallas_call x1, Pallas kernels, shards(): pl.pallas_call(own_kernel, in_specs=[smem, smem, hbm] + [whole()] * 3, ou...  6.06 us
    pallas_call x1, Pallas kernels, shards(): pl.pallas_call(functools.partial(others_kernel, parts), in_specs=[smem, s...  3.92 us
    ppermute x2, starting transfers between devices, sample_shift(): lax.ppermute(block, 'samp', [(i, (i - d) % count) for i in range(count)])  2.88 us
    unnamed x4, local copies, waits for them, and re-layouts  1.73 us
  transfers between devices with their start and end apart: 7, of which 2 were waited for; matrix products, arithmetic and copies ran while one was open for 0% of the time, Pallas kernels for 36%

profile of v9, /device:TPU:0, one launch (start us, length us, event | category | flops | bytes accessed | tf_op | source)
XLA Modules:
  0.0 54.0 jit_solution(16415804206659384834)
XLA Ops:
  0.6 0.1 pad_add_fusion.1.at
  0.7 0.0 copy-start
  0.7 1.0 %copy-done = bf16[128,2048]{1,0:T(8,128)(2,1)S(1)} copy-done((bf16[128,2048]{1,0:T(8,128)(2,1)S(1)}, bf16[128,2048]{1,0:T(8,128)(2,1)}, u32[]{:S(2)}) %copy-start) | copy-done | bytes 524312
  1.8 0.7 %prepare.1 = (bf16[128,2048]{1,0:T(8,128)(2,1)S(1)}, bf16[128,512]{1,0:T(8,128)(2,1)S(1)}, bf16[128,512]{1,0:T(8,128)(2,1)S(1)}) custom-call(s32[2]{0:T(128)S(1)} %pad_add_fusion.1.at, bf16[128,2048]{1,0:T(8,128)(2,1)S(1)} %copy-done), custom_call_target="tpu_custom_call" | custom-call | tf_op jit(solution)/shard_map/prepare/pallas_call | solution.py:437
  2.4 0.5 collective-permute-start
  2.9 0.7 %collective-permute-start.1 = (bf16[128,512]{1,0:T(8,128)(2,1)S(1)}, bf16[128,512]{1,0:T(8,128)(2,1)S(1)}, u32[]{:S(2)}, u32[]{:S(2)}) collective-permute-start(bf16[128,512]{1,0:T(8,128)(2,1)S(1)} %get-tuple-element.27), channel_id=1, source_target_pairs={{2,4},{4,2},{6,8},{8,6},{10,12},{12,10},{14,16},{16,14},{18,20},{2... | collective-permute-start | bytes 393224 | tf_op jit(solution)/shard_map/ppermute | solution.py:411
  3.6 0.3 collective-permute-done.first
  3.9 2.8 %collective-permute-start.2 = (bf16[128,512]{1,0:T(8,128)(2,1)S(1)}, bf16[128,512]{1,0:T(8,128)(2,1)S(1)}, u32[]{:S(2)}, u32[]{:S(2)}) collective-permute-start(bf16[128,512]{1,0:T(8,128)(2,1)S(1)} %collective-permute-done.first), channel_id=1, source_target_pairs={{0,1},{1,0},{2,3},{3,2},{4,5},{5,4},{6,7},{7,6},{8,9},{9,8},{10,11... | collective-permute-start | bytes 393224 | tf_op jit(solution)/shard_map/ppermute | solution.py:416
  6.8 0.0 collective-permute-done.1.second
  6.8 0.0 collective-permute-start.3
  6.8 0.1 pad_add_fusion.place
  6.9 0.0 copy-start.1
  6.9 0.7 %copy-done.1 = s32[16,8]{0,1:T(8,128)S(1)} copy-done((s32[16,8]{0,1:T(8,128)S(1)}, s32[16,8]{0,1:T(8,128)}, u32[]{:S(2)}) %copy-start.1) | copy-done | bytes 536
  7.6 6.1 %own.1 = (f32[128,2048]{1,0:T(8,128)}, bf16[16,8,128,128]{3,2,1,0:T(8,128)(2,1)S(1)}, bf16[128,2048]{1,0:T(8,128)(2,1)S(1)}, bf16[128,2048]{1,0:T(8,128)(2,1)S(1)}, f32[128,128]{1,0:T(8,128)S(1)}) custom-call(s32[2]{0:T(128)S(1)} %pad_add_fusion.place, s32[8,16]{1,0:T(8,128)S(1)} %bitcast.5, bf16[16,8,128,128]{3,2,1,0:T(8,128)(2,1)} %blocks_hbm.1, ...), custom_call_target="tpu_custom_call" | custom-call | flops 1073741824 | bytes 6291456 | tf_op jit(solution)/shard_map/own/pallas_call | solution.py:450
  13.6 0.0 collective-permute-done.2.refs_0_
  13.6 0.0 collective-permute-done.3.refs_1_
  13.6 3.9 %others.1 = (bf16[128,2048]{1,0:T(8,128)(2,1)S(1)}, bf16[128,2048]{1,0:T(8,128)(2,1)S(1)}, f32[264,128]{1,0:T(8,128)S(1)}) custom-call(s32[2]{0:T(128)S(1)} %pad_add_fusion.place, s32[8,16]{1,0:T(8,128)S(1)} %bitcast.6, bf16[16,8,128,128]{3,2,1,0:T(8,128)(2,1)S(1)} %get-tuple-element.29.blocks, bf16[128,512]{1,0:T(8,128)(2,1)S(1)} %collective-permute-done.2.refs_0_, ...), custom_call_target="tpu_custom_call" | custom-call | tf_op jit(solution)/shard_map/others/pallas_call | solution.py:476
  17.6 5.5 %collective-permute-start.4 = (f32[264,128]{1,0:T(8,128)S(1)}, f32[264,128]{1,0:T(8,128)S(1)}, u32[]{:S(2)}, u32[]{:S(2)}) collective-permute-start(f32[264,128]{1,0:T(8,128)S(1)} %get-tuple-element.33.packed_zero), channel_id=1, source_target_pairs={{0,2},{2,0},{4,6},{6,4},{8,10},{10,8},{12,14},{14,12},{16,18},{18,... | collective-permute-start | bytes 405512 | tf_op jit(solution)/shard_map/ppermute | solution.py:403
  23.1 1.0 %collective-permute-done.4 = f32[264,128]{1,0:T(8,128)S(1)} collective-permute-done((f32[264,128]{1,0:T(8,128)S(1)}, f32[264,128]{1,0:T(8,128)S(1)}, u32[]{:S(2)}, u32[]{:S(2)}) %collective-permute-start.4) | collective-permute-done | bytes 135200 | tf_op jit(solution)/shard_map/ppermute | solution.py:403
  24.1 2.2 %collective-permute-start.5 = (f32[264,128]{1,0:T(8,128)S(1)}, f32[264,128]{1,0:T(8,128)S(1)}, u32[]{:S(2)}, u32[]{:S(2)}) collective-permute-start(f32[264,128]{1,0:T(8,128)S(1)} %add.9.packed_one), channel_id=1, source_target_pairs={{0,4},{4,0},{2,6},{6,2},{8,12},{12,8},{10,14},{14,10},{16,20},{20,... | collective-permute-start | bytes 405512 | tf_op jit(solution)/shard_map/ppermute | solution.py:403
  26.3 7.0 %first.1 = (f32[2,256,256]{2,1,0:T(8,128)S(1)}, f32[2,256,256]{2,1,0:T(8,128)S(1)}) custom-call(f32[264,128]{1,0:T(8,128)S(1)} %get-tuple-element.33.packed_zero, f32[264,128]{1,0:T(8,128)S(1)} %add.9.packed_one), custom_call_target="tpu_custom_call" | custom-call | flops 3000000000 | bytes 1048576 | tf_op jit(solution)/shard_map/first/pallas_call | solution.py:491
  33.3 0.0 collective-permute-done.5
  33.3 1.6 %collective-permute-start.6 = (f32[264,128]{1,0:T(8,128)S(1)}, f32[264,128]{1,0:T(8,128)S(1)}, u32[]{:S(2)}, u32[]{:S(2)}) collective-permute-start(f32[264,128]{1,0:T(8,128)S(1)} %add.10.refs_0_), channel_id=1, source_target_pairs={{0,8},{8,0},{2,10},{10,2},{4,12},{12,4},{6,14},{14,6},{16,24},{24,... | collective-permute-start | bytes 405512 | tf_op jit(solution)/shard_map/ppermute | solution.py:403
  34.9 6.3 %second.1 = (f32[128,2048]{1,0:T(8,128)}, f32[256,128]{1,0:T(8,128)}, f32[128,256]{1,0:T(8,128)S(1)}, f32[2,256,256]{2,1,0:T(8,128)S(1)}, f32[2,256,256]{2,1,0:T(8,128)S(1)}) custom-call(s32[2]{0:T(128)S(1)} %pad_add_fusion.place, f32[264,128]{1,0:T(8,128)S(1)} %get-tuple-element.33.packed_zero, ...), custom_call_target="tpu_custom_call", output_to_operand_aliasing={{3}: (3, {}), {4}: (4, {})} | custom-call | flops 3000000000 | bytes 1048576 | tf_op jit(solution)/shard_map/second/pallas_call | solution.py:501
  41.2 0.0 collective-permute-done.6
  41.3 12.8 %tree.1 = (f32[256,128]{1,0:T(8,128)}, f32[256,128]{1,0:T(8,128)}, f32[256,128]{1,0:T(8,128)}) custom-call(s32[2]{0:T(128)S(1)} %pad_add_fusion.place, f32[128,256]{1,0:T(8,128)S(1)} %get-tuple-element.40.upper_own, f32[264,128]{1,0:T(8,128)S(1)} %add.10.refs_0_, f32[264,128]{1,0:T(8,128)S(1)} %add.11.refs_1_), custom_call_target="tpu_custom_call" | custom-call | tf_op jit(solution)/shard_map/tree/pallas_call | solution.py:511
  (3 shorter events, 0.1 us)
Async XLA Ops:
  0.7 1.0 %copy-start = (bf16[128,2048]{1,0:T(8,128)(2,1)S(1)}, bf16[128,2048]{1,0:T(8,128)(2,1)}, u32[]{:S(2)}) copy-start(bf16[128,2048]{1,0:T(8,128)(2,1)} %samples.1) | copy-start | bytes 1572868
  2.4 1.5 %collective-permute-start = (bf16[128,512]{1,0:T(8,128)(2,1)S(1)}, bf16[128,512]{1,0:T(8,128)(2,1)S(1)}, u32[]{:S(2)}, u32[]{:S(2)}) collective-permute-start(bf16[128,512]{1,0:T(8,128)(2,1)S(1)} %get-tuple-element.26), channel_id=1, source_target_pairs={{0,2},{2,0},{4,6},{6,4},{8,10},{10,8},{12,14},{14,12},{16,18},{18,... | collective-permute-start | bytes 393224 | tf_op jit(solution)/shard_map/ppermute | solution.py:411
  2.9 3.8 %collective-permute-start.1 = (bf16[128,512]{1,0:T(8,128)(2,1)S(1)}, bf16[128,512]{1,0:T(8,128)(2,1)S(1)}, u32[]{:S(2)}, u32[]{:S(2)}) collective-permute-start(bf16[128,512]{1,0:T(8,128)(2,1)S(1)} %get-tuple-element.27), channel_id=1, source_target_pairs={{2,4},{4,2},{6,8},{8,6},{10,12},{12,10},{14,16},{16,14},{18,20},{2... | collective-permute-start | bytes 393224 | tf_op jit(solution)/shard_map/ppermute | solution.py:411
  3.9 9.7 %collective-permute-start.2 = (bf16[128,512]{1,0:T(8,128)(2,1)S(1)}, bf16[128,512]{1,0:T(8,128)(2,1)S(1)}, u32[]{:S(2)}, u32[]{:S(2)}) collective-permute-start(bf16[128,512]{1,0:T(8,128)(2,1)S(1)} %collective-permute-done.first), channel_id=1, source_target_pairs={{0,1},{1,0},{2,3},{3,2},{4,5},{5,4},{6,7},{7,6},{8,9},{9,8},{10,11... | collective-permute-start | bytes 393224 | tf_op jit(solution)/shard_map/ppermute | solution.py:416
  6.8 6.9 %collective-permute-start.3 = (bf16[128,512]{1,0:T(8,128)(2,1)S(1)}, bf16[128,512]{1,0:T(8,128)(2,1)S(1)}, u32[]{:S(2)}, u32[]{:S(2)}) collective-permute-start(bf16[128,512]{1,0:T(8,128)(2,1)S(1)} %collective-permute-done.1.second), channel_id=1, source_target_pairs={{0,1},{1,0},{2,3},{3,2},{4,5},{5,4},{6,7},{7,6},{8,9},{9,8},{10,11... | collective-permute-start | bytes 393224 | tf_op jit(solution)/shard_map/ppermute | solution.py:416
  6.9 0.7 %copy-start.1 = (s32[16,8]{0,1:T(8,128)S(1)}, s32[16,8]{0,1:T(8,128)}, u32[]{:S(2)}) copy-start(s32[16,8]{0,1:T(8,128)} %param.4) | copy-start | bytes 1540
  17.6 6.5 %collective-permute-start.4 = (f32[264,128]{1,0:T(8,128)S(1)}, f32[264,128]{1,0:T(8,128)S(1)}, u32[]{:S(2)}, u32[]{:S(2)}) collective-permute-start(f32[264,128]{1,0:T(8,128)S(1)} %get-tuple-element.33.packed_zero), channel_id=1, source_target_pairs={{0,2},{2,0},{4,6},{6,4},{8,10},{10,8},{12,14},{14,12},{16,18},{18,... | collective-permute-start | bytes 405512 | tf_op jit(solution)/shard_map/ppermute | solution.py:403
  24.1 9.2 %collective-permute-start.5 = (f32[264,128]{1,0:T(8,128)S(1)}, f32[264,128]{1,0:T(8,128)S(1)}, u32[]{:S(2)}, u32[]{:S(2)}) collective-permute-start(f32[264,128]{1,0:T(8,128)S(1)} %add.9.packed_one), channel_id=1, source_target_pairs={{0,4},{4,0},{2,6},{6,2},{8,12},{12,8},{10,14},{14,10},{16,20},{20,... | collective-permute-start | bytes 405512 | tf_op jit(solution)/shard_map/ppermute | solution.py:403
  33.3 7.9 %collective-permute-start.6 = (f32[264,128]{1,0:T(8,128)S(1)}, f32[264,128]{1,0:T(8,128)S(1)}, u32[]{:S(2)}, u32[]{:S(2)}) collective-permute-start(f32[264,128]{1,0:T(8,128)S(1)} %add.10.refs_0_), channel_id=1, source_target_pairs={{0,8},{8,0},{2,10},{10,2},{4,12},{12,4},{6,14},{14,6},{16,24},{24,... | collective-permute-start | bytes 405512 | tf_op jit(solution)/shard_map/ppermute | solution.py:403

commit v10 on v8

--- a/solution.py
+++ b/solution.py
@@ -12,7 +12,7 @@
 LEVELS = 3
 LANES = 128
 GROUP = 8
-PANEL = 32
+PANEL = 16
 FIRST_EIGHTHS = 5
 ROWS_A_STEP = 4
 VMEM_LIMIT = 20 * 1024 * 1024

time: 50.9 us -> 52.7 us (1.035)
  Pallas kernels: 33.3 us -> 35.1 us
    pallas_call x1, Pallas kernels: 11.1 us -> 12 us  [shards(): pl.pallas_call(functools.partial(tree_kernel, 1.0 / math.sqrt(2 ** LEVELS...]
    pallas_call x1, Pallas kernels: 6.03 us -> 6.6 us  [shards(): pl.pallas_call(functools.partial(first_kernel, split_row), in_specs=[whol...]
where the time goes in v10:
time: 52.7 us; the launch traced here: 52.5 us
  Pallas kernels  35.1 us (67%)
  starting transfers between devices  13.4 us (25%)
  local copies, waits for them, and re-layouts  1.73 us (3%)
  waiting for transfers between devices  1.32 us (3%)
  between operations  0.73 us (1%)
    pallas_call x1, Pallas kernels, shards(): pl.pallas_call(functools.partial(tree_kernel, 1.0 / math.sqrt(2 ** LEVELS...  12 us
    ppermute x3, starting transfers between devices, from_partner(): return lax.ppermute(block, axis, route)  9.31 us
    pallas_call x1, Pallas kernels, shards(): pl.pallas_call(functools.partial(first_kernel, split_row), in_specs=[whol...  6.6 us
    pallas_call x1, Pallas kernels, shards(): pl.pallas_call(own_kernel, in_specs=[smem, smem, hbm] + [whole()] * 3, ou...  6.05 us
    pallas_call x1, Pallas kernels, shards(): pl.pallas_call(functools.partial(second_kernel, split_row, math.sqrt(row_...  5.88 us
    pallas_call x1, Pallas kernels, shards(): pl.pallas_call(functools.partial(others_kernel, parts), in_specs=[smem, s...  3.92 us
    ppermute x2, starting transfers between devices, sample_shift(): lax.ppermute(block, 'samp', [(i, (i - d) % count) for i in range(count)])  2.88 us
    unnamed x4, local copies, waits for them, and re-layouts  1.73 us
  transfers between devices with their start and end apart: 7, of which 2 were waited for; matrix products, arithmetic and copies ran while one was open for 0% of the time, Pallas kernels for 35%

profile of v10, /device:TPU:0, one launch (start us, length us, event | category | flops | bytes accessed | tf_op | source)
XLA Modules:
  0.0 52.5 jit_solution(10166117434895591767)
XLA Ops:
  0.6 0.1 pad_add_fusion.1.at
  0.7 0.0 copy-start
  0.7 1.0 %copy-done = bf16[128,2048]{1,0:T(8,128)(2,1)S(1)} copy-done((bf16[128,2048]{1,0:T(8,128)(2,1)S(1)}, bf16[128,2048]{1,0:T(8,128)(2,1)}, u32[]{:S(2)}) %copy-start) | copy-done | bytes 524312
  1.8 0.7 %prepare.1 = (bf16[128,2048]{1,0:T(8,128)(2,1)S(1)}, bf16[128,512]{1,0:T(8,128)(2,1)S(1)}, bf16[128,512]{1,0:T(8,128)(2,1)S(1)}) custom-call(s32[2]{0:T(128)S(1)} %pad_add_fusion.1.at, bf16[128,2048]{1,0:T(8,128)(2,1)S(1)} %copy-done), custom_call_target="tpu_custom_call" | custom-call | tf_op jit(solution)/shard_map/prepare/pallas_call | solution.py:422
  2.4 0.5 collective-permute-start
  2.9 0.7 %collective-permute-start.1 = (bf16[128,512]{1,0:T(8,128)(2,1)S(1)}, bf16[128,512]{1,0:T(8,128)(2,1)S(1)}, u32[]{:S(2)}, u32[]{:S(2)}) collective-permute-start(bf16[128,512]{1,0:T(8,128)(2,1)S(1)} %get-tuple-element.27), channel_id=1, source_target_pairs={{2,4},{4,2},{6,8},{8,6},{10,12},{12,10},{14,16},{16,14},{18,20},{2... | collective-permute-start | bytes 393224 | tf_op jit(solution)/shard_map/ppermute | solution.py:396
  3.6 0.3 collective-permute-done.first
  3.9 2.8 %collective-permute-start.2 = (bf16[128,512]{1,0:T(8,128)(2,1)S(1)}, bf16[128,512]{1,0:T(8,128)(2,1)S(1)}, u32[]{:S(2)}, u32[]{:S(2)}) collective-permute-start(bf16[128,512]{1,0:T(8,128)(2,1)S(1)} %collective-permute-done.first), channel_id=1, source_target_pairs={{0,1},{1,0},{2,3},{3,2},{4,5},{5,4},{6,7},{7,6},{8,9},{9,8},{10,11... | collective-permute-start | bytes 393224 | tf_op jit(solution)/shard_map/ppermute | solution.py:401
  6.8 0.0 collective-permute-done.1.second
  6.8 0.0 collective-permute-start.3
  6.8 0.1 pad_add_fusion.place
  6.9 0.0 copy-start.1
  6.9 0.7 %copy-done.1 = s32[16,8]{0,1:T(8,128)S(1)} copy-done((s32[16,8]{0,1:T(8,128)S(1)}, s32[16,8]{0,1:T(8,128)}, u32[]{:S(2)}) %copy-start.1) | copy-done | bytes 536
  7.6 6.1 %own.1 = (f32[128,2048]{1,0:T(8,128)}, bf16[16,8,128,128]{3,2,1,0:T(8,128)(2,1)S(1)}, bf16[128,2048]{1,0:T(8,128)(2,1)S(1)}, bf16[128,2048]{1,0:T(8,128)(2,1)S(1)}, f32[128,128]{1,0:T(8,128)S(1)}) custom-call(s32[2]{0:T(128)S(1)} %pad_add_fusion.place, s32[8,16]{1,0:T(8,128)S(1)} %bitcast.5, bf16[16,8,128,128]{3,2,1,0:T(8,128)(2,1)} %blocks_hbm.1, ...), custom_call_target="tpu_custom_call" | custom-call | flops 1073741824 | bytes 6291456 | tf_op jit(solution)/shard_map/own/pallas_call | solution.py:435
  13.6 0.0 collective-permute-done.2.refs_0_
  13.6 0.0 collective-permute-done.3.refs_1_
  13.6 3.9 %others.1 = (bf16[128,2048]{1,0:T(8,128)(2,1)S(1)}, bf16[128,2048]{1,0:T(8,128)(2,1)S(1)}, f32[264,128]{1,0:T(8,128)S(1)}) custom-call(s32[2]{0:T(128)S(1)} %pad_add_fusion.place, s32[8,16]{1,0:T(8,128)S(1)} %bitcast.6, bf16[16,8,128,128]{3,2,1,0:T(8,128)(2,1)S(1)} %get-tuple-element.29.blocks, bf16[128,512]{1,0:T(8,128)(2,1)S(1)} %collective-permute-done.2.refs_0_, ...), custom_call_target="tpu_custom_call" | custom-call | tf_op jit(solution)/shard_map/others/pallas_call | solution.py:461
  17.6 5.5 %collective-permute-start.4 = (f32[264,128]{1,0:T(8,128)S(1)}, f32[264,128]{1,0:T(8,128)S(1)}, u32[]{:S(2)}, u32[]{:S(2)}) collective-permute-start(f32[264,128]{1,0:T(8,128)S(1)} %get-tuple-element.33.packed_zero), channel_id=1, source_target_pairs={{0,2},{2,0},{4,6},{6,4},{8,10},{10,8},{12,14},{14,12},{16,18},{18,... | collective-permute-start | bytes 405512 | tf_op jit(solution)/shard_map/ppermute | solution.py:388
  23.1 1.0 %collective-permute-done.4 = f32[264,128]{1,0:T(8,128)S(1)} collective-permute-done((f32[264,128]{1,0:T(8,128)S(1)}, f32[264,128]{1,0:T(8,128)S(1)}, u32[]{:S(2)}, u32[]{:S(2)}) %collective-permute-start.4) | collective-permute-done | bytes 135200 | tf_op jit(solution)/shard_map/ppermute | solution.py:388
  24.1 2.2 %collective-permute-start.5 = (f32[264,128]{1,0:T(8,128)S(1)}, f32[264,128]{1,0:T(8,128)S(1)}, u32[]{:S(2)}, u32[]{:S(2)}) collective-permute-start(f32[264,128]{1,0:T(8,128)S(1)} %add.9.packed_one), channel_id=1, source_target_pairs={{0,4},{4,0},{2,6},{6,2},{8,12},{12,8},{10,14},{14,10},{16,20},{20,... | collective-permute-start | bytes 405512 | tf_op jit(solution)/shard_map/ppermute | solution.py:388
  26.3 6.6 %first.1 = (f32[2,256,256]{2,1,0:T(8,128)S(1)}, f32[2,256,256]{2,1,0:T(8,128)S(1)}) custom-call(f32[264,128]{1,0:T(8,128)S(1)} %get-tuple-element.33.packed_zero, f32[264,128]{1,0:T(8,128)S(1)} %add.9.packed_one), custom_call_target="tpu_custom_call" | custom-call | flops 3000000000 | bytes 1048576 | tf_op jit(solution)/shard_map/first/pallas_call | solution.py:476
  32.9 0.0 collective-permute-done.5
  32.9 1.6 %collective-permute-start.6 = (f32[264,128]{1,0:T(8,128)S(1)}, f32[264,128]{1,0:T(8,128)S(1)}, u32[]{:S(2)}, u32[]{:S(2)}) collective-permute-start(f32[264,128]{1,0:T(8,128)S(1)} %add.10.refs_0_), channel_id=1, source_target_pairs={{0,8},{8,0},{2,10},{10,2},{4,12},{12,4},{6,14},{14,6},{16,24},{24,... | collective-permute-start | bytes 405512 | tf_op jit(solution)/shard_map/ppermute | solution.py:388
  34.5 5.9 %second.1 = (f32[128,2048]{1,0:T(8,128)}, f32[256,128]{1,0:T(8,128)}, f32[128,256]{1,0:T(8,128)S(1)}, f32[2,256,256]{2,1,0:T(8,128)S(1)}, f32[2,256,256]{2,1,0:T(8,128)S(1)}) custom-call(s32[2]{0:T(128)S(1)} %pad_add_fusion.place, f32[264,128]{1,0:T(8,128)S(1)} %get-tuple-element.33.packed_zero, ...), custom_call_target="tpu_custom_call", output_to_operand_aliasing={{3}: (3, {}), {4}: (4, {})} | custom-call | flops 3000000000 | bytes 1048576 | tf_op jit(solution)/shard_map/second/pallas_call | solution.py:486
  40.4 0.0 collective-permute-done.6
  40.5 12.0 %tree.1 = (f32[256,128]{1,0:T(8,128)}, f32[256,128]{1,0:T(8,128)}, f32[256,128]{1,0:T(8,128)}) custom-call(s32[2]{0:T(128)S(1)} %pad_add_fusion.place, f32[128,256]{1,0:T(8,128)S(1)} %get-tuple-element.40.upper_own, f32[264,128]{1,0:T(8,128)S(1)} %add.10.refs_0_, f32[264,128]{1,0:T(8,128)S(1)} %add.11.refs_1_), custom_call_target="tpu_custom_call" | custom-call | tf_op jit(solution)/shard_map/tree/pallas_call | solution.py:496
  (3 shorter events, 0.1 us)
Async XLA Ops:
  0.7 1.0 %copy-start = (bf16[128,2048]{1,0:T(8,128)(2,1)S(1)}, bf16[128,2048]{1,0:T(8,128)(2,1)}, u32[]{:S(2)}) copy-start(bf16[128,2048]{1,0:T(8,128)(2,1)} %samples.1) | copy-start | bytes 1572868
  2.4 1.5 %collective-permute-start = (bf16[128,512]{1,0:T(8,128)(2,1)S(1)}, bf16[128,512]{1,0:T(8,128)(2,1)S(1)}, u32[]{:S(2)}, u32[]{:S(2)}) collective-permute-start(bf16[128,512]{1,0:T(8,128)(2,1)S(1)} %get-tuple-element.26), channel_id=1, source_target_pairs={{0,2},{2,0},{4,6},{6,4},{8,10},{10,8},{12,14},{14,12},{16,18},{18,... | collective-permute-start | bytes 393224 | tf_op jit(solution)/shard_map/ppermute | solution.py:396
  2.9 3.8 %collective-permute-start.1 = (bf16[128,512]{1,0:T(8,128)(2,1)S(1)}, bf16[128,512]{1,0:T(8,128)(2,1)S(1)}, u32[]{:S(2)}, u32[]{:S(2)}) collective-permute-start(bf16[128,512]{1,0:T(8,128)(2,1)S(1)} %get-tuple-element.27), channel_id=1, source_target_pairs={{2,4},{4,2},{6,8},{8,6},{10,12},{12,10},{14,16},{16,14},{18,20},{2... | collective-permute-start | bytes 393224 | tf_op jit(solution)/shard_map/ppermute | solution.py:396
  3.9 9.7 %collective-permute-start.2 = (bf16[128,512]{1,0:T(8,128)(2,1)S(1)}, bf16[128,512]{1,0:T(8,128)(2,1)S(1)}, u32[]{:S(2)}, u32[]{:S(2)}) collective-permute-start(bf16[128,512]{1,0:T(8,128)(2,1)S(1)} %collective-permute-done.first), channel_id=1, source_target_pairs={{0,1},{1,0},{2,3},{3,2},{4,5},{5,4},{6,7},{7,6},{8,9},{9,8},{10,11... | collective-permute-start | bytes 393224 | tf_op jit(solution)/shard_map/ppermute | solution.py:401
  6.8 6.9 %collective-permute-start.3 = (bf16[128,512]{1,0:T(8,128)(2,1)S(1)}, bf16[128,512]{1,0:T(8,128)(2,1)S(1)}, u32[]{:S(2)}, u32[]{:S(2)}) collective-permute-start(bf16[128,512]{1,0:T(8,128)(2,1)S(1)} %collective-permute-done.1.second), channel_id=1, source_target_pairs={{0,1},{1,0},{2,3},{3,2},{4,5},{5,4},{6,7},{7,6},{8,9},{9,8},{10,11... | collective-permute-start | bytes 393224 | tf_op jit(solution)/shard_map/ppermute | solution.py:401
  6.9 0.7 %copy-start.1 = (s32[16,8]{0,1:T(8,128)S(1)}, s32[16,8]{0,1:T(8,128)}, u32[]{:S(2)}) copy-start(s32[16,8]{0,1:T(8,128)} %param.4) | copy-start | bytes 1540
  17.6 6.5 %collective-permute-start.4 = (f32[264,128]{1,0:T(8,128)S(1)}, f32[264,128]{1,0:T(8,128)S(1)}, u32[]{:S(2)}, u32[]{:S(2)}) collective-permute-start(f32[264,128]{1,0:T(8,128)S(1)} %get-tuple-element.33.packed_zero), channel_id=1, source_target_pairs={{0,2},{2,0},{4,6},{6,4},{8,10},{10,8},{12,14},{14,12},{16,18},{18,... | collective-permute-start | bytes 405512 | tf_op jit(solution)/shard_map/ppermute | solution.py:388
  24.1 8.8 %collective-permute-start.5 = (f32[264,128]{1,0:T(8,128)S(1)}, f32[264,128]{1,0:T(8,128)S(1)}, u32[]{:S(2)}, u32[]{:S(2)}) collective-permute-start(f32[264,128]{1,0:T(8,128)S(1)} %add.9.packed_one), channel_id=1, source_target_pairs={{0,4},{4,0},{2,6},{6,2},{8,12},{12,8},{10,14},{14,10},{16,20},{20,... | collective-permute-start | bytes 405512 | tf_op jit(solution)/shard_map/ppermute | solution.py:388
  32.9 7.5 %collective-permute-start.6 = (f32[264,128]{1,0:T(8,128)S(1)}, f32[264,128]{1,0:T(8,128)S(1)}, u32[]{:S(2)}, u32[]{:S(2)}) collective-permute-start(f32[264,128]{1,0:T(8,128)S(1)} %add.10.refs_0_), channel_id=1, source_target_pairs={{0,8},{8,0},{2,10},{10,2},{4,12},{12,4},{6,14},{14,6},{16,24},{24,... | collective-permute-start | bytes 405512 | tf_op jit(solution)/shard_map/ppermute | solution.py:388

commit v11 on v10

--- a/solution.py
+++ b/solution.py
@@ -212,18 +212,24 @@
     tile = (batch, GROUP, LANES)
     sub = lax.broadcasted_iota(jnp.int32, tile, 1)
     lane = lax.broadcasted_iota(jnp.int32, tile, 2)
+    carried = None
     for p in range(first, last, PANEL):
         ch = p // LANES
+        end = (ch + 1) * LANES
         parts = [(a, ch), (m, ch)]
-        rows = [slice(p + GROUP * g, p + GROUP * (g + 1)) for g in range(groups)]
-        r = [[ref[:, rows[g], c * LANES : (c + 1) * LANES] for ref, c in parts] for g in range(groups)]
+        ahead = GROUP if p + PANEL < end else 0
+        reached = groups + ahead // GROUP
+        rows = [slice(p + GROUP * g, p + GROUP * (g + 1)) for g in range(reached)]
+        r = [[ref[:, rows[g], c * LANES : (c + 1) * LANES] for ref, c in parts] for g in range(reached)]
+        if carried is not None:
+            r[0] = carried
         for g0 in range(groups):
             at = p - ch * LANES + GROUP * g0
             v = [
                 [jnp.broadcast_to(r[g][0][:, :, at + k : at + k + 1], tile) for k in range(GROUP)]
                 if g >= g0
                 else None
-                for g in range(groups)
+                for g in range(reached)
             ]
             head, top = v[g0], r[g0]
             steps, leading = [], [None] * len(top)
@@ -256,7 +262,7 @@
                         head[k] = head[k] - w0 * v_rows[k][0] - w1 * v_rows[k][1]
                     for x in range(len(top)):
                         top[x] = top[x] - w0 * r_rows[x][0] - w1 * r_rows[x][1]
-            for g in range(g0 + 1, groups):
+            for g in range(g0 + 1, reached):
                 for j, q00, q10, q11, v_rows, r_rows in steps:
                     c0, c1 = v[g][j], v[g][j + 1]
                     w0, w1 = c0 * q00 - c1 * q10, c1 * q11 - c0 * q10
@@ -274,10 +280,14 @@
                     done = jnp.where(lane >= sub + at, done, 0.0)
                 r[g0][x] = done
                 ref[:, rows[g0], c * LANES : (c + 1) * LANES] = done
-        end = (ch + 1) * LANES
+        carried = None
         if p + PANEL == end:
             join_chunks(a, m, ch)
             continue
+        carried = r[groups]
+        if p + PANEL >= last:
+            for x, (ref, c) in enumerate(parts):
+                ref[:, rows[groups], c * LANES : (c + 1) * LANES] = carried[x]
         for b in range(batch):
             panel = jnp.concatenate(
                 [jnp.concatenate([r[g][x][b] for g in range(groups)], axis=0) for x in range(len(parts))], axis=1
@@ -285,10 +295,13 @@
             high, low = split_two(panel)
             left = jnp.concatenate([high[:, :LANES], high[:, :LANES], low[:, :LANES]], axis=0)
             right = jnp.concatenate([high, low, high], axis=0)
-            update = dot(left, right, TN)[p + PANEL - ch * LANES :, :]
+            start = p + PANEL + ahead
+            if start == end:
+                continue
+            update = dot(left, right, TN)[start - ch * LANES :, :]
             for x, (ref, e) in enumerate(parts):
                 lanes = slice(e * LANES, (e + 1) * LANES)
-                ref[b, p + PANEL : end, lanes] = ref[b, p + PANEL : end, lanes] - update[:, x * LANES : (x + 1) * LANES]
+                ref[b, start:end, lanes] = ref[b, start:end, lanes] - update[:, x * LANES : (x + 1) * LANES]
 
 
 def join_chunks(a, m, ch):

time: 52.7 us -> 52.1 us (0.989)
  no operation moved by 1% of the time
where the time goes in v11:
time: 52.1 us; the launch traced here: 51.9 us
  Pallas kernels  34.6 us (66%)
  starting transfers between devices  13.4 us (26%)
  local copies, waits for them, and re-layouts  1.73 us (3%)
  waiting for transfers between devices  1.32 us (3%)
  between operations  0.73 us (1%)
    pallas_call x1, Pallas kernels, shards(): pl.pallas_call(functools.partial(tree_kernel, 1.0 / math.sqrt(2 ** LEVELS...  11.7 us
    ppermute x3, starting transfers between devices, from_partner(): return lax.ppermute(block, axis, route)  9.31 us
    pallas_call x1, Pallas kernels, shards(): pl.pallas_call(functools.partial(first_kernel, split_row), in_specs=[whol...  6.49 us
    pallas_call x1, Pallas kernels, shards(): pl.pallas_call(own_kernel, in_specs=[smem, smem, hbm] + [whole()] * 3, ou...  6.06 us
    pallas_call x1, Pallas kernels, shards(): pl.pallas_call(functools.partial(second_kernel, split_row, math.sqrt(row_...  5.8 us
    pallas_call x1, Pallas kernels, shards(): pl.pallas_call(functools.partial(others_kernel, parts), in_specs=[smem, s...  3.92 us
    ppermute x2, starting transfers between devices, sample_shift(): lax.ppermute(block, 'samp', [(i, (i - d) % count) for i in range(count)])  2.88 us
    unnamed x4, local copies, waits for them, and re-layouts  1.73 us
  transfers between devices with their start and end apart: 7, of which 2 were waited for; matrix products, arithmetic and copies ran while one was open for 0% of the time, Pallas kernels for 35%

profile of v11, /device:TPU:0, one launch (start us, length us, event | category | flops | bytes accessed | tf_op | source)
XLA Modules:
  0.0 51.9 jit_solution(7910900420692704781)
XLA Ops:
  0.6 0.1 pad_add_fusion.1.at
  0.7 0.0 copy-start
  0.7 1.0 %copy-done = bf16[128,2048]{1,0:T(8,128)(2,1)S(1)} copy-done((bf16[128,2048]{1,0:T(8,128)(2,1)S(1)}, bf16[128,2048]{1,0:T(8,128)(2,1)}, u32[]{:S(2)}) %copy-start) | copy-done | bytes 524312
  1.8 0.7 %prepare.1 = (bf16[128,2048]{1,0:T(8,128)(2,1)S(1)}, bf16[128,512]{1,0:T(8,128)(2,1)S(1)}, bf16[128,512]{1,0:T(8,128)(2,1)S(1)}) custom-call(s32[2]{0:T(128)S(1)} %pad_add_fusion.1.at, bf16[128,2048]{1,0:T(8,128)(2,1)S(1)} %copy-done), custom_call_target="tpu_custom_call" | custom-call | tf_op jit(solution)/shard_map/prepare/pallas_call | solution.py:435
  2.4 0.5 collective-permute-start
  2.9 0.7 %collective-permute-start.1 = (bf16[128,512]{1,0:T(8,128)(2,1)S(1)}, bf16[128,512]{1,0:T(8,128)(2,1)S(1)}, u32[]{:S(2)}, u32[]{:S(2)}) collective-permute-start(bf16[128,512]{1,0:T(8,128)(2,1)S(1)} %get-tuple-element.27), channel_id=1, source_target_pairs={{2,4},{4,2},{6,8},{8,6},{10,12},{12,10},{14,16},{16,14},{18,20},{2... | collective-permute-start | bytes 393224 | tf_op jit(solution)/shard_map/ppermute | solution.py:409
  3.6 0.3 collective-permute-done.first
  3.9 2.8 %collective-permute-start.2 = (bf16[128,512]{1,0:T(8,128)(2,1)S(1)}, bf16[128,512]{1,0:T(8,128)(2,1)S(1)}, u32[]{:S(2)}, u32[]{:S(2)}) collective-permute-start(bf16[128,512]{1,0:T(8,128)(2,1)S(1)} %collective-permute-done.first), channel_id=1, source_target_pairs={{0,1},{1,0},{2,3},{3,2},{4,5},{5,4},{6,7},{7,6},{8,9},{9,8},{10,11... | collective-permute-start | bytes 393224 | tf_op jit(solution)/shard_map/ppermute | solution.py:414
  6.8 0.0 collective-permute-done.1.second
  6.8 0.0 collective-permute-start.3
  6.8 0.1 pad_add_fusion.place
  6.9 0.0 copy-start.1
  6.9 0.7 %copy-done.1 = s32[16,8]{0,1:T(8,128)S(1)} copy-done((s32[16,8]{0,1:T(8,128)S(1)}, s32[16,8]{0,1:T(8,128)}, u32[]{:S(2)}) %copy-start.1) | copy-done | bytes 536
  7.6 6.1 %own.1 = (f32[128,2048]{1,0:T(8,128)}, bf16[16,8,128,128]{3,2,1,0:T(8,128)(2,1)S(1)}, bf16[128,2048]{1,0:T(8,128)(2,1)S(1)}, bf16[128,2048]{1,0:T(8,128)(2,1)S(1)}, f32[128,128]{1,0:T(8,128)S(1)}) custom-call(s32[2]{0:T(128)S(1)} %pad_add_fusion.place, s32[8,16]{1,0:T(8,128)S(1)} %bitcast.5, bf16[16,8,128,128]{3,2,1,0:T(8,128)(2,1)} %blocks_hbm.1, ...), custom_call_target="tpu_custom_call" | custom-call | flops 1073741824 | bytes 6291456 | tf_op jit(solution)/shard_map/own/pallas_call | solution.py:448
  13.6 0.0 collective-permute-done.2.refs_0_
  13.6 0.0 collective-permute-done.3.refs_1_
  13.7 3.9 %others.1 = (bf16[128,2048]{1,0:T(8,128)(2,1)S(1)}, bf16[128,2048]{1,0:T(8,128)(2,1)S(1)}, f32[264,128]{1,0:T(8,128)S(1)}) custom-call(s32[2]{0:T(128)S(1)} %pad_add_fusion.place, s32[8,16]{1,0:T(8,128)S(1)} %bitcast.6, bf16[16,8,128,128]{3,2,1,0:T(8,128)(2,1)S(1)} %get-tuple-element.29.blocks, bf16[128,512]{1,0:T(8,128)(2,1)S(1)} %collective-permute-done.2.refs_0_, ...), custom_call_target="tpu_custom_call" | custom-call | tf_op jit(solution)/shard_map/others/pallas_call | solution.py:474
  17.6 5.5 %collective-permute-start.4 = (f32[264,128]{1,0:T(8,128)S(1)}, f32[264,128]{1,0:T(8,128)S(1)}, u32[]{:S(2)}, u32[]{:S(2)}) collective-permute-start(f32[264,128]{1,0:T(8,128)S(1)} %get-tuple-element.33.packed_zero), channel_id=1, source_target_pairs={{0,2},{2,0},{4,6},{6,4},{8,10},{10,8},{12,14},{14,12},{16,18},{18,... | collective-permute-start | bytes 405512 | tf_op jit(solution)/shard_map/ppermute | solution.py:401
  23.0 1.0 %collective-permute-done.4 = f32[264,128]{1,0:T(8,128)S(1)} collective-permute-done((f32[264,128]{1,0:T(8,128)S(1)}, f32[264,128]{1,0:T(8,128)S(1)}, u32[]{:S(2)}, u32[]{:S(2)}) %collective-permute-start.4) | collective-permute-done | bytes 135200 | tf_op jit(solution)/shard_map/ppermute | solution.py:401
  24.1 2.2 %collective-permute-start.5 = (f32[264,128]{1,0:T(8,128)S(1)}, f32[264,128]{1,0:T(8,128)S(1)}, u32[]{:S(2)}, u32[]{:S(2)}) collective-permute-start(f32[264,128]{1,0:T(8,128)S(1)} %add.9.packed_one), channel_id=1, source_target_pairs={{0,4},{4,0},{2,6},{6,2},{8,12},{12,8},{10,14},{14,10},{16,20},{20,... | collective-permute-start | bytes 405512 | tf_op jit(solution)/shard_map/ppermute | solution.py:401
  26.3 6.5 %first.1 = (f32[2,256,256]{2,1,0:T(8,128)S(1)}, f32[2,256,256]{2,1,0:T(8,128)S(1)}) custom-call(f32[264,128]{1,0:T(8,128)S(1)} %get-tuple-element.33.packed_zero, f32[264,128]{1,0:T(8,128)S(1)} %add.9.packed_one), custom_call_target="tpu_custom_call" | custom-call | flops 3000000000 | bytes 1048576 | tf_op jit(solution)/shard_map/first/pallas_call | solution.py:489
  32.8 0.0 collective-permute-done.5
  32.8 1.6 %collective-permute-start.6 = (f32[264,128]{1,0:T(8,128)S(1)}, f32[264,128]{1,0:T(8,128)S(1)}, u32[]{:S(2)}, u32[]{:S(2)}) collective-permute-start(f32[264,128]{1,0:T(8,128)S(1)} %add.10.refs_0_), channel_id=1, source_target_pairs={{0,8},{8,0},{2,10},{10,2},{4,12},{12,4},{6,14},{14,6},{16,24},{24,... | collective-permute-start | bytes 405512 | tf_op jit(solution)/shard_map/ppermute | solution.py:401
  34.4 5.8 %second.1 = (f32[128,2048]{1,0:T(8,128)}, f32[256,128]{1,0:T(8,128)}, f32[128,256]{1,0:T(8,128)S(1)}, f32[2,256,256]{2,1,0:T(8,128)S(1)}, f32[2,256,256]{2,1,0:T(8,128)S(1)}) custom-call(s32[2]{0:T(128)S(1)} %pad_add_fusion.place, f32[264,128]{1,0:T(8,128)S(1)} %get-tuple-element.33.packed_zero, ...), custom_call_target="tpu_custom_call", output_to_operand_aliasing={{3}: (3, {}), {4}: (4, {})} | custom-call | flops 3000000000 | bytes 1048576 | tf_op jit(solution)/shard_map/second/pallas_call | solution.py:499
  40.2 0.0 collective-permute-done.6
  40.3 11.7 %tree.1 = (f32[256,128]{1,0:T(8,128)}, f32[256,128]{1,0:T(8,128)}, f32[256,128]{1,0:T(8,128)}) custom-call(s32[2]{0:T(128)S(1)} %pad_add_fusion.place, f32[128,256]{1,0:T(8,128)S(1)} %get-tuple-element.40.upper_own, f32[264,128]{1,0:T(8,128)S(1)} %add.10.refs_0_, f32[264,128]{1,0:T(8,128)S(1)} %add.11.refs_1_), custom_call_target="tpu_custom_call" | custom-call | tf_op jit(solution)/shard_map/tree/pallas_call | solution.py:509
  (3 shorter events, 0.1 us)
Async XLA Ops:
  0.7 1.0 %copy-start = (bf16[128,2048]{1,0:T(8,128)(2,1)S(1)}, bf16[128,2048]{1,0:T(8,128)(2,1)}, u32[]{:S(2)}) copy-start(bf16[128,2048]{1,0:T(8,128)(2,1)} %samples.1) | copy-start | bytes 1572868
  2.4 1.5 %collective-permute-start = (bf16[128,512]{1,0:T(8,128)(2,1)S(1)}, bf16[128,512]{1,0:T(8,128)(2,1)S(1)}, u32[]{:S(2)}, u32[]{:S(2)}) collective-permute-start(bf16[128,512]{1,0:T(8,128)(2,1)S(1)} %get-tuple-element.26), channel_id=1, source_target_pairs={{0,2},{2,0},{4,6},{6,4},{8,10},{10,8},{12,14},{14,12},{16,18},{18,... | collective-permute-start | bytes 393224 | tf_op jit(solution)/shard_map/ppermute | solution.py:409
  2.9 3.8 %collective-permute-start.1 = (bf16[128,512]{1,0:T(8,128)(2,1)S(1)}, bf16[128,512]{1,0:T(8,128)(2,1)S(1)}, u32[]{:S(2)}, u32[]{:S(2)}) collective-permute-start(bf16[128,512]{1,0:T(8,128)(2,1)S(1)} %get-tuple-element.27), channel_id=1, source_target_pairs={{2,4},{4,2},{6,8},{8,6},{10,12},{12,10},{14,16},{16,14},{18,20},{2... | collective-permute-start | bytes 393224 | tf_op jit(solution)/shard_map/ppermute | solution.py:409
  3.9 9.7 %collective-permute-start.2 = (bf16[128,512]{1,0:T(8,128)(2,1)S(1)}, bf16[128,512]{1,0:T(8,128)(2,1)S(1)}, u32[]{:S(2)}, u32[]{:S(2)}) collective-permute-start(bf16[128,512]{1,0:T(8,128)(2,1)S(1)} %collective-permute-done.first), channel_id=1, source_target_pairs={{0,1},{1,0},{2,3},{3,2},{4,5},{5,4},{6,7},{7,6},{8,9},{9,8},{10,11... | collective-permute-start | bytes 393224 | tf_op jit(solution)/shard_map/ppermute | solution.py:414
  6.8 6.9 %collective-permute-start.3 = (bf16[128,512]{1,0:T(8,128)(2,1)S(1)}, bf16[128,512]{1,0:T(8,128)(2,1)S(1)}, u32[]{:S(2)}, u32[]{:S(2)}) collective-permute-start(bf16[128,512]{1,0:T(8,128)(2,1)S(1)} %collective-permute-done.1.second), channel_id=1, source_target_pairs={{0,1},{1,0},{2,3},{3,2},{4,5},{5,4},{6,7},{7,6},{8,9},{9,8},{10,11... | collective-permute-start | bytes 393224 | tf_op jit(solution)/shard_map/ppermute | solution.py:414
  6.9 0.7 %copy-start.1 = (s32[16,8]{0,1:T(8,128)S(1)}, s32[16,8]{0,1:T(8,128)}, u32[]{:S(2)}) copy-start(s32[16,8]{0,1:T(8,128)} %param.4) | copy-start | bytes 1540
  17.6 6.5 %collective-permute-start.4 = (f32[264,128]{1,0:T(8,128)S(1)}, f32[264,128]{1,0:T(8,128)S(1)}, u32[]{:S(2)}, u32[]{:S(2)}) collective-permute-start(f32[264,128]{1,0:T(8,128)S(1)} %get-tuple-element.33.packed_zero), channel_id=1, source_target_pairs={{0,2},{2,0},{4,6},{6,4},{8,10},{10,8},{12,14},{14,12},{16,18},{18,... | collective-permute-start | bytes 405512 | tf_op jit(solution)/shard_map/ppermute | solution.py:401
  24.1 8.7 %collective-permute-start.5 = (f32[264,128]{1,0:T(8,128)S(1)}, f32[264,128]{1,0:T(8,128)S(1)}, u32[]{:S(2)}, u32[]{:S(2)}) collective-permute-start(f32[264,128]{1,0:T(8,128)S(1)} %add.9.packed_one), channel_id=1, source_target_pairs={{0,4},{4,0},{2,6},{6,2},{8,12},{12,8},{10,14},{14,10},{16,20},{20,... | collective-permute-start | bytes 405512 | tf_op jit(solution)/shard_map/ppermute | solution.py:401
  32.8 7.4 %collective-permute-start.6 = (f32[264,128]{1,0:T(8,128)S(1)}, f32[264,128]{1,0:T(8,128)S(1)}, u32[]{:S(2)}, u32[]{:S(2)}) collective-permute-start(f32[264,128]{1,0:T(8,128)S(1)} %add.10.refs_0_), channel_id=1, source_target_pairs={{0,8},{8,0},{2,10},{10,2},{4,12},{12,4},{6,14},{14,6},{16,24},{24,... | collective-permute-start | bytes 405512 | tf_op jit(solution)/shard_map/ppermute | solution.py:401

commit v12 on v8

--- a/solution.py
+++ b/solution.py
@@ -328,46 +328,43 @@
     factor(a, m, 0, stop)
 
 
-def second_kernel(start, scale, place, packed_zero, packed_one, a_in, m_in, own_high, own_low, rest_high, rest_low,
-                  bases, transfer, upper_own, a, m):
+def second_kernel(start, a_in, m_in, a, m):
     del a_in, m_in
+    factor(a, m, start, a.shape[1])
+    clear_lower(a)
+
+
+def tree_kernel(
+    scale, top_scale, place, packed_zero, packed_one, packed_two, packed_three, a_low, m_low,
+    own_high, own_low, rest_high, rest_low,
+    bases, transfer_one, transfer_two, transfer_three, top, a, m, basis_rows, leaving,
+):
     n = a.shape[1]
-    factor(a, m, start, n)
-    clear_lower(a)
-    own = upper_own.shape[0]
+    own = own_high.shape[0]
     rows = own_rows(place, own)
-    size_zero, size_one = largest(packed_zero), largest(packed_one)
-    upper_own[...] = a[1, rows, :] * jnp.sqrt(size_one)
-    child = a[0, rows, :] * (jnp.sqrt(size_zero) * lax.rsqrt(size_one))
-    transfer[...] = dot_split(split_two(m[1]), split_two(child), NT)
-    turned = pltpu.roll(m[0, rows, :] * (lax.rsqrt(size_zero) * scale), lax.rem(n - place[1] * own, n), 1)
+    sizes = [largest(ref) for ref in (packed_zero, packed_one, packed_two, packed_three)]
+    turned = pltpu.roll(m_low[0, rows, :] * (lax.rsqrt(sizes[0]) * scale), lax.rem(n - place[1] * own, n), 1)
     inverse = split_two(turned)
     for c in range(0, own_high.shape[1], 512):
         lanes = slice(c, c + 512)
         high = jnp.concatenate([own_high[:, lanes], rest_high[:, lanes]], axis=0)
         low = jnp.concatenate([own_low[:, lanes], rest_low[:, lanes]], axis=0)
-        bases[:, lanes] = dot_split(inverse, (high, low), NN)
-
-
-def tree_kernel(top_scale, place, upper_own, *refs):
-    levels = (len(refs) - 3) // 2
-    packed = refs[:levels]
-    transfers = refs[levels : 2 * levels]
-    top, a, m = refs[2 * levels :]
-    for b in range(levels):
-        unpack_symmetric(packed[b], a, b)
+        basis_rows[:, lanes] = dot_split(inverse, (high, low), NN)
+    leave = pltpu.make_async_copy(basis_rows, bases, leaving)
+    leave.start()
+    unpack_symmetric(packed_two, a, 0)
+    unpack_symmetric(packed_three, a, 1)
     start_inverse(m)
-    factor(a, m, 0, a.shape[1])
+    factor(a, m, 0, n)
     clear_lower(a)
-    own = upper_own.shape[0]
-    rows = own_rows(place, own)
-    sizes = [largest(ref) for ref in packed]
-    child = upper_own[...]
-    for b in range(levels):
-        child = child * lax.rsqrt(sizes[b])
-        transfers[b][...] = dot_split(split_two(m[b]), split_two(child), NT)
-        child = a[b, rows, :] * jnp.sqrt(sizes[b])
-    top[...] = (child * top_scale).T
+    uppers = [a_low[0, rows, :], a_low[1, rows, :], a[0, rows, :], a[1, rows, :]]
+    inverses = [m_low[1], m[0], m[1]]
+    transfers = [transfer_one, transfer_two, transfer_three]
+    for b in range(LEVELS):
+        child = uppers[b] * (jnp.sqrt(sizes[b]) * lax.rsqrt(sizes[b + 1]))
+        transfers[b][...] = dot_split(split_two(inverses[b]), split_two(child), NT)
+    top[...] = (uppers[LEVELS] * (jnp.sqrt(sizes[LEVELS]) * top_scale)).T
+    leave.wait()
 
 
 def whole():
@@ -483,25 +480,26 @@
         name="first",
     )(packed, gram_one)
     gram_three = gram_two + from_partner(gram_two, "leaf", 2)
-    bases, transfer_one, upper_own, _, _ = pl.pallas_call(
-        functools.partial(second_kernel, split_row, math.sqrt(row_count)),
-        in_specs=[smem] + [whole()] * 8,
-        out_specs=[whole()] * 5,
-        out_shape=[shape((own, row_count), F32), transfer_shape, shape((own, total), F32), square, square],
-        input_output_aliases={3: 3, 4: 4},
+    a, m = pl.pallas_call(
+        functools.partial(second_kernel, split_row),
+        in_specs=[whole()] * 2,
+        out_specs=[whole()] * 2,
+        out_shape=[square] * 2,
+        input_output_aliases={0: 0, 1: 1},
         compiler_params=params(),
         cost_estimate=pl.CostEstimate(flops=3 * 10**9, bytes_accessed=1024 * 1024, transcendentals=0),
         name="second",
-    )(place, packed, gram_one, a, m, own_high, own_low, rest_high, rest_low)
-    transfer_two, transfer_three, top_factor = pl.pallas_call(
-        functools.partial(tree_kernel, 1.0 / math.sqrt(2**LEVELS * row_count)),
-        in_specs=[smem] + [whole()] * 3,
-        out_specs=[whole()] * 3,
-        out_shape=[transfer_shape] * 3,
-        scratch_shapes=[pltpu.VMEM((2, total, total), F32)] * 2,
+    )(a, m)
+    bases, transfer_one, transfer_two, transfer_three, top_factor = pl.pallas_call(
+        functools.partial(tree_kernel, math.sqrt(row_count), 1.0 / math.sqrt(2**LEVELS * row_count)),
+        in_specs=[smem] + [whole()] * 10,
+        out_specs=[hbm] + [whole()] * (LEVELS + 1),
+        out_shape=[shape((own, row_count), F32)] + [transfer_shape] * (LEVELS + 1),
+        scratch_shapes=[pltpu.VMEM((2, total, total), F32)] * 2
+        + [pltpu.VMEM((own, row_count), F32), pltpu.SemaphoreType.DMA],
         compiler_params=params(),
         name="tree",
-    )(place, upper_own, gram_two, gram_three)
+    )(place, packed, gram_one, gram_two, gram_three, a, m, own_high, own_low, rest_high, rest_low)
     return (products, bases, transfer_one, transfer_two, transfer_three, top_factor)
 
 

time: 50.9 us -> 50.3 us (0.988)
  Pallas kernels: 33.3 us -> 31.9 us
  waiting for transfers between devices: 1.32 us -> 2 us
    pallas_call x2, Pallas kernels: 16.6 us -> 15.2 us  [the longest x1 11.9 us: shards(): pl.pallas_call(functools.partial(tree_kernel, math.sqrt(row_count), 1.0 /...]
    ppermute x3, waiting for transfers between devices: 1 us -> 1.67 us  [from_partner(): return lax.ppermute(block, axis, route)]
  transfers between devices with their start and end apart: 7 -> 7, of which waited for: 2 -> 3; matrix products, arithmetic and copies ran while one was open for 0% -> 0% of each run, Pallas kernels for 35% -> 31%
where the time goes in v12:
time: 50.3 us; the launch traced here: 50.1 us
  Pallas kernels  31.9 us (63%)
  starting transfers between devices  13.4 us (27%)
  waiting for transfers between devices  2 us (4%)
  local copies, waits for them, and re-layouts  1.73 us (3%)
  between operations  0.89 us (2%)
    pallas_call x1, Pallas kernels, shards(): pl.pallas_call(functools.partial(tree_kernel, math.sqrt(row_count), 1.0 /...  11.9 us
    ppermute x3, starting transfers between devices, from_partner(): return lax.ppermute(block, axis, route)  9.33 us
    pallas_call x1, Pallas kernels, shards(): pl.pallas_call(own_kernel, in_specs=[smem, smem, hbm] + [whole()] * 3, ou...  6.04 us
    pallas_call x1, Pallas kernels, shards(): pl.pallas_call(functools.partial(first_kernel, split_row), in_specs=[whol...  6.04 us
    pallas_call x1, Pallas kernels, shards(): pl.pallas_call(functools.partial(others_kernel, parts), in_specs=[smem, s...  3.95 us
    pallas_call x1, Pallas kernels, shards(): pl.pallas_call(functools.partial(second_kernel, split_row), in_specs=[who...  3.31 us
    ppermute x2, starting transfers between devices, sample_shift(): lax.ppermute(block, 'samp', [(i, (i - d) % count) for i in range(count)])  2.88 us
    unnamed x4, local copies, waits for them, and re-layouts  1.73 us
  transfers between devices with their start and end apart: 7, of which 3 were waited for; matrix products, arithmetic and copies ran while one was open for 0% of the time, Pallas kernels for 31%

profile of v12, /device:TPU:0, one launch (start us, length us, event | category | flops | bytes accessed | tf_op | source)
XLA Modules:
  0.0 50.1 jit_solution(13984827722099990764)
XLA Ops:
  0.6 0.1 pad_add_fusion.1.at
  0.7 0.0 copy-start
  0.7 1.0 %copy-done = bf16[128,2048]{1,0:T(8,128)(2,1)S(1)} copy-done((bf16[128,2048]{1,0:T(8,128)(2,1)S(1)}, bf16[128,2048]{1,0:T(8,128)(2,1)}, u32[]{:S(2)}) %copy-start) | copy-done | bytes 524312
  1.8 0.7 %prepare.1 = (bf16[128,2048]{1,0:T(8,128)(2,1)S(1)}, bf16[128,512]{1,0:T(8,128)(2,1)S(1)}, bf16[128,512]{1,0:T(8,128)(2,1)S(1)}) custom-call(s32[2]{0:T(128)S(1)} %pad_add_fusion.1.at, bf16[128,2048]{1,0:T(8,128)(2,1)S(1)} %copy-done), custom_call_target="tpu_custom_call" | custom-call | tf_op jit(solution)/shard_map/prepare/pallas_call | solution.py:419
  2.4 0.5 %collective-permute-start = (bf16[128,512]{1,0:T(8,128)(2,1)S(1)}, bf16[128,512]{1,0:T(8,128)(2,1)S(1)}, u32[]{:S(2)}, u32[]{:S(2)}) collective-permute-start(bf16[128,512]{1,0:T(8,128)(2,1)S(1)} %get-tuple-element.27), channel_id=1, source_target_pairs={{0,2},{2,0},{4,6},{6,4},{8,10},{10,8},{12,14},{14,12},{16,18},{18,... | collective-permute-start | bytes 393224 | tf_op jit(solution)/shard_map/ppermute | solution.py:393
  2.9 0.7 %collective-permute-start.1 = (bf16[128,512]{1,0:T(8,128)(2,1)S(1)}, bf16[128,512]{1,0:T(8,128)(2,1)S(1)}, u32[]{:S(2)}, u32[]{:S(2)}) collective-permute-start(bf16[128,512]{1,0:T(8,128)(2,1)S(1)} %get-tuple-element.28), channel_id=1, source_target_pairs={{2,4},{4,2},{6,8},{8,6},{10,12},{12,10},{14,16},{16,14},{18,20},{2... | collective-permute-start | bytes 393224 | tf_op jit(solution)/shard_map/ppermute | solution.py:393
  3.6 0.3 collective-permute-done.first
  3.9 2.8 %collective-permute-start.2 = (bf16[128,512]{1,0:T(8,128)(2,1)S(1)}, bf16[128,512]{1,0:T(8,128)(2,1)S(1)}, u32[]{:S(2)}, u32[]{:S(2)}) collective-permute-start(bf16[128,512]{1,0:T(8,128)(2,1)S(1)} %collective-permute-done.first), channel_id=1, source_target_pairs={{0,1},{1,0},{2,3},{3,2},{4,5},{5,4},{6,7},{7,6},{8,9},{9,8},{10,11... | collective-permute-start | bytes 393224 | tf_op jit(solution)/shard_map/ppermute | solution.py:398
  6.8 0.0 collective-permute-done.1.second
  6.8 0.0 collective-permute-start.3
  6.8 0.1 pad_add_fusion.place
  6.9 0.0 copy-start.1
  6.9 0.7 %copy-done.1 = s32[16,8]{0,1:T(8,128)S(1)} copy-done((s32[16,8]{0,1:T(8,128)S(1)}, s32[16,8]{0,1:T(8,128)}, u32[]{:S(2)}) %copy-start.1) | copy-done | bytes 536
  7.6 6.0 %own.1 = (f32[128,2048]{1,0:T(8,128)}, bf16[16,8,128,128]{3,2,1,0:T(8,128)(2,1)S(1)}, bf16[128,2048]{1,0:T(8,128)(2,1)S(1)}, bf16[128,2048]{1,0:T(8,128)(2,1)S(1)}, f32[128,128]{1,0:T(8,128)S(1)}) custom-call(s32[2]{0:T(128)S(1)} %pad_add_fusion.place, s32[8,16]{1,0:T(8,128)S(1)} %bitcast.5, bf16[16,8,128,128]{3,2,1,0:T(8,128)(2,1)} %blocks_hbm.1, ...), custom_call_target="tpu_custom_call" | custom-call | flops 1073741824 | bytes 6291456 | tf_op jit(solution)/shard_map/own/pallas_call | solution.py:432
  13.6 0.0 collective-permute-done.2.refs_0_
  13.6 0.0 collective-permute-done.3.refs_1_
  13.6 3.9 %others.1 = (bf16[128,2048]{1,0:T(8,128)(2,1)S(1)}, bf16[128,2048]{1,0:T(8,128)(2,1)S(1)}, f32[264,128]{1,0:T(8,128)S(1)}) custom-call(s32[2]{0:T(128)S(1)} %pad_add_fusion.place, s32[8,16]{1,0:T(8,128)S(1)} %bitcast.6, bf16[16,8,128,128]{3,2,1,0:T(8,128)(2,1)S(1)} %get-tuple-element.30.blocks, bf16[128,512]{1,0:T(8,128)(2,1)S(1)} %collective-permute-done.2.refs_0_, ...), custom_call_target="tpu_custom_call" | custom-call | tf_op jit(solution)/shard_map/others/pallas_call | solution.py:458
  17.6 5.5 %collective-permute-start.4 = (f32[264,128]{1,0:T(8,128)S(1)}, f32[264,128]{1,0:T(8,128)S(1)}, u32[]{:S(2)}, u32[]{:S(2)}) collective-permute-start(f32[264,128]{1,0:T(8,128)S(1)} %get-tuple-element.34.packed_zero), channel_id=1, source_target_pairs={{0,2},{2,0},{4,6},{6,4},{8,10},{10,8},{12,14},{14,12},{16,18},{18,... | collective-permute-start | bytes 405512 | tf_op jit(solution)/shard_map/ppermute | solution.py:385
  23.1 1.0 %collective-permute-done.4 = f32[264,128]{1,0:T(8,128)S(1)} collective-permute-done((f32[264,128]{1,0:T(8,128)S(1)}, f32[264,128]{1,0:T(8,128)S(1)}, u32[]{:S(2)}, u32[]{:S(2)}) %collective-permute-start.4) | collective-permute-done | bytes 135200 | tf_op jit(solution)/shard_map/ppermute | solution.py:385
  24.1 2.2 %collective-permute-start.5 = (f32[264,128]{1,0:T(8,128)S(1)}, f32[264,128]{1,0:T(8,128)S(1)}, u32[]{:S(2)}, u32[]{:S(2)}) collective-permute-start(f32[264,128]{1,0:T(8,128)S(1)} %add.9.packed_one), channel_id=1, source_target_pairs={{0,4},{4,0},{2,6},{6,2},{8,12},{12,8},{10,14},{14,10},{16,20},{20,... | collective-permute-start | bytes 405512 | tf_op jit(solution)/shard_map/ppermute | solution.py:385
  26.3 6.0 %first.1 = (f32[2,256,256]{2,1,0:T(8,128)S(1)}, f32[2,256,256]{2,1,0:T(8,128)S(1)}) custom-call(f32[264,128]{1,0:T(8,128)S(1)} %get-tuple-element.34.packed_zero, f32[264,128]{1,0:T(8,128)S(1)} %add.9.packed_one), custom_call_target="tpu_custom_call" | custom-call | flops 3000000000 | bytes 1048576 | tf_op jit(solution)/shard_map/first/pallas_call | solution.py:473
  32.3 0.0 collective-permute-done.5
  32.4 1.6 %collective-permute-start.6 = (f32[264,128]{1,0:T(8,128)S(1)}, f32[264,128]{1,0:T(8,128)S(1)}, u32[]{:S(2)}, u32[]{:S(2)}) collective-permute-start(f32[264,128]{1,0:T(8,128)S(1)} %add.10.packed_two), channel_id=1, source_target_pairs={{0,8},{8,0},{2,10},{10,2},{4,12},{12,4},{6,14},{14,6},{16,24},{24,... | collective-permute-start | bytes 405512 | tf_op jit(solution)/shard_map/ppermute | solution.py:385
  34.0 3.3 %second.1 = (f32[2,256,256]{2,1,0:T(8,128)S(1)}, f32[2,256,256]{2,1,0:T(8,128)S(1)}) custom-call(f32[2,256,256]{2,1,0:T(8,128)S(1)} %get-tuple-element.35.a_in, f32[2,256,256]{2,1,0:T(8,128)S(1)} %get-tuple-element.36.m_in), custom_call_target="tpu_custom_call", output_to_operand_aliasing={{0}: (0, {}), {1}: (1, {})} | custom-call | flops 3000000000 | bytes 1048576 | tf_op jit(solution)/shard_map/second/pallas_call | solution.py:483
  37.3 0.7 %collective-permute-done.6 = f32[264,128]{1,0:T(8,128)S(1)} collective-permute-done((f32[264,128]{1,0:T(8,128)S(1)}, f32[264,128]{1,0:T(8,128)S(1)}, u32[]{:S(2)}, u32[]{:S(2)}) %collective-permute-start.6) | collective-permute-done | bytes 135200 | tf_op jit(solution)/shard_map/ppermute | solution.py:385
  38.0 11.9 %tree.1 = (f32[128,2048]{1,0:T(8,128)}, f32[256,128]{1,0:T(8,128)}, f32[256,128]{1,0:T(8,128)}, f32[256,128]{1,0:T(8,128)}, f32[256,128]{1,0:T(8,128)}) custom-call(s32[2]{0:T(128)S(1)} %pad_add_fusion.place, f32[264,128]{1,0:T(8,128)S(1)} %get-tuple-element.34.packed_zero, f32[264,128]{1,0:T(8,128)S(1)} %add.9.packed_one, f32[264,128]{1,0:T(8,128)S(1)} %add.10.packed_two, ...), custom_call_target="tpu_custom_call" | custom-call | tf_op jit(solution)/shard_map/tree/pallas_call | solution.py:493
  (3 shorter events, 0.1 us)
Async XLA Ops:
  0.7 1.0 %copy-start = (bf16[128,2048]{1,0:T(8,128)(2,1)S(1)}, bf16[128,2048]{1,0:T(8,128)(2,1)}, u32[]{:S(2)}) copy-start(bf16[128,2048]{1,0:T(8,128)(2,1)} %samples.1) | copy-start | bytes 1572868
  2.4 1.5 %collective-permute-start = (bf16[128,512]{1,0:T(8,128)(2,1)S(1)}, bf16[128,512]{1,0:T(8,128)(2,1)S(1)}, u32[]{:S(2)}, u32[]{:S(2)}) collective-permute-start(bf16[128,512]{1,0:T(8,128)(2,1)S(1)} %get-tuple-element.27), channel_id=1, source_target_pairs={{0,2},{2,0},{4,6},{6,4},{8,10},{10,8},{12,14},{14,12},{16,18},{18,... | collective-permute-start | bytes 393224 | tf_op jit(solution)/shard_map/ppermute | solution.py:393
  2.9 3.8 %collective-permute-start.1 = (bf16[128,512]{1,0:T(8,128)(2,1)S(1)}, bf16[128,512]{1,0:T(8,128)(2,1)S(1)}, u32[]{:S(2)}, u32[]{:S(2)}) collective-permute-start(bf16[128,512]{1,0:T(8,128)(2,1)S(1)} %get-tuple-element.28), channel_id=1, source_target_pairs={{2,4},{4,2},{6,8},{8,6},{10,12},{12,10},{14,16},{16,14},{18,20},{2... | collective-permute-start | bytes 393224 | tf_op jit(solution)/shard_map/ppermute | solution.py:393
  3.9 9.7 %collective-permute-start.2 = (bf16[128,512]{1,0:T(8,128)(2,1)S(1)}, bf16[128,512]{1,0:T(8,128)(2,1)S(1)}, u32[]{:S(2)}, u32[]{:S(2)}) collective-permute-start(bf16[128,512]{1,0:T(8,128)(2,1)S(1)} %collective-permute-done.first), channel_id=1, source_target_pairs={{0,1},{1,0},{2,3},{3,2},{4,5},{5,4},{6,7},{7,6},{8,9},{9,8},{10,11... | collective-permute-start | bytes 393224 | tf_op jit(solution)/shard_map/ppermute | solution.py:398
  6.8 6.9 %collective-permute-start.3 = (bf16[128,512]{1,0:T(8,128)(2,1)S(1)}, bf16[128,512]{1,0:T(8,128)(2,1)S(1)}, u32[]{:S(2)}, u32[]{:S(2)}) collective-permute-start(bf16[128,512]{1,0:T(8,128)(2,1)S(1)} %collective-permute-done.1.second), channel_id=1, source_target_pairs={{0,1},{1,0},{2,3},{3,2},{4,5},{5,4},{6,7},{7,6},{8,9},{9,8},{10,11... | collective-permute-start | bytes 393224 | tf_op jit(solution)/shard_map/ppermute | solution.py:398
  6.9 0.7 %copy-start.1 = (s32[16,8]{0,1:T(8,128)S(1)}, s32[16,8]{0,1:T(8,128)}, u32[]{:S(2)}) copy-start(s32[16,8]{0,1:T(8,128)} %param.4) | copy-start | bytes 1540
  17.6 6.5 %collective-permute-start.4 = (f32[264,128]{1,0:T(8,128)S(1)}, f32[264,128]{1,0:T(8,128)S(1)}, u32[]{:S(2)}, u32[]{:S(2)}) collective-permute-start(f32[264,128]{1,0:T(8,128)S(1)} %get-tuple-element.34.packed_zero), channel_id=1, source_target_pairs={{0,2},{2,0},{4,6},{6,4},{8,10},{10,8},{12,14},{14,12},{16,18},{18,... | collective-permute-start | bytes 405512 | tf_op jit(solution)/shard_map/ppermute | solution.py:385
  24.1 8.3 %collective-permute-start.5 = (f32[264,128]{1,0:T(8,128)S(1)}, f32[264,128]{1,0:T(8,128)S(1)}, u32[]{:S(2)}, u32[]{:S(2)}) collective-permute-start(f32[264,128]{1,0:T(8,128)S(1)} %add.9.packed_one), channel_id=1, source_target_pairs={{0,4},{4,0},{2,6},{6,2},{8,12},{12,8},{10,14},{14,10},{16,20},{20,... | collective-permute-start | bytes 405512 | tf_op jit(solution)/shard_map/ppermute | solution.py:385
  32.4 5.6 %collective-permute-start.6 = (f32[264,128]{1,0:T(8,128)S(1)}, f32[264,128]{1,0:T(8,128)S(1)}, u32[]{:S(2)}, u32[]{:S(2)}) collective-permute-start(f32[264,128]{1,0:T(8,128)S(1)} %add.10.packed_two), channel_id=1, source_target_pairs={{0,8},{8,0},{2,10},{10,2},{4,12},{12,4},{6,14},{14,6},{16,24},{24,... | collective-permute-start | bytes 405512 | tf_op jit(solution)/shard_map/ppermute | solution.py:385

commit v13 on v12

--- a/solution.py
+++ b/solution.py
@@ -328,16 +328,19 @@
     factor(a, m, 0, stop)
 
 
-def second_kernel(start, a_in, m_in, a, m):
+def second_kernel(start, place, packed_zero, packed_one, a_in, m_in, transfer, a, m):
     del a_in, m_in
     factor(a, m, start, a.shape[1])
     clear_lower(a)
+    child = a[0, own_rows(place, transfer.shape[1]), :]
+    child = child * (jnp.sqrt(largest(packed_zero)) * lax.rsqrt(largest(packed_one)))
+    transfer[...] = dot_split(split_two(m[1]), split_two(child), NT)
 
 
 def tree_kernel(
     scale, top_scale, place, packed_zero, packed_one, packed_two, packed_three, a_low, m_low,
     own_high, own_low, rest_high, rest_low,
-    bases, transfer_one, transfer_two, transfer_three, top, a, m, basis_rows, leaving,
+    bases, transfer_two, transfer_three, top, a, m, basis_rows, leaving,
 ):
     n = a.shape[1]
     own = own_high.shape[0]
@@ -357,13 +360,11 @@
     start_inverse(m)
     factor(a, m, 0, n)
     clear_lower(a)
-    uppers = [a_low[0, rows, :], a_low[1, rows, :], a[0, rows, :], a[1, rows, :]]
-    inverses = [m_low[1], m[0], m[1]]
-    transfers = [transfer_one, transfer_two, transfer_three]
-    for b in range(LEVELS):
-        child = uppers[b] * (jnp.sqrt(sizes[b]) * lax.rsqrt(sizes[b + 1]))
-        transfers[b][...] = dot_split(split_two(inverses[b]), split_two(child), NT)
-    top[...] = (uppers[LEVELS] * (jnp.sqrt(sizes[LEVELS]) * top_scale)).T
+    uppers = [a_low[1, rows, :], a[0, rows, :], a[1, rows, :]]
+    for b, transfer in enumerate((transfer_two, transfer_three)):
+        child = uppers[b] * (jnp.sqrt(sizes[b + 1]) * lax.rsqrt(sizes[b + 2]))
+        transfer[...] = dot_split(split_two(m[b]), split_two(child), NT)
+    top[...] = (uppers[-1] * (jnp.sqrt(sizes[-1]) * top_scale)).T
     leave.wait()
 
 
@@ -480,21 +481,21 @@
         name="first",
     )(packed, gram_one)
     gram_three = gram_two + from_partner(gram_two, "leaf", 2)
-    a, m = pl.pallas_call(
+    transfer_one, a, m = pl.pallas_call(
         functools.partial(second_kernel, split_row),
-        in_specs=[whole()] * 2,
-        out_specs=[whole()] * 2,
-        out_shape=[square] * 2,
-        input_output_aliases={0: 0, 1: 1},
+        in_specs=[smem] + [whole()] * 4,
+        out_specs=[whole()] * 3,
+        out_shape=[transfer_shape, square, square],
+        input_output_aliases={3: 1, 4: 2},
         compiler_params=params(),
         cost_estimate=pl.CostEstimate(flops=3 * 10**9, bytes_accessed=1024 * 1024, transcendentals=0),
         name="second",
-    )(a, m)
-    bases, transfer_one, transfer_two, transfer_three, top_factor = pl.pallas_call(
+    )(place, packed, gram_one, a, m)
+    bases, transfer_two, transfer_three, top_factor = pl.pallas_call(
         functools.partial(tree_kernel, math.sqrt(row_count), 1.0 / math.sqrt(2**LEVELS * row_count)),
         in_specs=[smem] + [whole()] * 10,
-        out_specs=[hbm] + [whole()] * (LEVELS + 1),
-        out_shape=[shape((own, row_count), F32)] + [transfer_shape] * (LEVELS + 1),
+        out_specs=[hbm] + [whole()] * LEVELS,
+        out_shape=[shape((own, row_count), F32)] + [transfer_shape] * LEVELS,
         scratch_shapes=[pltpu.VMEM((2, total, total), F32)] * 2
         + [pltpu.VMEM((own, row_count), F32), pltpu.SemaphoreType.DMA],
         compiler_params=params(),

time: 50.3 us -> 50.8 us (level)
  Pallas kernels: 31.9 us -> 33.1 us
  waiting for transfers between devices: 2 us -> 1.32 us
    pallas_call x1, Pallas kernels: 3.31 us -> 4.75 us  [shards(): pl.pallas_call(functools.partial(second_kernel, split_row), in_specs=[sme...]
    ppermute x3, waiting for transfers between devices: 1.67 us -> 1 us  [from_partner(): return lax.ppermute(block, axis, route)]
  transfers between devices with their start and end apart: 7 -> 7, of which waited for: 3 -> 2; matrix products, arithmetic and copies ran while one was open for 0% -> 0% of each run, Pallas kernels for 31% -> 33%
where the time goes in v13:
time: 50.8 us; the launch traced here: 50.6 us
  Pallas kernels  33.1 us (65%)
  starting transfers between devices  13.4 us (26%)
  local copies, waits for them, and re-layouts  1.73 us (3%)
  waiting for transfers between devices  1.32 us (3%)
  between operations  0.88 us (2%)
    pallas_call x1, Pallas kernels, shards(): pl.pallas_call(functools.partial(tree_kernel, math.sqrt(row_count), 1.0 /...  11.7 us
    ppermute x3, starting transfers between devices, from_partner(): return lax.ppermute(block, axis, route)  9.31 us
    pallas_call x1, Pallas kernels, shards(): pl.pallas_call(own_kernel, in_specs=[smem, smem, hbm] + [whole()] * 3, ou...  6.05 us
    pallas_call x1, Pallas kernels, shards(): pl.pallas_call(functools.partial(first_kernel, split_row), in_specs=[whol...  6.04 us
    pallas_call x1, Pallas kernels, shards(): pl.pallas_call(functools.partial(second_kernel, split_row), in_specs=[sme...  4.75 us
    pallas_call x1, Pallas kernels, shards(): pl.pallas_call(functools.partial(others_kernel, parts), in_specs=[smem, s...  3.93 us
    ppermute x2, starting transfers between devices, sample_shift(): lax.ppermute(block, 'samp', [(i, (i - d) % count) for i in range(count)])  2.88 us
    unnamed x4, local copies, waits for them, and re-layouts  1.73 us
  transfers between devices with their start and end apart: 7, of which 2 were waited for; matrix products, arithmetic and copies ran while one was open for 0% of the time, Pallas kernels for 33%

profile of v13, /device:TPU:0, one launch (start us, length us, event | category | flops | bytes accessed | tf_op | source)
XLA Modules:
  0.0 50.6 jit_solution(11673714720865315541)
XLA Ops:
  0.6 0.1 pad_add_fusion.1.at
  0.7 0.0 copy-start
  0.7 1.0 %copy-done = bf16[128,2048]{1,0:T(8,128)(2,1)S(1)} copy-done((bf16[128,2048]{1,0:T(8,128)(2,1)S(1)}, bf16[128,2048]{1,0:T(8,128)(2,1)}, u32[]{:S(2)}) %copy-start) | copy-done | bytes 524312
  1.8 0.7 %prepare.1 = (bf16[128,2048]{1,0:T(8,128)(2,1)S(1)}, bf16[128,512]{1,0:T(8,128)(2,1)S(1)}, bf16[128,512]{1,0:T(8,128)(2,1)S(1)}) custom-call(s32[2]{0:T(128)S(1)} %pad_add_fusion.1.at, bf16[128,2048]{1,0:T(8,128)(2,1)S(1)} %copy-done), custom_call_target="tpu_custom_call" | custom-call | tf_op jit(solution)/shard_map/prepare/pallas_call | solution.py:420
  2.4 0.5 %collective-permute-start = (bf16[128,512]{1,0:T(8,128)(2,1)S(1)}, bf16[128,512]{1,0:T(8,128)(2,1)S(1)}, u32[]{:S(2)}, u32[]{:S(2)}) collective-permute-start(bf16[128,512]{1,0:T(8,128)(2,1)S(1)} %get-tuple-element.27), channel_id=1, source_target_pairs={{0,2},{2,0},{4,6},{6,4},{8,10},{10,8},{12,14},{14,12},{16,18},{18,... | collective-permute-start | bytes 393224 | tf_op jit(solution)/shard_map/ppermute | solution.py:394
  2.9 0.7 %collective-permute-start.1 = (bf16[128,512]{1,0:T(8,128)(2,1)S(1)}, bf16[128,512]{1,0:T(8,128)(2,1)S(1)}, u32[]{:S(2)}, u32[]{:S(2)}) collective-permute-start(bf16[128,512]{1,0:T(8,128)(2,1)S(1)} %get-tuple-element.28), channel_id=1, source_target_pairs={{2,4},{4,2},{6,8},{8,6},{10,12},{12,10},{14,16},{16,14},{18,20},{2... | collective-permute-start | bytes 393224 | tf_op jit(solution)/shard_map/ppermute | solution.py:394
  3.6 0.3 collective-permute-done.first
  3.9 2.8 %collective-permute-start.2 = (bf16[128,512]{1,0:T(8,128)(2,1)S(1)}, bf16[128,512]{1,0:T(8,128)(2,1)S(1)}, u32[]{:S(2)}, u32[]{:S(2)}) collective-permute-start(bf16[128,512]{1,0:T(8,128)(2,1)S(1)} %collective-permute-done.first), channel_id=1, source_target_pairs={{0,1},{1,0},{2,3},{3,2},{4,5},{5,4},{6,7},{7,6},{8,9},{9,8},{10,11... | collective-permute-start | bytes 393224 | tf_op jit(solution)/shard_map/ppermute | solution.py:399
  6.8 0.0 collective-permute-done.1.second
  6.8 0.0 collective-permute-start.3
  6.8 0.1 pad_add_fusion.place
  6.9 0.0 copy-start.1
  6.9 0.7 %copy-done.1 = s32[16,8]{0,1:T(8,128)S(1)} copy-done((s32[16,8]{0,1:T(8,128)S(1)}, s32[16,8]{0,1:T(8,128)}, u32[]{:S(2)}) %copy-start.1) | copy-done | bytes 536
  7.6 6.1 %own.1 = (f32[128,2048]{1,0:T(8,128)}, bf16[16,8,128,128]{3,2,1,0:T(8,128)(2,1)S(1)}, bf16[128,2048]{1,0:T(8,128)(2,1)S(1)}, bf16[128,2048]{1,0:T(8,128)(2,1)S(1)}, f32[128,128]{1,0:T(8,128)S(1)}) custom-call(s32[2]{0:T(128)S(1)} %pad_add_fusion.place, s32[8,16]{1,0:T(8,128)S(1)} %bitcast.5, bf16[16,8,128,128]{3,2,1,0:T(8,128)(2,1)} %blocks_hbm.1, ...), custom_call_target="tpu_custom_call" | custom-call | flops 1073741824 | bytes 6291456 | tf_op jit(solution)/shard_map/own/pallas_call | solution.py:433
  13.6 0.0 collective-permute-done.2.refs_0_
  13.6 0.0 collective-permute-done.3.refs_1_
  13.6 3.9 %others.1 = (bf16[128,2048]{1,0:T(8,128)(2,1)S(1)}, bf16[128,2048]{1,0:T(8,128)(2,1)S(1)}, f32[264,128]{1,0:T(8,128)S(1)}) custom-call(s32[2]{0:T(128)S(1)} %pad_add_fusion.place, s32[8,16]{1,0:T(8,128)S(1)} %bitcast.6, bf16[16,8,128,128]{3,2,1,0:T(8,128)(2,1)S(1)} %get-tuple-element.30.blocks, bf16[128,512]{1,0:T(8,128)(2,1)S(1)} %collective-permute-done.2.refs_0_, ...), custom_call_target="tpu_custom_call" | custom-call | tf_op jit(solution)/shard_map/others/pallas_call | solution.py:459
  17.6 5.5 %collective-permute-start.4 = (f32[264,128]{1,0:T(8,128)S(1)}, f32[264,128]{1,0:T(8,128)S(1)}, u32[]{:S(2)}, u32[]{:S(2)}) collective-permute-start(f32[264,128]{1,0:T(8,128)S(1)} %get-tuple-element.34.packed_zero), channel_id=1, source_target_pairs={{0,2},{2,0},{4,6},{6,4},{8,10},{10,8},{12,14},{14,12},{16,18},{18,... | collective-permute-start | bytes 405512 | tf_op jit(solution)/shard_map/ppermute | solution.py:386
  23.0 1.0 %collective-permute-done.4 = f32[264,128]{1,0:T(8,128)S(1)} collective-permute-done((f32[264,128]{1,0:T(8,128)S(1)}, f32[264,128]{1,0:T(8,128)S(1)}, u32[]{:S(2)}, u32[]{:S(2)}) %collective-permute-start.4) | collective-permute-done | bytes 135200 | tf_op jit(solution)/shard_map/ppermute | solution.py:386
  24.1 2.2 %collective-permute-start.5 = (f32[264,128]{1,0:T(8,128)S(1)}, f32[264,128]{1,0:T(8,128)S(1)}, u32[]{:S(2)}, u32[]{:S(2)}) collective-permute-start(f32[264,128]{1,0:T(8,128)S(1)} %add.9.packed_one), channel_id=1, source_target_pairs={{0,4},{4,0},{2,6},{6,2},{8,12},{12,8},{10,14},{14,10},{16,20},{20,... | collective-permute-start | bytes 405512 | tf_op jit(solution)/shard_map/ppermute | solution.py:386
  26.3 6.0 %first.1 = (f32[2,256,256]{2,1,0:T(8,128)S(1)}, f32[2,256,256]{2,1,0:T(8,128)S(1)}) custom-call(f32[264,128]{1,0:T(8,128)S(1)} %get-tuple-element.34.packed_zero, f32[264,128]{1,0:T(8,128)S(1)} %add.9.packed_one), custom_call_target="tpu_custom_call" | custom-call | flops 3000000000 | bytes 1048576 | tf_op jit(solution)/shard_map/first/pallas_call | solution.py:474
  32.3 0.0 collective-permute-done.5
  32.3 1.7 %collective-permute-start.6 = (f32[264,128]{1,0:T(8,128)S(1)}, f32[264,128]{1,0:T(8,128)S(1)}, u32[]{:S(2)}, u32[]{:S(2)}) collective-permute-start(f32[264,128]{1,0:T(8,128)S(1)} %add.10.packed_two), channel_id=1, source_target_pairs={{0,8},{8,0},{2,10},{10,2},{4,12},{12,4},{6,14},{14,6},{16,24},{24,... | collective-permute-start | bytes 405512 | tf_op jit(solution)/shard_map/ppermute | solution.py:386
  34.0 4.8 %second.1 = (f32[256,128]{1,0:T(8,128)}, f32[2,256,256]{2,1,0:T(8,128)S(1)}, f32[2,256,256]{2,1,0:T(8,128)S(1)}) custom-call(s32[2]{0:T(128)S(1)} %pad_add_fusion.place, f32[264,128]{1,0:T(8,128)S(1)} %get-tuple-element.34.packed_zero, f32[264,128]{1,0:T(8,128)S(1)} %add.9.packed_one, ...), custom_call_target="tpu_custom_call", output_to_operand_aliasing={{1}: (3, {}), {2}: (4, {})} | custom-call | flops 3000000000 | bytes 1048576 | tf_op jit(solution)/shard_map/second/pallas_call | solution.py:484
  38.7 0.0 collective-permute-done.6
  38.8 11.7 %tree.1 = (f32[128,2048]{1,0:T(8,128)}, f32[256,128]{1,0:T(8,128)}, f32[256,128]{1,0:T(8,128)}, f32[256,128]{1,0:T(8,128)}) custom-call(s32[2]{0:T(128)S(1)} %pad_add_fusion.place, f32[264,128]{1,0:T(8,128)S(1)} %get-tuple-element.34.packed_zero, f32[264,128]{1,0:T(8,128)S(1)} %add.9.packed_one, f32[264,128]{1,0:T(8,128)S(1)} %add.10.packed_two, ...), custom_call_target="tpu_custom_call" | custom-call | tf_op jit(solution)/shard_map/tree/pallas_call | solution.py:494
  (3 shorter events, 0.1 us)
Async XLA Ops:
  0.7 1.0 %copy-start = (bf16[128,2048]{1,0:T(8,128)(2,1)S(1)}, bf16[128,2048]{1,0:T(8,128)(2,1)}, u32[]{:S(2)}) copy-start(bf16[128,2048]{1,0:T(8,128)(2,1)} %samples.1) | copy-start | bytes 1572868
  2.4 1.5 %collective-permute-start = (bf16[128,512]{1,0:T(8,128)(2,1)S(1)}, bf16[128,512]{1,0:T(8,128)(2,1)S(1)}, u32[]{:S(2)}, u32[]{:S(2)}) collective-permute-start(bf16[128,512]{1,0:T(8,128)(2,1)S(1)} %get-tuple-element.27), channel_id=1, source_target_pairs={{0,2},{2,0},{4,6},{6,4},{8,10},{10,8},{12,14},{14,12},{16,18},{18,... | collective-permute-start | bytes 393224 | tf_op jit(solution)/shard_map/ppermute | solution.py:394
  2.9 3.8 %collective-permute-start.1 = (bf16[128,512]{1,0:T(8,128)(2,1)S(1)}, bf16[128,512]{1,0:T(8,128)(2,1)S(1)}, u32[]{:S(2)}, u32[]{:S(2)}) collective-permute-start(bf16[128,512]{1,0:T(8,128)(2,1)S(1)} %get-tuple-element.28), channel_id=1, source_target_pairs={{2,4},{4,2},{6,8},{8,6},{10,12},{12,10},{14,16},{16,14},{18,20},{2... | collective-permute-start | bytes 393224 | tf_op jit(solution)/shard_map/ppermute | solution.py:394
  3.9 9.7 %collective-permute-start.2 = (bf16[128,512]{1,0:T(8,128)(2,1)S(1)}, bf16[128,512]{1,0:T(8,128)(2,1)S(1)}, u32[]{:S(2)}, u32[]{:S(2)}) collective-permute-start(bf16[128,512]{1,0:T(8,128)(2,1)S(1)} %collective-permute-done.first), channel_id=1, source_target_pairs={{0,1},{1,0},{2,3},{3,2},{4,5},{5,4},{6,7},{7,6},{8,9},{9,8},{10,11... | collective-permute-start | bytes 393224 | tf_op jit(solution)/shard_map/ppermute | solution.py:399
  6.8 6.9 %collective-permute-start.3 = (bf16[128,512]{1,0:T(8,128)(2,1)S(1)}, bf16[128,512]{1,0:T(8,128)(2,1)S(1)}, u32[]{:S(2)}, u32[]{:S(2)}) collective-permute-start(bf16[128,512]{1,0:T(8,128)(2,1)S(1)} %collective-permute-done.1.second), channel_id=1, source_target_pairs={{0,1},{1,0},{2,3},{3,2},{4,5},{5,4},{6,7},{7,6},{8,9},{9,8},{10,11... | collective-permute-start | bytes 393224 | tf_op jit(solution)/shard_map/ppermute | solution.py:399
  6.9 0.7 %copy-start.1 = (s32[16,8]{0,1:T(8,128)S(1)}, s32[16,8]{0,1:T(8,128)}, u32[]{:S(2)}) copy-start(s32[16,8]{0,1:T(8,128)} %param.4) | copy-start | bytes 1540
  17.6 6.4 %collective-permute-start.4 = (f32[264,128]{1,0:T(8,128)S(1)}, f32[264,128]{1,0:T(8,128)S(1)}, u32[]{:S(2)}, u32[]{:S(2)}) collective-permute-start(f32[264,128]{1,0:T(8,128)S(1)} %get-tuple-element.34.packed_zero), channel_id=1, source_target_pairs={{0,2},{2,0},{4,6},{6,4},{8,10},{10,8},{12,14},{14,12},{16,18},{18,... | collective-permute-start | bytes 405512 | tf_op jit(solution)/shard_map/ppermute | solution.py:386
  24.1 8.3 %collective-permute-start.5 = (f32[264,128]{1,0:T(8,128)S(1)}, f32[264,128]{1,0:T(8,128)S(1)}, u32[]{:S(2)}, u32[]{:S(2)}) collective-permute-start(f32[264,128]{1,0:T(8,128)S(1)} %add.9.packed_one), channel_id=1, source_target_pairs={{0,4},{4,0},{2,6},{6,2},{8,12},{12,8},{10,14},{14,10},{16,20},{20,... | collective-permute-start | bytes 405512 | tf_op jit(solution)/shard_map/ppermute | solution.py:386
  32.3 6.4 %collective-permute-start.6 = (f32[264,128]{1,0:T(8,128)S(1)}, f32[264,128]{1,0:T(8,128)S(1)}, u32[]{:S(2)}, u32[]{:S(2)}) collective-permute-start(f32[264,128]{1,0:T(8,128)S(1)} %add.10.packed_two), channel_id=1, source_target_pairs={{0,8},{8,0},{2,10},{10,2},{4,12},{12,4},{6,14},{14,6},{16,24},{24,... | collective-permute-start | bytes 405512 | tf_op jit(solution)/shard_map/ppermute | solution.py:386
